TPU v7x, 32 devices: a whole 2x2x4 slice. The times are simulated.
32 devices in a mesh: groups: 2 (over x), rows: 8 (over z, y), rep: 2 (over core).
Axes of the slice: x: 2, y: 2, z: 4, core: 2. Of those that a mesh axis runs over, the one named last changes fastest.
Arguments:
- features: bfloat16 [8192, 256], P(('groups', 'rows')), parts along dimension 0, may hold values from -6 to 6
- weight: bfloat16 [256, 256], replicated, may hold values from -0.375 to 0.375
- tiles: bfloat16 [2048, 128, 128], P(('groups', 'rows', 'rep')), parts along dimension 0, as said below
- tile_place: int32 [128, 16], P(('groups', 'rows', 'rep')), parts along dimension 0, may hold values from 0 to 15, as said below
- panel_count: int32 [128], P(('groups', 'rows', 'rep')), parts along dimension 0, may hold values from 0 to 16, as said below
Outputs:
- diffused: bfloat16 [8192, 256], P(('groups', 'rows', 'rep')), parts along dimension 0
There are 2 independent parts, one for each index of `groups`. A program takes and returns all parts, laid end to end along the dimension named above; an argument that names none is the same for every part. Nothing has to cross between parts.
Inputs may be any that keep to these rules, and one draw needn't show every extreme that they name: `tile_place`: each panel's 16 entries are a permutation of 0 to 15. `panel_count`: slots from the count on are not part of the matrix; in every draw some panel is full and some panel is empty. `tiles`: entries are zero or positive.
All inputs are finite; a program needn't handle non-finite values.
Results may differ from a plain program's by a relative error of at most 0.0065.
Values may be sent and summed in bfloat16 or wider, within the bound.
No kernel may reach another device: no remote copies, remote signals or barrier semaphores. Data moves between devices by JAX's collectives and lax.ppermute only.
A program may use at most 64 MiB of HBM per device.

v0:
```python
import jax
import jax.numpy as jnp
from jax import lax
from jax.sharding import PartitionSpec as P


def passed_along(block, axis, distance):
    devices = range(lax.axis_size(axis))
    route = [((i - distance) % len(devices), i) for i in devices]
    return lax.ppermute(block, axis, route)


def panel_term(tiles, tile_place, panel_count, section_idx, features_in, tile_span):
    tile_dim = tiles.shape[1]
    width = features_in.shape[1]
    slot_total = tile_span * tile_span
    pieces = features_in.reshape(tile_span, tile_dim, width)
    spots_all = lax.dynamic_index_in_dim(tile_place, section_idx, 0, keepdims=False)
    filled = lax.dynamic_index_in_dim(panel_count, section_idx, 0, keepdims=False)
    squares = lax.dynamic_slice_in_dim(tiles, section_idx * slot_total + 0, slot_total, 0)
    inputs = jnp.take(pieces, spots_all % tile_span, axis=0)
    products = jnp.einsum("kij,kjf->kif", squares, inputs, preferred_element_type=jnp.float32)
    is_alive = 0 + jnp.arange(slot_total) < filled
    chosen = (
        (spots_all[None, :] // tile_span == jnp.arange(tile_span)[:, None]) & is_alive[None, :]
    ).astype(jnp.float32)
    summed = jnp.einsum("ak,kif->aif", chosen, products, precision=lax.Precision.HIGHEST)
    return summed.reshape(tile_span * tile_dim, width)


def per_device(features, weight, tiles, tile_place, panel_count):
    rows_here = features.shape[0]
    tile_dim = tiles.shape[1]
    tile_span = rows_here // tile_dim
    slot_total = tile_span * tile_span
    section_total = panel_count.shape[0]
    replica = lax.axis_index("rep")
    half_rows = rows_here // lax.axis_size("rep")
    row_sums = jnp.sum(tiles, axis=2, dtype=jnp.float32)
    is_alive = (jnp.arange(slot_total)[None, :] < panel_count[:, None]).reshape(-1)
    chosen = (
        (tile_place.reshape(-1)[None, :] // tile_span == jnp.arange(tile_span)[:, None])
        & is_alive[None, :]
    ).astype(jnp.float32)
    partial_degree = jnp.dot(chosen, row_sums, precision=lax.Precision.HIGHEST)
    degree = 1.0 + lax.psum(partial_degree, "rep").reshape(rows_here)
    scale = lax.rsqrt(degree)
    first = (scale[:, None] * features).astype(jnp.bfloat16)

    def section_term(section_idx, features_in):
        return panel_term(tiles, tile_place, panel_count, section_idx, features_in, tile_span)

    def image_part(field):
        lower = passed_along(field, "rows", 1)
        current = jnp.where(replica == 0, field, lower)
        summed = section_term(0, current)

        def advance(section_idx, carry):
            moving, running = carry
            moving = passed_along(moving, "rows", 2)
            return (moving, running + section_term(section_idx, moving))

        current, summed = lax.fori_loop(1, section_total, advance, (current, summed))
        return summed

    lower_row = replica * half_rows
    scale_half = lax.dynamic_slice_in_dim(scale, lower_row, half_rows, 0)
    part_one = image_part(first)
    first_share = lax.psum_scatter(part_one, "rep", scatter_dimension=0, tiled=True)
    first_half = lax.dynamic_slice_in_dim(first, lower_row, half_rows, 0)
    heat_one = scale_half[:, None] * (first_share + first_half)
    second = lax.all_gather(
        (scale_half[:, None] * heat_one).astype(jnp.bfloat16), "rep", axis=0, tiled=True
    )
    part_two = image_part(second)
    second_share = lax.psum_scatter(part_two, "rep", scatter_dimension=0, tiled=True)
    second_half = lax.dynamic_slice_in_dim(second, lower_row, half_rows, 0)
    heat_two = scale_half[:, None] * (second_share + second_half)
    feature_half = lax.dynamic_slice_in_dim(features, lower_row, half_rows, 0)
    mixed = (feature_half + 5.0 * heat_one + 12.5 * heat_two).astype(jnp.bfloat16)
    return jnp.dot(mixed, weight, preferred_element_type=jnp.float32).astype(jnp.bfloat16)


def solution(mesh):
    in_specs = (
        P(("groups", "rows"), None),
        P(),
        P(("groups", "rows", "rep"), None, None),
        P(("groups", "rows", "rep"), None),
        P(("groups", "rows", "rep")),
    )
    out_specs = P(("groups", "rows", "rep"), None)
    return jax.shard_map(
        per_device, mesh=mesh, in_specs=in_specs, out_specs=out_specs, check_vma=False
    )
```

profile of v0, /device:TPU:0, one launch (start us, length us, event | category | flops | bytes accessed | tf_op | source)
XLA Modules:
  0.0 160.0 jit_solution(8028838191775564648)
XLA Ops:
  6.6 2.3 %convert_reduce_fusion = f32[64,128]{1,0:T(8,128)S(1)} fusion(bf16[64,128,128]{2,1,0:T(8,128)(2,1)} %param.13), kind=kLoop, calls=%fused_computation.62 | loop fusion | flops 2088960 | bytes 2129920 | tf_op jit(solution)/shard_map/reduce_sum | solution.py:39
  9.3 2.7 %psum.7 = f32[4,128]{1,0:T(4,128)S(1)} all-reduce(f32[4,128]{1,0:T(4,128)S(1)} %fusion.53), channel_id=1, replica_groups=mesh['groups'=2,'rows'=8,'rep'=2] {'rep'}, use_global_device_ids=true, to_apply=%region_1.2 | all-reduce | flops 512 | bytes 4096 | tf_op jit(solution)/shard_map/psum | solution.py:46
  12.2 2.9 %collective-permute-start.2 = (bf16[512,256]{1,0:T(8,128)(2,1)S(1)}, bf16[512,256]{1,0:T(8,128)(2,1)S(1)}, u32[]{:S(2)}, u32[]{:S(2)}) collective-permute-start(bf16[512,256]{1,0:T(8,128)(2,1)S(1)} %multiply_convert_fusion), channel_id=1, source_target_pairs={{14,0},{0,2},{2,4},{4,6},{6,8},{8,10},{10,12},{12,14},{15,1},{1,3}... | collective-permute-start | bytes 786440 | tf_op jit(solution)/shard_map/ppermute | solution.py:10
  15.2 9.5 %collective-permute-done.2 = bf16[512,256]{1,0:T(8,128)(2,1)S(1)} collective-permute-done((bf16[512,256]{1,0:T(8,128)(2,1)S(1)}, bf16[512,256]{1,0:T(8,128)(2,1)S(1)}, u32[]{:S(2)}, u32[]{:S(2)}) %collective-permute-start.2) | collective-permute-done | bytes 262176 | tf_op jit(solution)/shard_map/ppermute | solution.py:10
  24.9 1.6 %gather_fusion.2 = bf16[16,128,256]{2,1,0:T(8,128)(2,1)} fusion(bf16[4,128,256]{2,1,0:T(8,128)(2,1)S(1)} %bitcast.74, s32[1024]{0:T(1024)S(1)} %pad_clamp_fusion.2), kind=kCustom, calls=%fused_computation.2.clone | custom fusion | bytes 2097216 | tf_op jit(solution)/shard_map/jit(_take)/gather | solution.py:21
  26.5 3.1 %fusion.38 = f32[16,256,128]{2,1,0:T(8,128)} fusion(bf16[16,128,256]{2,1,0:T(8,128)(2,1)} %gather_fusion.2, pred[16]{0:T(512)(128)(4,1)S(1)} %get-tuple-element.440, bf16[64,128,128]{2,1,0:T(8,128)(2,1)S(1)} %copy-done.1), kind=kOutput, calls=%fused_computation.70 | convolution fusion | flops 134742016 | bytes 3670528 | tf_op jit(solution)/shard_map/kij,kjf->kif/dot_general | solution.py:22
  29.6 3.1 %copy.12 = f32[16,256,128]{1,0,2:T(8,128)} copy(f32[16,256,128]{2,1,0:T(8,128)} %fusion.38) | data formatting | bytes 4194304 | tf_op jit(solution)/shard_map/kij,kjf->kif/dot_general | solution.py:22
  32.7 2.4 %fusion.34 = f32[4,128,256]{2,0,1:T(4,128)S(1)} fusion(f32[16,256,128]{1,0,2:T(8,128)} %copy.12, s32[16]{0:T(128)S(1)} %fusion.61, pred[16]{0:T(512)(128)(4,1)S(1)} %iota_compare_fusion.7), kind=kOutput, calls=%fused_computation.65 | convolution fusion | flops 25165952 | bytes 2621520 | tf_op jit(solution)/shard_map/ak,kif->aif/dot_general | solution.py:27
  36.0 39.6 %while.38 = (s32[]{:T(128)}, bf16[512,256]{1,0:T(8,128)(2,1)S(1)}, f32[512,256]{1,0:T(8,128)}, s32[4,16]{1,0:T(4,128)S(1)}, s32[4]{0:T(128)S(1)}, /*index=5*/bf1...) while((s32[]{:T(128)}, bf16[512,256]{1,0:T(8,128)(2,1)S(1)}, ...), condition=%wide.region_3.5_spmd, body=%wide.region_2.4_spmd.sunk | while | flops 160040608 | bytes 16783116 | solution.py:63
  38.5 7.2 %collective-permute-done = bf16[512,256]{1,0:T(8,128)(2,1)S(1)} collective-permute-done((bf16[512,256]{1,0:T(8,128)(2,1)S(1)}, bf16[512,256]{1,0:T(8,128)(2,1)S(1)}, u32[]{:S(2)}, u32[]{:S(2)}) %collective-permute-start) | collective-permute-done | bytes 262176 | tf_op jit(solution)/shard_map/while/body/eval_jaxpr/ppermute | solution.py:10
  47.0 2.0 %fusion.90 = f32[4,128,256]{2,0,1:T(4,128)S(1)} fusion(f32[16,128,256]{2,1,0:T(8,128)S(1)} %fusion.88, s32[16]{0:T(128)S(1)} %copy-done.10, pred[16]{0:T(512)(128)(4,1)S(1)} %copy-done.11), kind=kOutput, calls=%fused_computation.4.clone.1 | convolution fusion | flops 25165952 | bytes 2621520 | tf_op jit(solution)/shard_map/while/body/eval_jaxpr/ak,kif->aif/dot_general | solution.py:27
  52.5 6.3 %collective-permute-done = bf16[512,256]{1,0:T(8,128)(2,1)S(1)} collective-permute-done((bf16[512,256]{1,0:T(8,128)(2,1)S(1)}, bf16[512,256]{1,0:T(8,128)(2,1)S(1)}, u32[]{:S(2)}, u32[]{:S(2)}) %collective-permute-start) | collective-permute-done | bytes 262176 | tf_op jit(solution)/shard_map/while/body/eval_jaxpr/ppermute | solution.py:10
  60.1 2.0 %fusion.90 = f32[4,128,256]{2,0,1:T(4,128)S(1)} fusion(f32[16,128,256]{2,1,0:T(8,128)S(1)} %fusion.88, s32[16]{0:T(128)S(1)} %copy-done.10, pred[16]{0:T(512)(128)(4,1)S(1)} %copy-done.11), kind=kOutput, calls=%fused_computation.4.clone.1 | convolution fusion | flops 25165952 | bytes 2621520 | tf_op jit(solution)/shard_map/while/body/eval_jaxpr/ak,kif->aif/dot_general | solution.py:27
  65.6 5.7 %collective-permute-done = bf16[512,256]{1,0:T(8,128)(2,1)S(1)} collective-permute-done((bf16[512,256]{1,0:T(8,128)(2,1)S(1)}, bf16[512,256]{1,0:T(8,128)(2,1)S(1)}, u32[]{:S(2)}, u32[]{:S(2)}) %collective-permute-start) | collective-permute-done | bytes 262176 | tf_op jit(solution)/shard_map/while/body/eval_jaxpr/ppermute | solution.py:10
  72.6 2.0 %fusion.90 = f32[4,128,256]{2,0,1:T(4,128)S(1)} fusion(f32[16,128,256]{2,1,0:T(8,128)S(1)} %fusion.88, s32[16]{0:T(128)S(1)} %copy-done.10, pred[16]{0:T(512)(128)(4,1)S(1)} %copy-done.11), kind=kOutput, calls=%fused_computation.4.clone.1 | convolution fusion | flops 25165952 | bytes 2621520 | tf_op jit(solution)/shard_map/while/body/eval_jaxpr/ak,kif->aif/dot_general | solution.py:27
  75.8 4.8 %reduce-scatter.3.cloned.1.call-done = f32[256,256]{1,0:T(8,128)} async-done(((f32[512,256]{1,0:T(8,128)}), f32[256,256]{1,0:T(8,128)}) %reduce-scatter.3.cloned.1.call-update) | async-done | bytes 262160 | tf_op jit(solution)/shard_map/reduce_scatter | solution.py:69
  81.7 2.0 %all_gather.3 = bf16[512,256]{1,0:T(8,128)(2,1)S(1)} all-gather(bf16[256,256]{1,0:T(8,128)(2,1)S(1)} %multiply_convert_fusion.1), channel_id=1, replica_groups=mesh['groups'=2,'rows'=8,'rep'=2] {'rep'}, dimensions={0}, use_global_device_ids=true | all-gather | bytes 393216 | tf_op jit(solution)/shard_map/all_gather | solution.py:72
  83.7 1.8 %collective-permute-start.3 = (bf16[512,256]{1,0:T(8,128)(2,1)S(1)}, bf16[512,256]{1,0:T(8,128)(2,1)S(1)}, u32[]{:S(2)}, u32[]{:S(2)}) collective-permute-start(bf16[512,256]{1,0:T(8,128)(2,1)S(1)} %all_gather.3), channel_id=1, source_target_pairs={{14,0},{0,2},{2,4},{4,6},{6,8},{8,10},{10,12},{12,14},{15,1},{1,3}... | collective-permute-start | bytes 786440 | tf_op jit(solution)/shard_map/ppermute | solution.py:10
  85.5 9.6 %collective-permute-done.3 = bf16[512,256]{1,0:T(8,128)(2,1)S(1)} collective-permute-done((bf16[512,256]{1,0:T(8,128)(2,1)S(1)}, bf16[512,256]{1,0:T(8,128)(2,1)S(1)}, u32[]{:S(2)}, u32[]{:S(2)}) %collective-permute-start.3) | collective-permute-done | bytes 262176 | tf_op jit(solution)/shard_map/ppermute | solution.py:10
  95.1 1.7 %gather_fusion.3 = bf16[16,128,256]{2,1,0:T(8,128)(2,1)} fusion(bf16[4,128,256]{2,1,0:T(8,128)(2,1)S(1)} %bitcast.73, s32[1024]{0:T(1024)} %copy-done.14), kind=kCustom, calls=%fused_computation.3.clone | custom fusion | bytes 2097216 | tf_op jit(solution)/shard_map/jit(_take)/gather | solution.py:21
  96.9 3.1 %fusion.36 = f32[16,256,128]{2,1,0:T(8,128)} fusion(bf16[16,128,256]{2,1,0:T(8,128)(2,1)} %gather_fusion.3, pred[16]{0:T(512)(128)(4,1)S(1)} %copy-done.20, bf16[64,128,128]{2,1,0:T(8,128)(2,1)S(1)} %get-tuple-element.613), kind=kOutput, calls=%fused_computation.68 | convolution fusion | flops 134742016 | bytes 3670528 | tf_op jit(solution)/shard_map/kij,kjf->kif/dot_general | solution.py:22
  100.0 3.1 %copy.13 = f32[16,256,128]{1,0,2:T(8,128)} copy(f32[16,256,128]{2,1,0:T(8,128)} %fusion.36) | data formatting | bytes 4194304 | tf_op jit(solution)/shard_map/kij,kjf->kif/dot_general | solution.py:22
  103.1 2.4 %fusion.32 = f32[4,128,256]{2,0,1:T(4,128)S(1)} fusion(f32[16,256,128]{1,0,2:T(8,128)} %copy.13, s32[16]{0:T(128)S(1)} %copy-done.18, pred[16]{0:T(512)(128)(4,1)S(1)} %copy-done.16), kind=kOutput, calls=%fused_computation.63 | convolution fusion | flops 25165952 | bytes 2621520 | tf_op jit(solution)/shard_map/ak,kif->aif/dot_general | solution.py:27
  106.5 39.2 %while.39 = (s32[]{:T(128)}, bf16[512,256]{1,0:T(8,128)(2,1)S(1)}, f32[512,256]{1,0:T(8,128)}, s32[4,16]{1,0:T(4,128)S(1)}, s32[4]{0:T(128)S(1)}, /*index=5*/bf1...) while((s32[]{:T(128)}, bf16[512,256]{1,0:T(8,128)(2,1)S(1)}, ...), condition=%wide.region_6.8_spmd, body=%wide.region_5.7_spmd.sunk | while | flops 160040608 | bytes 16782916 | solution.py:63
  108.3 7.8 %collective-permute-done.1 = bf16[512,256]{1,0:T(8,128)(2,1)S(1)} collective-permute-done((bf16[512,256]{1,0:T(8,128)(2,1)S(1)}, bf16[512,256]{1,0:T(8,128)(2,1)S(1)}, u32[]{:S(2)}, u32[]{:S(2)}) %collective-permute-start.1) | collective-permute-done | bytes 262176 | tf_op jit(solution)/shard_map/while/body/eval_jaxpr/ppermute | solution.py:10
  117.3 2.0 %fusion.97 = f32[4,128,256]{2,0,1:T(4,128)S(1)} fusion(f32[16,128,256]{2,1,0:T(8,128)S(1)} %fusion.95, s32[16]{0:T(128)S(1)} %fusion.96, pred[16]{0:T(512)(128)(4,1)S(1)} %copy-done.12), kind=kOutput, calls=%fused_computation.33.clone.1 | convolution fusion | flops 25165952 | bytes 2621520 | tf_op jit(solution)/shard_map/while/body/eval_jaxpr/ak,kif->aif/dot_general | solution.py:27
  122.1 6.8 %collective-permute-done.1 = bf16[512,256]{1,0:T(8,128)(2,1)S(1)} collective-permute-done((bf16[512,256]{1,0:T(8,128)(2,1)S(1)}, bf16[512,256]{1,0:T(8,128)(2,1)S(1)}, u32[]{:S(2)}, u32[]{:S(2)}) %collective-permute-start.1) | collective-permute-done | bytes 262176 | tf_op jit(solution)/shard_map/while/body/eval_jaxpr/ppermute | solution.py:10
  130.2 2.0 %fusion.97 = f32[4,128,256]{2,0,1:T(4,128)S(1)} fusion(f32[16,128,256]{2,1,0:T(8,128)S(1)} %fusion.95, s32[16]{0:T(128)S(1)} %fusion.96, pred[16]{0:T(512)(128)(4,1)S(1)} %copy-done.12), kind=kOutput, calls=%fused_computation.33.clone.1 | convolution fusion | flops 25165952 | bytes 2621520 | tf_op jit(solution)/shard_map/while/body/eval_jaxpr/ak,kif->aif/dot_general | solution.py:27
  135.1 6.3 %collective-permute-done.1 = bf16[512,256]{1,0:T(8,128)(2,1)S(1)} collective-permute-done((bf16[512,256]{1,0:T(8,128)(2,1)S(1)}, bf16[512,256]{1,0:T(8,128)(2,1)S(1)}, u32[]{:S(2)}, u32[]{:S(2)}) %collective-permute-start.1) | collective-permute-done | bytes 262176 | tf_op jit(solution)/shard_map/while/body/eval_jaxpr/ppermute | solution.py:10
  142.7 2.0 %fusion.97 = f32[4,128,256]{2,0,1:T(4,128)S(1)} fusion(f32[16,128,256]{2,1,0:T(8,128)S(1)} %fusion.95, s32[16]{0:T(128)S(1)} %fusion.96, pred[16]{0:T(512)(128)(4,1)S(1)} %copy-done.12), kind=kOutput, calls=%fused_computation.33.clone.1 | convolution fusion | flops 25165952 | bytes 2621520 | tf_op jit(solution)/shard_map/while/body/eval_jaxpr/ak,kif->aif/dot_general | solution.py:27
  145.7 5.4 %reduce-scatter.5.cloned.1.call-done = f32[256,256]{1,0:T(8,128)} async-done(((f32[512,256]{1,0:T(8,128)}), f32[256,256]{1,0:T(8,128)}) %reduce-scatter.5.cloned.1.call-update) | async-done | bytes 262160 | tf_op jit(solution)/shard_map/reduce_scatter | solution.py:76
  151.1 2.1 %convolution_convert_fusion = bf16[256,256]{1,0:T(8,128)(2,1)} fusion(bf16[256,256]{1,0:T(8,128)(2,1)S(1)} %copy-done, f32[256,256]{1,0:T(8,128)} %reduce-scatter.5.cloned.1.call-done, f32[256,256]{1,0:T(8,128)} %reduce-scatter.3.cloned.1.call-done, bf16[512,256]{1,0:T(8,128)(2,1)} %copy-done.7, s32[]{:T(128)S(6)} %select_n.176, f32[256]{0:T(256)} %copy-done.13, ...), kind=kOutput, calls=%fused_computation.67 | convolution fusion | flops 34406400 | bytes 1180676 | tf_op jit(solution)/shard_map/dot_general | solution.py:81
  (177 shorter events, 30.4 us)
Async XLA Ops:
  6.5 144.6 %copy-start = (bf16[256,256]{1,0:T(8,128)(2,1)S(1)}, bf16[256,256]{1,0:T(8,128)(2,1)}, u32[]{:S(2)}) copy-start(bf16[256,256]{1,0:T(8,128)(2,1)} %param.12) | copy-start | bytes 393220
  6.5 2.3 %copy-start.9 = (s32[4,16]{1,0:T(4,128)S(1)}, s32[4,16]{1,0:T(4,128)}, u32[]{:S(2)}) copy-start(s32[4,16]{1,0:T(4,128)} %param.14) | copy-start | bytes 772
  6.5 2.5 %copy-start.21 = (s32[4]{0:T(128)S(1)}, s32[4]{0:T(128)}, u32[]{:S(2)}) copy-start(s32[4]{0:T(128)} %param.15) | copy-start | bytes 52
  6.5 5.5 %copy-start.6 = (bf16[512,256]{1,0:T(8,128)(2,1)S(1)}, bf16[512,256]{1,0:T(8,128)(2,1)}, u32[]{:S(2)}) copy-start(bf16[512,256]{1,0:T(8,128)(2,1)} %param.11) | copy-start | bytes 786436
  6.5 74.1 %reduce-scatter.3.cloned.1.call-start = ((), (), s32[]{:S(2)}) async-start(), calls=%async_computation.2 | async-start | bytes 786432 | tf_op jit(solution)/shard_map/reduce_scatter | solution.py:69
  8.9 17.6 %copy-start.1 = (bf16[64,128,128]{2,1,0:T(8,128)(2,1)S(1)}, bf16[64,128,128]{2,1,0:T(8,128)(2,1)}, u32[]{:S(2)}) copy-start(bf16[64,128,128]{2,1,0:T(8,128)(2,1)} %param.13) | copy-start | bytes 6291460
  12.1 3.0 %copy-start.8 = (bf16[512,256]{1,0:T(8,128)(2,1)}, bf16[512,256]{1,0:T(8,128)(2,1)S(1)}, u32[]{:S(2)}) copy-start(bf16[512,256]{1,0:T(8,128)(2,1)S(1)} %multiply_convert_fusion) | copy-start | bytes 786436
  12.2 12.6 %collective-permute-start.2 = (bf16[512,256]{1,0:T(8,128)(2,1)S(1)}, bf16[512,256]{1,0:T(8,128)(2,1)S(1)}, u32[]{:S(2)}, u32[]{:S(2)}) collective-permute-start(bf16[512,256]{1,0:T(8,128)(2,1)S(1)} %multiply_convert_fusion), channel_id=1, source_target_pairs={{14,0},{0,2},{2,4},{4,6},{6,8},{8,10},{10,12},{12,14},{15,1},{1,3}... | collective-permute-start | bytes 786440 | tf_op jit(solution)/shard_map/ppermute | solution.py:10
  15.1 14.6 %copy-start.19 = (pred[16]{0:T(512)(128)(4,1)}, pred[16]{0:T(512)(128)(4,1)S(1)}, u32[]{:S(2)}) copy-start(pred[16]{0:T(512)(128)(4,1)S(1)} %get-tuple-element.440) | copy-start | bytes 52
  15.1 14.5 %copy-start.14 = (s32[1024]{0:T(1024)}, s32[1024]{0:T(1024)S(1)}, u32[]{:S(2)}) copy-start(s32[1024]{0:T(1024)S(1)} %pad_clamp_fusion.2) | copy-start | bytes 12292
  15.2 17.5 %copy-start.15 = (pred[16]{0:T(512)(128)(4,1)}, pred[16]{0:T(512)(128)(4,1)S(1)}, u32[]{:S(2)}) copy-start(pred[16]{0:T(512)(128)(4,1)S(1)} %iota_compare_fusion.7) | copy-start | bytes 52
  15.2 17.5 %copy-start.17 = (s32[16]{0:T(128)}, s32[16]{0:T(128)S(1)}, u32[]{:S(2)}) copy-start(s32[16]{0:T(128)S(1)} %fusion.61) | copy-start | bytes 196
  36.0 9.7 %collective-permute-start = (bf16[512,256]{1,0:T(8,128)(2,1)S(1)}, bf16[512,256]{1,0:T(8,128)(2,1)S(1)}, u32[]{:S(2)}, u32[]{:S(2)}) collective-permute-start(bf16[512,256]{1,0:T(8,128)(2,1)S(1)} %get-tuple-element.536), channel_id=1, source_target_pairs={{12,0},{14,2},{0,4},{2,6},{4,8},{6,10},{8,12},{10,14},{13,1},{15,3... | collective-permute-start | bytes 786440 | tf_op jit(solution)/shard_map/while/body/eval_jaxpr/ppermute | solution.py:10
  47.0 2.1 %copy-start.2 = (f32[512,256]{1,0:T(8,128)S(1)}, f32[512,256]{1,0:T(8,128)}, u32[]{:S(2)}) copy-start(f32[512,256]{1,0:T(8,128)} %get-tuple-element.537) | copy-start | bytes 1572868 | tf_op jit(solution)/shard_map/while
  50.0 8.8 %collective-permute-start = (bf16[512,256]{1,0:T(8,128)(2,1)S(1)}, bf16[512,256]{1,0:T(8,128)(2,1)S(1)}, u32[]{:S(2)}, u32[]{:S(2)}) collective-permute-start(bf16[512,256]{1,0:T(8,128)(2,1)S(1)} %get-tuple-element.536), channel_id=1, source_target_pairs={{12,0},{14,2},{0,4},{2,6},{4,8},{6,10},{8,12},{10,14},{13,1},{15,3... | collective-permute-start | bytes 786440 | tf_op jit(solution)/shard_map/while/body/eval_jaxpr/ppermute | solution.py:10
  60.1 2.1 %copy-start.2 = (f32[512,256]{1,0:T(8,128)S(1)}, f32[512,256]{1,0:T(8,128)}, u32[]{:S(2)}) copy-start(f32[512,256]{1,0:T(8,128)} %get-tuple-element.537) | copy-start | bytes 1572868 | tf_op jit(solution)/shard_map/while
  63.1 8.2 %collective-permute-start = (bf16[512,256]{1,0:T(8,128)(2,1)S(1)}, bf16[512,256]{1,0:T(8,128)(2,1)S(1)}, u32[]{:S(2)}, u32[]{:S(2)}) collective-permute-start(bf16[512,256]{1,0:T(8,128)(2,1)S(1)} %get-tuple-element.536), channel_id=1, source_target_pairs={{12,0},{14,2},{0,4},{2,6},{4,8},{6,10},{8,12},{10,14},{13,1},{15,3... | collective-permute-start | bytes 786440 | tf_op jit(solution)/shard_map/while/body/eval_jaxpr/ppermute | solution.py:10
  72.6 2.1 %copy-start.2 = (f32[512,256]{1,0:T(8,128)S(1)}, f32[512,256]{1,0:T(8,128)}, u32[]{:S(2)}) copy-start(f32[512,256]{1,0:T(8,128)} %get-tuple-element.537) | copy-start | bytes 1572868 | tf_op jit(solution)/shard_map/while
  75.6 21.3 %copy-start.20 = (pred[16]{0:T(512)(128)(4,1)S(1)}, pred[16]{0:T(512)(128)(4,1)}, u32[]{:S(2)}) copy-start(pred[16]{0:T(512)(128)(4,1)} %copy-done.19) | copy-start | bytes 52
  75.7 75.5 %reduce-scatter.5.cloned.1.call-start = ((), (), s32[]{:S(2)}) async-start(), calls=%async_computation.3 | async-start | bytes 786432 | tf_op jit(solution)/shard_map/reduce_scatter | solution.py:76
  75.8 4.8 %copy-start.13 = (f32[256]{0:T(256)}, f32[256]{0:T(256)S(1)}, u32[]{:S(2)}) copy-start(f32[256]{0:T(256)S(1)} %dynamic_slice.105) | copy-start | bytes 3076
  83.7 16.3 %copy-start.7 = (bf16[512,256]{1,0:T(8,128)(2,1)}, bf16[512,256]{1,0:T(8,128)(2,1)S(1)}, u32[]{:S(2)}) copy-start(bf16[512,256]{1,0:T(8,128)(2,1)S(1)} %all_gather.3) | copy-start | bytes 786436
  83.7 11.4 %collective-permute-start.3 = (bf16[512,256]{1,0:T(8,128)(2,1)S(1)}, bf16[512,256]{1,0:T(8,128)(2,1)S(1)}, u32[]{:S(2)}, u32[]{:S(2)}) collective-permute-start(bf16[512,256]{1,0:T(8,128)(2,1)S(1)} %all_gather.3), channel_id=1, source_target_pairs={{14,0},{0,2},{2,4},{4,6},{6,8},{8,10},{10,12},{12,14},{15,1},{1,3}... | collective-permute-start | bytes 786440 | tf_op jit(solution)/shard_map/ppermute | solution.py:10
  100.0 3.2 %copy-start.16 = (pred[16]{0:T(512)(128)(4,1)S(1)}, pred[16]{0:T(512)(128)(4,1)}, u32[]{:S(2)}) copy-start(pred[16]{0:T(512)(128)(4,1)} %copy-done.15) | copy-start | bytes 52
  100.0 3.2 %copy-start.18 = (s32[16]{0:T(128)S(1)}, s32[16]{0:T(128)}, u32[]{:S(2)}) copy-start(s32[16]{0:T(128)} %copy-done.17) | copy-start | bytes 196
  106.5 9.6 %copy-start.23 = (s32[4]{0:T(128)}, s32[4]{0:T(128)S(1)}, u32[]{:S(2)}) copy-start(s32[4]{0:T(128)S(1)} %get-tuple-element.583) | copy-start | bytes 52 | tf_op jit(solution)/shard_map/while
  106.5 9.6 %collective-permute-start.1 = (bf16[512,256]{1,0:T(8,128)(2,1)S(1)}, bf16[512,256]{1,0:T(8,128)(2,1)S(1)}, u32[]{:S(2)}, u32[]{:S(2)}) collective-permute-start(bf16[512,256]{1,0:T(8,128)(2,1)S(1)} %get-tuple-element.569), channel_id=1, source_target_pairs={{12,0},{14,2},{0,4},{2,6},{4,8},{6,10},{8,12},{10,14},{13,1},{15,3... | collective-permute-start | bytes 786440 | tf_op jit(solution)/shard_map/while/body/eval_jaxpr/ppermute | solution.py:10
  120.3 8.7 %copy-start.23 = (s32[4]{0:T(128)}, s32[4]{0:T(128)S(1)}, u32[]{:S(2)}) copy-start(s32[4]{0:T(128)S(1)} %get-tuple-element.583) | copy-start | bytes 52 | tf_op jit(solution)/shard_map/while
  120.3 8.7 %collective-permute-start.1 = (bf16[512,256]{1,0:T(8,128)(2,1)S(1)}, bf16[512,256]{1,0:T(8,128)(2,1)S(1)}, u32[]{:S(2)}, u32[]{:S(2)}) collective-permute-start(bf16[512,256]{1,0:T(8,128)(2,1)S(1)} %get-tuple-element.569), channel_id=1, source_target_pairs={{12,0},{14,2},{0,4},{2,6},{4,8},{6,10},{8,12},{10,14},{13,1},{15,3... | collective-permute-start | bytes 786440 | tf_op jit(solution)/shard_map/while/body/eval_jaxpr/ppermute | solution.py:10
  133.2 8.2 %copy-start.23 = (s32[4]{0:T(128)}, s32[4]{0:T(128)S(1)}, u32[]{:S(2)}) copy-start(s32[4]{0:T(128)S(1)} %get-tuple-element.583) | copy-start | bytes 52 | tf_op jit(solution)/shard_map/while
  133.2 8.2 %collective-permute-start.1 = (bf16[512,256]{1,0:T(8,128)(2,1)S(1)}, bf16[512,256]{1,0:T(8,128)(2,1)S(1)}, u32[]{:S(2)}, u32[]{:S(2)}) collective-permute-start(bf16[512,256]{1,0:T(8,128)(2,1)S(1)} %get-tuple-element.569), channel_id=1, source_target_pairs={{12,0},{14,2},{0,4},{2,6},{4,8},{6,10},{8,12},{10,14},{13,1},{15,3... | collective-permute-start | bytes 786440 | tf_op jit(solution)/shard_map/while/body/eval_jaxpr/ppermute | solution.py:10
  142.7 2.1 %copy-start.4 = (f32[512,256]{1,0:T(8,128)S(1)}, f32[512,256]{1,0:T(8,128)}, u32[]{:S(2)}) copy-start(f32[512,256]{1,0:T(8,128)} %get-tuple-element.570) | copy-start | bytes 1572868 | tf_op jit(solution)/shard_map/while
  (23 other events, 21.1 us)
Sparse Core Ops, SparseCore 0:
  75.8 4.8 reduce-scatter.2
  145.8 5.2 reduce-scatter.4
where the time goes:
time: 161 us; the launch traced here: 160 us
  waiting for transfers between devices  69.4 us (43%)
  matrix products  28 us (17%)
  local copies, waits for them, and re-layouts  25.3 us (16%)
  other arithmetic  13.6 us (8%)
  between operations  13.6 us (8%)
  starting transfers between devices  4.82 us (3%)
  blocking collectives  4.71 us (3%)
    ppermute x8, waiting for transfers between devices, passed_along(): return lax.ppermute(block, axis, route)  59.1 us
    dot_general x8, matrix products, panel_term(): jnp.einsum('ak,kif->aif', chosen, products, precision=lax.Precision.HIGHEST)  16.6 us
    dot_general x8, matrix products, panel_term(): jnp.einsum('kij,kjf->kif', squares, inputs, preferred_element_type=jnp.fl...  9.23 us
    lt x7, other arithmetic, panel_term(): is_alive = 0 + jnp.arange(slot_total) < filled  7.39 us
    gather x8, local copies, waits for them, and re-layouts, panel_term(): inputs = jnp.take(pieces, spots_all % tile_span, axis=0)  7.03 us
    dot_general x2, local copies, waits for them, and re-layouts, panel_term(): jnp.einsum('kij,kjf->kif', squares, inputs, preferred_element_type=jnp.fl...  6.21 us
    while x66, local copies, waits for them, and re-layouts  5.59 us
    reduce_scatter x1, waiting for transfers between devices, per_device(): lax.psum_scatter(part_two, 'rep', scatter_dimension=0, tiled=True)  5.41 us
  transfers between devices with their start and end apart: 10, of which 10 were waited for; matrix products, arithmetic and copies ran while one was open for 8% of the time, Pallas kernels for 0%

commit v1 on v0

v1 whole, which is shorter than its diff:
```python
import functools

import jax
import jax.numpy as jnp
from jax import lax
from jax.experimental import pallas as pl
from jax.experimental.pallas import tpu as pltpu
from jax.sharding import PartitionSpec as P

F32 = jnp.float32
BF16 = jnp.bfloat16
VMEM = pl.BlockSpec(memory_space=pltpu.VMEM)
SMEM = pl.BlockSpec(memory_space=pltpu.SMEM)
ANY = pl.BlockSpec(memory_space=pl.ANY)
PARAMS = pltpu.CompilerParams(vmem_limit_bytes=56 * 2**20)


def xor_permute(block, axis, distance):
    return lax.ppermute(block, axis, [(i, i ^ distance) for i in range(lax.axis_size(axis))])


def gathered(block, axis, size):
    if size == 1:
        return [block]
    if size == 2:
        return [block, xor_permute(block, axis, 1)]
    half = size // 2
    far = xor_permute(block, axis, half)
    near = gathered(block, axis, half)
    return near + [far] + [xor_permute(far, axis, d) for d in range(1, half)]


def swapped(block, axis):
    return lax.ppermute(block, axis, [(0, 1), (1, 0)])


def place_kernel(place_ref, count_ref, tiles_ref, dense_ref, degree_ref, sems):
    section_total, slot_total = place_ref.shape
    rows_here = dense_ref.shape[1]
    tile_dim = tiles_ref.shape[1]
    tile_span = rows_here // tile_dim

    def spot(s, k):
        place = place_ref[s, k]
        row = pl.multiple_of((place // tile_span) * tile_dim, tile_dim)
        col = pl.multiple_of((place % tile_span) * tile_dim, tile_dim)
        return dense_ref.at[s, pl.ds(row, tile_dim), pl.ds(col, tile_dim)]

    def copy(s, k):
        slot = s * slot_total + k
        return pltpu.make_async_copy(tiles_ref.at[slot], spot(s, k), sems.at[slot])

    def place_section(s, carry):
        for k in range(slot_total):

            @pl.when(k < count_ref[s])
            def _():
                copy(s, k).start()

            @pl.when(k >= count_ref[s])
            def _():
                spot(s, k)[...] = jnp.zeros((tile_dim, tile_dim), BF16)

        return carry

    lax.fori_loop(0, section_total, place_section, 0)
    degree_ref[...] = jnp.zeros_like(degree_ref)
    ones = jnp.ones((rows_here, degree_ref.shape[1]), BF16)

    def sum_section(s, carry):
        for k in range(slot_total):

            @pl.when(k < count_ref[s])
            def _():
                copy(s, k).wait()

        degree_ref[...] += jnp.dot(dense_ref[s], ones, preferred_element_type=F32)
        return carry

    lax.fori_loop(0, section_total, sum_section, 0)


def image(index_ref, own_ref, other_ref, block_refs, held):
    for d, block_ref in enumerate(block_refs):
        held[d] = block_ref[...]
    total = held[0].astype(F32)
    for core, dense_ref in enumerate((own_ref, other_ref)):
        for s in range(dense_ref.shape[0]):
            total += jnp.dot(
                dense_ref[s], held[index_ref[core, s]], preferred_element_type=F32
            )
    return total


def first_kernel(block_total, index_ref, own_ref, other_ref, scale_ref, *refs):
    block_refs = refs[:block_total]
    heat_ref, second_ref, held = refs[block_total:]
    scale = scale_ref[...]
    heat = scale * image(index_ref, own_ref, other_ref, block_refs, held)
    heat_ref[...] = heat
    second_ref[...] = (scale * heat).astype(BF16)


def second_kernel(
    block_total, index_ref, replica_ref, own_ref, other_ref, scale_ref, heat_ref, feature_ref, *refs
):
    block_refs = refs[:block_total]
    keep_ref, send_ref, held, mixed = refs[block_total:]
    heat_two = scale_ref[...] * image(index_ref, own_ref, other_ref, block_refs, held)
    mixed[...] = (
        feature_ref[...].astype(F32) + 5.0 * heat_ref[...] + 12.5 * heat_two
    ).astype(BF16)
    half = keep_ref.shape[0]
    replica = replica_ref[0]
    keep_ref[...] = mixed[pl.ds(pl.multiple_of(replica * half, half), half), :]
    send_ref[...] = mixed[pl.ds(pl.multiple_of((1 - replica) * half, half), half), :]


def per_device(features, weight, tiles, tile_place, panel_count):
    rows_here, width = features.shape
    section_total = panel_count.shape[0]
    row_total = lax.axis_size("rows")
    rep_total = lax.axis_size("rep")
    row_index = lax.axis_index("rows")
    replica = lax.axis_index("rep")
    half_rows = rows_here // rep_total
    part = width // rep_total
    shape = jax.ShapeDtypeStruct

    dense, degree = pl.pallas_call(
        place_kernel,
        out_shape=(
            shape((section_total, rows_here, rows_here), BF16),
            shape((rows_here, part), F32),
        ),
        in_specs=[SMEM, SMEM, ANY],
        out_specs=(VMEM, VMEM),
        scratch_shapes=[pltpu.SemaphoreType.DMA((tiles.shape[0],))],
        compiler_params=PARAMS,
    )(tile_place, panel_count, tiles)
    scale = lax.rsqrt(1.0 + (degree + swapped(degree, "rep")))
    features_part = lax.dynamic_slice_in_dim(features, replica * part, part, 1)
    first = (scale * features_part).astype(BF16)
    dense_other = swapped(dense, "rep")

    cores = jnp.stack([replica, 1 - replica])[:, None]
    steps = cores + rep_total * jnp.arange(section_total)[None, :]
    index = (row_index ^ ((row_index - steps) % row_total)).astype(jnp.int32)

    blocks = gathered(first, "rows", row_total)
    held = pltpu.VMEM((row_total, rows_here, part), BF16)
    heat_one, second = pl.pallas_call(
        functools.partial(first_kernel, row_total),
        out_shape=(shape((rows_here, part), F32), shape((rows_here, part), BF16)),
        in_specs=[SMEM] + [VMEM] * (3 + row_total),
        out_specs=(VMEM, VMEM),
        scratch_shapes=[held],
        compiler_params=PARAMS,
    )(index, dense, dense_other, scale, *blocks)

    blocks = gathered(second, "rows", row_total)
    keep, send = pl.pallas_call(
        functools.partial(second_kernel, row_total),
        out_shape=(shape((half_rows, part), BF16),) * 2,
        in_specs=[SMEM, SMEM] + [VMEM] * (5 + row_total),
        out_specs=(VMEM, VMEM),
        scratch_shapes=[held, pltpu.VMEM((rows_here, part), BF16)],
        compiler_params=PARAMS,
    )(index, replica.reshape(1), dense, dense_other, scale, heat_one, features_part, *blocks)
    got = swapped(send, "rep")
    weight_own = lax.dynamic_slice_in_dim(weight, replica * part, part, 0)
    weight_other = lax.dynamic_slice_in_dim(weight, (1 - replica) * part, part, 0)
    return (
        jnp.dot(keep, weight_own, preferred_element_type=F32)
        + jnp.dot(got, weight_other, preferred_element_type=F32)
    ).astype(BF16)


def solution(mesh):
    in_specs = (
        P(("groups", "rows"), None),
        P(),
        P(("groups", "rows", "rep"), None, None),
        P(("groups", "rows", "rep"), None),
        P(("groups", "rows", "rep")),
    )
    out_specs = P(("groups", "rows", "rep"), None)
    return jax.shard_map(
        per_device, mesh=mesh, in_specs=in_specs, out_specs=out_specs, check_vma=False
    )
```

time: 161 us -> 69.5 us (0.43)
  waiting for transfers between devices: 69.4 us -> 25 us
  matrix products: 28 us -> 1.85 us
  local copies, waits for them, and re-layouts: 25.3 us -> 1.98 us
  starting transfers between devices: 4.82 us -> 23.1 us
  Pallas kernels: 0 us -> 15.3 us
  between operations: 13.6 us -> 0.13 us
  other arithmetic: 13.6 us -> 2.5 us
  blocking collectives: 4.71 us -> 0 us
    ppermute x8 -> x17, waiting for transfers between devices: 59.1 us -> 25 us  [the longest x14 19.3 us: xor_permute(): lax.ppermute(block, axis, [(i, i ^ distance) for i in range(lax.axis_size...]
    dot_general x18 -> x2, matrix products: 28 us -> 1.85 us  [the longest x1 1.68 us: per_device(): jnp.dot(keep, weight_own, preferred_element_type=F32)]
    ppermute x8 -> x17, starting transfers between devices: 4.74 us -> 23.1 us  [the longest x14 22.4 us: xor_permute(): lax.ppermute(block, axis, [(i, i ^ distance) for i in range(lax.axis_size...]
    pallas_call x0 -> x3, Pallas kernels: none -> 15.3 us  [the longest x1 6.09 us: per_device(): pl.pallas_call(place_kernel, out_shape=(shape((section_total, rows_here,...]
    reduce_scatter x2 -> x0, waiting for transfers between devices: 10.2 us -> none  [the longest x1 5.41 us: per_device(): lax.psum_scatter(part_two, 'rep', scatter_dimension=0, tiled=True)]
    dot_general x10 -> x0, local copies, waits for them, and re-layouts: 8.64 us -> none  [the longest x2 6.21 us: panel_term(): jnp.einsum('kij,kjf->kif', squares, inputs, preferred_element_type=jnp.fl...]
    lt x8 -> x0, other arithmetic: 7.46 us -> none  [the longest x7 7.39 us: panel_term(): is_alive = 0 + jnp.arange(slot_total) < filled]
    gather x8 -> x0, local copies, waits for them, and re-layouts: 7.03 us -> none  [panel_term(): inputs = jnp.take(pieces, spots_all % tile_span, axis=0)]
  transfers between devices with their start and end apart: 10 -> 17, of which waited for: 10 -> 12; matrix products, arithmetic and copies ran while one was open for 8% -> 4% of each run, Pallas kernels for 0% -> 0%
where the time goes in v1:
time: 69.5 us; the launch traced here: 69.9 us
  waiting for transfers between devices  25 us (36%)
  starting transfers between devices  23.1 us (33%)
  Pallas kernels  15.3 us (22%)
  other arithmetic  2.5 us (4%)
  local copies, waits for them, and re-layouts  1.98 us (3%)
  matrix products  1.85 us (3%)
    ppermute x14, starting transfers between devices, xor_permute(): lax.ppermute(block, axis, [(i, i ^ distance) for i in range(lax.axis_size...  22.4 us
    ppermute x14, waiting for transfers between devices, xor_permute(): lax.ppermute(block, axis, [(i, i ^ distance) for i in range(lax.axis_size...  19.3 us
    pallas_call x1, Pallas kernels, per_device(): pl.pallas_call(place_kernel, out_shape=(shape((section_total, rows_here,...  6.09 us
    ppermute x3, waiting for transfers between devices, swapped(): return lax.ppermute(block, axis, [(0, 1), (1, 0)])  5.76 us
    pallas_call x1, Pallas kernels, per_device(): pl.pallas_call(functools.partial(second_kernel, row_total), out_shape=(sh...  4.63 us
    pallas_call x1, Pallas kernels, per_device(): pl.pallas_call(functools.partial(first_kernel, row_total), out_shape=(sha...  4.6 us
    unnamed x36, local copies, waits for them, and re-layouts  1.98 us
    convert_element_type x1, other arithmetic, per_device(): first = (scale * features_part).astype(BF16)  1.77 us
  transfers between devices with their start and end apart: 17, of which 12 were waited for; matrix products, arithmetic and copies ran while one was open for 4% of the time, Pallas kernels for 0%

profile of v1, /device:TPU:0, one launch (start us, length us, event | category | flops | bytes accessed | tf_op | source)
XLA Modules:
  0.0 69.9 jit_solution(5762889862238138893)
XLA Ops:
  0.0 6.1 %shard_map.55 = (bf16[4,512,512]{2,1,0:T(8,128)(2,1)}, f32[512,128]{1,0:T(8,128)}) custom-call(s32[4,16]{1,0:T(4,128)} %place_ref.1, s32[4]{0:T(128)} %count_ref.1, bf16[64,128,128]{2,1,0:T(8,128)(2,1)} %tiles_ref.1), custom_call_target="tpu_custom_call" | custom-call | tf_op jit(solution)/shard_map/pallas_call | solution.py:130
  6.7 4.3 %collective-permute-done.1 = f32[512,128]{1,0:T(8,128)S(1)} collective-permute-done((f32[512,128]{1,0:T(8,128)}, f32[512,128]{1,0:T(8,128)S(1)}, u32[]{:S(2)}, u32[]{:S(2)}) %collective-permute-start.1) | collective-permute-done | bytes 262176 | tf_op jit(solution)/shard_map/ppermute | solution.py:34
  11.0 1.8 %multiply_convert_fusion = (bf16[512,128]{1,0:T(8,128)(2,1)S(1)}, bf16[512,128]{1,0:T(8,128)(2,1)}, f32[512,128]{1,0:T(8,128)}) fusion(bf16[512,256]{1,0:T(8,128)(2,1)S(1)} %copy-done.17, s32[]{:T(128)S(6)} %select_n.15, f32[512,128]{1,0:T(8,128)} %get-tuple-element.12, f32[512,128]{1,0:T(8,128)S(1)} %collective-permute-done.1), kind=kLoop, calls=%fused_computation.2 | loop fusion | flops 327680 | bytes 1179652 | tf_op jit(solution)/shard_map/convert_element_type | solution.py:143
  12.8 3.7 %collective-permute-start.5 = (bf16[512,128]{1,0:T(8,128)(2,1)S(1)}, bf16[512,128]{1,0:T(8,128)(2,1)S(1)}, u32[]{:S(2)}, u32[]{:S(2)}) collective-permute-start(bf16[512,128]{1,0:T(8,128)(2,1)S(1)} %get-tuple-element.17.refs_0_), channel_id=1, source_target_pairs={{0,8},{2,10},{4,12},{6,14},{8,0},{10,2},{12,4},{14,6},{1,9},{3,11}... | collective-permute-start | bytes 393224 | tf_op jit(solution)/shard_map/ppermute | solution.py:19
  16.5 1.5 %collective-permute-start.3 = (bf16[512,128]{1,0:T(8,128)(2,1)S(1)}, bf16[512,128]{1,0:T(8,128)(2,1)S(1)}, u32[]{:S(2)}, u32[]{:S(2)}) collective-permute-start(bf16[512,128]{1,0:T(8,128)(2,1)S(1)} %get-tuple-element.17.refs_0_), channel_id=1, source_target_pairs={{0,4},{2,6},{4,0},{6,2},{8,12},{10,14},{12,8},{14,10},{1,5},{3,7},... | collective-permute-start | bytes 393224 | tf_op jit(solution)/shard_map/ppermute | solution.py:19
  18.0 1.8 %collective-permute-start.2 = (bf16[512,128]{1,0:T(8,128)(2,1)S(1)}, bf16[512,128]{1,0:T(8,128)(2,1)S(1)}, u32[]{:S(2)}, u32[]{:S(2)}) collective-permute-start(bf16[512,128]{1,0:T(8,128)(2,1)S(1)} %get-tuple-element.17.refs_0_), channel_id=1, source_target_pairs={{0,2},{2,0},{4,6},{6,4},{8,10},{10,8},{12,14},{14,12},{1,3},{3,1},... | collective-permute-start | bytes 393224 | tf_op jit(solution)/shard_map/ppermute | solution.py:19
  19.9 3.3 %collective-permute-done.5.refs_4_ = bf16[512,128]{1,0:T(8,128)(2,1)S(1)} collective-permute-done((bf16[512,128]{1,0:T(8,128)(2,1)S(1)}, bf16[512,128]{1,0:T(8,128)(2,1)S(1)}, u32[]{:S(2)}, u32[]{:S(2)}) %collective-permute-start.5) | collective-permute-done | bytes 131104 | tf_op jit(solution)/shard_map/ppermute | solution.py:19
  23.3 1.6 %collective-permute-start.8 = (bf16[512,128]{1,0:T(8,128)(2,1)S(1)}, bf16[512,128]{1,0:T(8,128)(2,1)S(1)}, u32[]{:S(2)}, u32[]{:S(2)}) collective-permute-start(bf16[512,128]{1,0:T(8,128)(2,1)S(1)} %collective-permute-done.5.refs_4_), channel_id=1, source_target_pairs={{0,6},{2,4},{4,2},{6,0},{8,14},{10,12},{12,10},{14,8},{1,7},{3,5},... | collective-permute-start | bytes 393224 | tf_op jit(solution)/shard_map/ppermute | solution.py:19
  24.8 1.4 %collective-permute-start.7 = (bf16[512,128]{1,0:T(8,128)(2,1)S(1)}, bf16[512,128]{1,0:T(8,128)(2,1)S(1)}, u32[]{:S(2)}, u32[]{:S(2)}) collective-permute-start(bf16[512,128]{1,0:T(8,128)(2,1)S(1)} %collective-permute-done.5.refs_4_), channel_id=1, source_target_pairs={{0,4},{2,6},{4,0},{6,2},{8,12},{10,14},{12,8},{14,10},{1,5},{3,7},... | collective-permute-start | bytes 393224 | tf_op jit(solution)/shard_map/ppermute | solution.py:19
  26.8 1.5 %collective-permute-start.4 = (bf16[512,128]{1,0:T(8,128)(2,1)S(1)}, bf16[512,128]{1,0:T(8,128)(2,1)S(1)}, u32[]{:S(2)}, u32[]{:S(2)}) collective-permute-start(bf16[512,128]{1,0:T(8,128)(2,1)S(1)} %collective-permute-done.3.refs_2_), channel_id=1, source_target_pairs={{0,2},{2,0},{4,6},{6,4},{8,10},{10,8},{12,14},{14,12},{1,3},{3,1},... | collective-permute-start | bytes 393224 | tf_op jit(solution)/shard_map/ppermute | solution.py:19
  28.3 0.7 fusion.4.index_ref
  28.9 1.6 %collective-permute-done.8.refs_7_ = bf16[512,128]{1,0:T(8,128)(2,1)S(1)} collective-permute-done((bf16[512,128]{1,0:T(8,128)(2,1)S(1)}, bf16[512,128]{1,0:T(8,128)(2,1)S(1)}, u32[]{:S(2)}, u32[]{:S(2)}) %collective-permute-start.8) | collective-permute-done | bytes 131104 | tf_op jit(solution)/shard_map/ppermute | solution.py:19
  30.5 1.2 %collective-permute-done.7.refs_6_ = bf16[512,128]{1,0:T(8,128)(2,1)S(1)} collective-permute-done((bf16[512,128]{1,0:T(8,128)(2,1)S(1)}, bf16[512,128]{1,0:T(8,128)(2,1)S(1)}, u32[]{:S(2)}, u32[]{:S(2)}) %collective-permute-start.7) | collective-permute-done | bytes 131104 | tf_op jit(solution)/shard_map/ppermute | solution.py:19
  31.7 1.3 %collective-permute-done.6.refs_5_ = bf16[512,128]{1,0:T(8,128)(2,1)S(1)} collective-permute-done((bf16[512,128]{1,0:T(8,128)(2,1)S(1)}, bf16[512,128]{1,0:T(8,128)(2,1)S(1)}, u32[]{:S(2)}, u32[]{:S(2)}) %collective-permute-start.6) | collective-permute-done | bytes 131104 | tf_op jit(solution)/shard_map/ppermute | solution.py:19
  33.1 1.6 %collective-permute-done.4.refs_3_ = bf16[512,128]{1,0:T(8,128)(2,1)S(1)} collective-permute-done((bf16[512,128]{1,0:T(8,128)(2,1)S(1)}, bf16[512,128]{1,0:T(8,128)(2,1)S(1)}, u32[]{:S(2)}, u32[]{:S(2)}) %collective-permute-start.4) | collective-permute-done | bytes 131104 | tf_op jit(solution)/shard_map/ppermute | solution.py:19
  35.4 0.7 %copy-done.1 = bf16[4,512,512]{2,1,0:T(8,128)(2,1)} copy-done((bf16[4,512,512]{2,1,0:T(8,128)(2,1)}, bf16[4,512,512]{2,1,0:T(8,128)(2,1)S(1)}, u32[]{:S(2)}) %copy-start.1) | copy-done | bytes 2097176
  36.1 4.6 %shard_map.56 = (f32[512,128]{1,0:T(8,128)}, bf16[512,128]{1,0:T(8,128)(2,1)}) custom-call(s32[2,4]{1,0:T(2,128)} %fusion.4.index_ref, bf16[4,512,512]{2,1,0:T(8,128)(2,1)} %get-tuple-element.11.own_ref, bf16[4,512,512]{2,1,0:T(8,128)(2,1)} %copy-done.1, f32[512,128]{1,0:T(8,128)} %get-tuple-element.19.scale_ref, bf16[512,128]{1,0:T(8,128)(2,1)} %copy-done.2, ...), custom_call_target="tpu_custom_call" | custom-call | tf_op jit(solution)/shard_map/pallas_call | solution.py:152
  40.7 2.8 %collective-permute-start.12 = (bf16[512,128]{1,0:T(8,128)(2,1)}, bf16[512,128]{1,0:T(8,128)(2,1)S(1)}, u32[]{:S(2)}, u32[]{:S(2)}) collective-permute-start(bf16[512,128]{1,0:T(8,128)(2,1)} %get-tuple-element.14.refs_0_), channel_id=1, source_target_pairs={{0,8},{2,10},{4,12},{6,14},{8,0},{10,2},{12,4},{14,6},{1,9},{3,11}... | collective-permute-start | bytes 393224 | tf_op jit(solution)/shard_map/ppermute | solution.py:19
  43.5 1.7 %collective-permute-start.10 = (bf16[512,128]{1,0:T(8,128)(2,1)}, bf16[512,128]{1,0:T(8,128)(2,1)S(1)}, u32[]{:S(2)}, u32[]{:S(2)}) collective-permute-start(bf16[512,128]{1,0:T(8,128)(2,1)} %get-tuple-element.14.refs_0_), channel_id=1, source_target_pairs={{0,4},{2,6},{4,0},{6,2},{8,12},{10,14},{12,8},{14,10},{1,5},{3,7},... | collective-permute-start | bytes 393224 | tf_op jit(solution)/shard_map/ppermute | solution.py:19
  45.2 1.6 %collective-permute-start.9 = (bf16[512,128]{1,0:T(8,128)(2,1)}, bf16[512,128]{1,0:T(8,128)(2,1)S(1)}, u32[]{:S(2)}, u32[]{:S(2)}) collective-permute-start(bf16[512,128]{1,0:T(8,128)(2,1)} %get-tuple-element.14.refs_0_), channel_id=1, source_target_pairs={{0,2},{2,0},{4,6},{6,4},{8,10},{10,8},{12,14},{14,12},{1,3},{3,1},... | collective-permute-start | bytes 393224 | tf_op jit(solution)/shard_map/ppermute | solution.py:19
  46.7 3.4 %collective-permute-done.12.refs_4_ = bf16[512,128]{1,0:T(8,128)(2,1)S(1)} collective-permute-done((bf16[512,128]{1,0:T(8,128)(2,1)}, bf16[512,128]{1,0:T(8,128)(2,1)S(1)}, u32[]{:S(2)}, u32[]{:S(2)}) %collective-permute-start.12) | collective-permute-done | bytes 131104 | tf_op jit(solution)/shard_map/ppermute | solution.py:19
  50.1 0.8 %collective-permute-start.15 = (bf16[512,128]{1,0:T(8,128)(2,1)S(1)}, bf16[512,128]{1,0:T(8,128)(2,1)S(1)}, u32[]{:S(2)}, u32[]{:S(2)}) collective-permute-start(bf16[512,128]{1,0:T(8,128)(2,1)S(1)} %collective-permute-done.12.refs_4_), channel_id=1, source_target_pairs={{0,6},{2,4},{4,2},{6,0},{8,14},{10,12},{12,10},{14,8},{1,7},{3,5},... | collective-permute-start | bytes 393224 | tf_op jit(solution)/shard_map/ppermute | solution.py:19
  51.0 1.5 %collective-permute-start.14 = (bf16[512,128]{1,0:T(8,128)(2,1)S(1)}, bf16[512,128]{1,0:T(8,128)(2,1)S(1)}, u32[]{:S(2)}, u32[]{:S(2)}) collective-permute-start(bf16[512,128]{1,0:T(8,128)(2,1)S(1)} %collective-permute-done.12.refs_4_), channel_id=1, source_target_pairs={{0,4},{2,6},{4,0},{6,2},{8,12},{10,14},{12,8},{14,10},{1,5},{3,7},... | collective-permute-start | bytes 393224 | tf_op jit(solution)/shard_map/ppermute | solution.py:19
  52.5 1.2 %collective-permute-start.13 = (bf16[512,128]{1,0:T(8,128)(2,1)S(1)}, bf16[512,128]{1,0:T(8,128)(2,1)S(1)}, u32[]{:S(2)}, u32[]{:S(2)}) collective-permute-start(bf16[512,128]{1,0:T(8,128)(2,1)S(1)} %collective-permute-done.12.refs_4_), channel_id=1, source_target_pairs={{0,2},{2,0},{4,6},{6,4},{8,10},{10,8},{12,14},{14,12},{1,3},{3,1},... | collective-permute-start | bytes 393224 | tf_op jit(solution)/shard_map/ppermute | solution.py:19
  53.6 0.9 %collective-permute-start.11 = (bf16[512,128]{1,0:T(8,128)(2,1)S(1)}, bf16[512,128]{1,0:T(8,128)(2,1)S(1)}, u32[]{:S(2)}, u32[]{:S(2)}) collective-permute-start(bf16[512,128]{1,0:T(8,128)(2,1)S(1)} %collective-permute-done.10.refs_2_), channel_id=1, source_target_pairs={{0,2},{2,0},{4,6},{6,4},{8,10},{10,8},{12,14},{14,12},{1,3},{3,1},... | collective-permute-start | bytes 393224 | tf_op jit(solution)/shard_map/ppermute | solution.py:19
  54.5 2.6 %collective-permute-done.15.refs_7_ = bf16[512,128]{1,0:T(8,128)(2,1)S(1)} collective-permute-done((bf16[512,128]{1,0:T(8,128)(2,1)S(1)}, bf16[512,128]{1,0:T(8,128)(2,1)S(1)}, u32[]{:S(2)}, u32[]{:S(2)}) %collective-permute-start.15) | collective-permute-done | bytes 131104 | tf_op jit(solution)/shard_map/ppermute | solution.py:19
  57.5 2.1 %collective-permute-done.13.refs_5_ = bf16[512,128]{1,0:T(8,128)(2,1)S(1)} collective-permute-done((bf16[512,128]{1,0:T(8,128)(2,1)S(1)}, bf16[512,128]{1,0:T(8,128)(2,1)S(1)}, u32[]{:S(2)}, u32[]{:S(2)}) %collective-permute-start.13) | collective-permute-done | bytes 131104 | tf_op jit(solution)/shard_map/ppermute | solution.py:19
  59.6 1.7 %collective-permute-done.11.refs_3_ = bf16[512,128]{1,0:T(8,128)(2,1)S(1)} collective-permute-done((bf16[512,128]{1,0:T(8,128)(2,1)S(1)}, bf16[512,128]{1,0:T(8,128)(2,1)S(1)}, u32[]{:S(2)}, u32[]{:S(2)}) %collective-permute-start.11) | collective-permute-done | bytes 131104 | tf_op jit(solution)/shard_map/ppermute | solution.py:19
  61.3 0.6 copy-done.15
  61.9 4.6 %shard_map.57 = (bf16[256,128]{1,0:T(8,128)(2,1)}, bf16[256,128]{1,0:T(8,128)(2,1)}) custom-call(s32[2,4]{1,0:T(2,128)} %fusion.4.index_ref, s32[1]{0:T(128)} %bitcast.replica_ref, bf16[4,512,512]{2,1,0:T(8,128)(2,1)} %get-tuple-element.11.own_ref, bf16[4,512,512]{2,1,0:T(8,128)(2,1)} %copy-done.1, f32[512,128]{1,0:T(8,128)} %get-tuple-element.19.scale_ref, ...), custom_call_target="tpu_custom_call" | custom-call | tf_op jit(solution)/shard_map/pallas_call | solution.py:162
  66.6 1.5 %collective-permute-done.16 = bf16[256,128]{1,0:T(8,128)(2,1)S(1)} collective-permute-done((bf16[256,128]{1,0:T(8,128)(2,1)}, bf16[256,128]{1,0:T(8,128)(2,1)S(1)}, u32[]{:S(2)}, u32[]{:S(2)}) %collective-permute-start.16) | collective-permute-done | bytes 65568 | tf_op jit(solution)/shard_map/ppermute | solution.py:34
  68.2 1.7 %fusion = bf16[256,256]{1,0:T(8,128)(2,1)} fusion(f32[256,256]{1,0:T(8,128)S(1)} %fusion.1, bf16[256,128]{1,0:T(8,128)(2,1)} %get-tuple-element.15, bf16[256,256]{1,0:T(8,128)(2,1)S(1)} %copy-done, s32[]{:T(128)S(6)} %select_n.15), kind=kOutput, calls=%fused_computation.1 | convolution fusion | flops 16908288 | bytes 524292 | tf_op jit(solution)/shard_map/dot_general | solution.py:174
  (47 shorter events, 2.4 us)
Async XLA Ops:
  0.0 68.0 %copy-start = (bf16[256,256]{1,0:T(8,128)(2,1)S(1)}, bf16[256,256]{1,0:T(8,128)(2,1)}, u32[]{:S(2)}) copy-start(bf16[256,256]{1,0:T(8,128)(2,1)} %param.6) | copy-start | bytes 393220
  0.0 11.0 %copy-start.17 = (bf16[512,256]{1,0:T(8,128)(2,1)S(1)}, bf16[512,256]{1,0:T(8,128)(2,1)}, u32[]{:S(2)}) copy-start(bf16[512,256]{1,0:T(8,128)(2,1)} %param.5) | copy-start | bytes 786436
  6.1 28.6 %collective-permute-start = (bf16[4,512,512]{2,1,0:T(8,128)(2,1)}, bf16[4,512,512]{2,1,0:T(8,128)(2,1)S(1)}, u32[]{:S(2)}, u32[]{:S(2)}) collective-permute-start(bf16[4,512,512]{2,1,0:T(8,128)(2,1)} %get-tuple-element.11.own_ref), channel_id=1, source_target_pairs={{0,1},{1,0},{2,3},{3,2},{4,5},{5,4},{6,7},{7,6},{8,9},{9,8},{10,11... | collective-permute-start | bytes 6291464 | tf_op jit(solution)/shard_map/ppermute | solution.py:34
  6.7 4.4 %collective-permute-start.1 = (f32[512,128]{1,0:T(8,128)}, f32[512,128]{1,0:T(8,128)S(1)}, u32[]{:S(2)}, u32[]{:S(2)}) collective-permute-start(f32[512,128]{1,0:T(8,128)} %get-tuple-element.12), channel_id=1, source_target_pairs={{0,1},{1,0},{2,3},{3,2},{4,5},{5,4},{6,7},{7,6},{8,9},{9,8},{10,11... | collective-permute-start | bytes 786440 | tf_op jit(solution)/shard_map/ppermute | solution.py:34
  12.8 21.9 %copy-start.2 = (bf16[512,128]{1,0:T(8,128)(2,1)}, bf16[512,128]{1,0:T(8,128)(2,1)S(1)}, u32[]{:S(2)}) copy-start(bf16[512,128]{1,0:T(8,128)(2,1)S(1)} %get-tuple-element.17.refs_0_) | copy-start | bytes 393220
  12.8 10.5 %collective-permute-start.5 = (bf16[512,128]{1,0:T(8,128)(2,1)S(1)}, bf16[512,128]{1,0:T(8,128)(2,1)S(1)}, u32[]{:S(2)}, u32[]{:S(2)}) collective-permute-start(bf16[512,128]{1,0:T(8,128)(2,1)S(1)} %get-tuple-element.17.refs_0_), channel_id=1, source_target_pairs={{0,8},{2,10},{4,12},{6,14},{8,0},{10,2},{12,4},{14,6},{1,9},{3,11}... | collective-permute-start | bytes 393224 | tf_op jit(solution)/shard_map/ppermute | solution.py:19
  16.5 9.7 %collective-permute-start.3 = (bf16[512,128]{1,0:T(8,128)(2,1)S(1)}, bf16[512,128]{1,0:T(8,128)(2,1)S(1)}, u32[]{:S(2)}, u32[]{:S(2)}) collective-permute-start(bf16[512,128]{1,0:T(8,128)(2,1)S(1)} %get-tuple-element.17.refs_0_), channel_id=1, source_target_pairs={{0,4},{2,6},{4,0},{6,2},{8,12},{10,14},{12,8},{14,10},{1,5},{3,7},... | collective-permute-start | bytes 393224 | tf_op jit(solution)/shard_map/ppermute | solution.py:19
  18.0 8.8 %collective-permute-start.2 = (bf16[512,128]{1,0:T(8,128)(2,1)S(1)}, bf16[512,128]{1,0:T(8,128)(2,1)S(1)}, u32[]{:S(2)}, u32[]{:S(2)}) collective-permute-start(bf16[512,128]{1,0:T(8,128)(2,1)S(1)} %get-tuple-element.17.refs_0_), channel_id=1, source_target_pairs={{0,2},{2,0},{4,6},{6,4},{8,10},{10,8},{12,14},{14,12},{1,3},{3,1},... | collective-permute-start | bytes 393224 | tf_op jit(solution)/shard_map/ppermute | solution.py:19
  23.3 11.5 %copy-start.3 = (bf16[512,128]{1,0:T(8,128)(2,1)}, bf16[512,128]{1,0:T(8,128)(2,1)S(1)}, u32[]{:S(2)}) copy-start(bf16[512,128]{1,0:T(8,128)(2,1)S(1)} %collective-permute-done.5.refs_4_) | copy-start | bytes 393220
  23.3 7.2 %collective-permute-start.8 = (bf16[512,128]{1,0:T(8,128)(2,1)S(1)}, bf16[512,128]{1,0:T(8,128)(2,1)S(1)}, u32[]{:S(2)}, u32[]{:S(2)}) collective-permute-start(bf16[512,128]{1,0:T(8,128)(2,1)S(1)} %collective-permute-done.5.refs_4_), channel_id=1, source_target_pairs={{0,6},{2,4},{4,2},{6,0},{8,14},{10,12},{12,10},{14,8},{1,7},{3,5},... | collective-permute-start | bytes 393224 | tf_op jit(solution)/shard_map/ppermute | solution.py:19
  24.8 6.9 %collective-permute-start.7 = (bf16[512,128]{1,0:T(8,128)(2,1)S(1)}, bf16[512,128]{1,0:T(8,128)(2,1)S(1)}, u32[]{:S(2)}, u32[]{:S(2)}) collective-permute-start(bf16[512,128]{1,0:T(8,128)(2,1)S(1)} %collective-permute-done.5.refs_4_), channel_id=1, source_target_pairs={{0,4},{2,6},{4,0},{6,2},{8,12},{10,14},{12,8},{14,10},{1,5},{3,7},... | collective-permute-start | bytes 393224 | tf_op jit(solution)/shard_map/ppermute | solution.py:19
  26.2 8.5 %copy-start.4 = (bf16[512,128]{1,0:T(8,128)(2,1)}, bf16[512,128]{1,0:T(8,128)(2,1)S(1)}, u32[]{:S(2)}) copy-start(bf16[512,128]{1,0:T(8,128)(2,1)S(1)} %collective-permute-done.3.refs_2_) | copy-start | bytes 393220
  26.3 6.8 %collective-permute-start.6 = (bf16[512,128]{1,0:T(8,128)(2,1)S(1)}, bf16[512,128]{1,0:T(8,128)(2,1)S(1)}, u32[]{:S(2)}, u32[]{:S(2)}) collective-permute-start(bf16[512,128]{1,0:T(8,128)(2,1)S(1)} %collective-permute-done.5.refs_4_), channel_id=1, source_target_pairs={{0,2},{2,0},{4,6},{6,4},{8,10},{10,8},{12,14},{14,12},{1,3},{3,1},... | collective-permute-start | bytes 393224 | tf_op jit(solution)/shard_map/ppermute | solution.py:19
  26.8 8.0 %copy-start.5 = (bf16[512,128]{1,0:T(8,128)(2,1)}, bf16[512,128]{1,0:T(8,128)(2,1)S(1)}, u32[]{:S(2)}) copy-start(bf16[512,128]{1,0:T(8,128)(2,1)S(1)} %collective-permute-done.2.refs_1_) | copy-start | bytes 393220
  26.8 7.9 %collective-permute-start.4 = (bf16[512,128]{1,0:T(8,128)(2,1)S(1)}, bf16[512,128]{1,0:T(8,128)(2,1)S(1)}, u32[]{:S(2)}, u32[]{:S(2)}) collective-permute-start(bf16[512,128]{1,0:T(8,128)(2,1)S(1)} %collective-permute-done.3.refs_2_), channel_id=1, source_target_pairs={{0,2},{2,0},{4,6},{6,4},{8,10},{10,8},{12,14},{14,12},{1,3},{3,1},... | collective-permute-start | bytes 393224 | tf_op jit(solution)/shard_map/ppermute | solution.py:19
  30.5 4.2 %copy-start.10 = (bf16[512,128]{1,0:T(8,128)(2,1)}, bf16[512,128]{1,0:T(8,128)(2,1)S(1)}, u32[]{:S(2)}) copy-start(bf16[512,128]{1,0:T(8,128)(2,1)S(1)} %collective-permute-done.8.refs_7_) | copy-start | bytes 393220
  31.7 3.0 %copy-start.12 = (bf16[512,128]{1,0:T(8,128)(2,1)}, bf16[512,128]{1,0:T(8,128)(2,1)S(1)}, u32[]{:S(2)}) copy-start(bf16[512,128]{1,0:T(8,128)(2,1)S(1)} %collective-permute-done.7.refs_6_) | copy-start | bytes 393220
  33.1 1.7 %copy-start.14 = (bf16[512,128]{1,0:T(8,128)(2,1)}, bf16[512,128]{1,0:T(8,128)(2,1)S(1)}, u32[]{:S(2)}) copy-start(bf16[512,128]{1,0:T(8,128)(2,1)S(1)} %collective-permute-done.6.refs_5_) | copy-start | bytes 393220
  40.7 9.5 %collective-permute-start.12 = (bf16[512,128]{1,0:T(8,128)(2,1)}, bf16[512,128]{1,0:T(8,128)(2,1)S(1)}, u32[]{:S(2)}, u32[]{:S(2)}) collective-permute-start(bf16[512,128]{1,0:T(8,128)(2,1)} %get-tuple-element.14.refs_0_), channel_id=1, source_target_pairs={{0,8},{2,10},{4,12},{6,14},{8,0},{10,2},{12,4},{14,6},{1,9},{3,11}... | collective-permute-start | bytes 393224 | tf_op jit(solution)/shard_map/ppermute | solution.py:19
  43.5 10.1 %collective-permute-start.10 = (bf16[512,128]{1,0:T(8,128)(2,1)}, bf16[512,128]{1,0:T(8,128)(2,1)S(1)}, u32[]{:S(2)}, u32[]{:S(2)}) collective-permute-start(bf16[512,128]{1,0:T(8,128)(2,1)} %get-tuple-element.14.refs_0_), channel_id=1, source_target_pairs={{0,4},{2,6},{4,0},{6,2},{8,12},{10,14},{12,8},{14,10},{1,5},{3,7},... | collective-permute-start | bytes 393224 | tf_op jit(solution)/shard_map/ppermute | solution.py:19
  45.2 9.3 %collective-permute-start.9 = (bf16[512,128]{1,0:T(8,128)(2,1)}, bf16[512,128]{1,0:T(8,128)(2,1)S(1)}, u32[]{:S(2)}, u32[]{:S(2)}) collective-permute-start(bf16[512,128]{1,0:T(8,128)(2,1)} %get-tuple-element.14.refs_0_), channel_id=1, source_target_pairs={{0,2},{2,0},{4,6},{6,4},{8,10},{10,8},{12,14},{14,12},{1,3},{3,1},... | collective-permute-start | bytes 393224 | tf_op jit(solution)/shard_map/ppermute | solution.py:19
  50.1 11.1 %copy-start.6 = (bf16[512,128]{1,0:T(8,128)(2,1)}, bf16[512,128]{1,0:T(8,128)(2,1)S(1)}, u32[]{:S(2)}) copy-start(bf16[512,128]{1,0:T(8,128)(2,1)S(1)} %collective-permute-done.12.refs_4_) | copy-start | bytes 393220
  50.1 7.0 %collective-permute-start.15 = (bf16[512,128]{1,0:T(8,128)(2,1)S(1)}, bf16[512,128]{1,0:T(8,128)(2,1)S(1)}, u32[]{:S(2)}, u32[]{:S(2)}) collective-permute-start(bf16[512,128]{1,0:T(8,128)(2,1)S(1)} %collective-permute-done.12.refs_4_), channel_id=1, source_target_pairs={{0,6},{2,4},{4,2},{6,0},{8,14},{10,12},{12,10},{14,8},{1,7},{3,5},... | collective-permute-start | bytes 393224 | tf_op jit(solution)/shard_map/ppermute | solution.py:19
  51.0 6.5 %collective-permute-start.14 = (bf16[512,128]{1,0:T(8,128)(2,1)S(1)}, bf16[512,128]{1,0:T(8,128)(2,1)S(1)}, u32[]{:S(2)}, u32[]{:S(2)}) collective-permute-start(bf16[512,128]{1,0:T(8,128)(2,1)S(1)} %collective-permute-done.12.refs_4_), channel_id=1, source_target_pairs={{0,4},{2,6},{4,0},{6,2},{8,12},{10,14},{12,8},{14,10},{1,5},{3,7},... | collective-permute-start | bytes 393224 | tf_op jit(solution)/shard_map/ppermute | solution.py:19
  52.5 7.2 %collective-permute-start.13 = (bf16[512,128]{1,0:T(8,128)(2,1)S(1)}, bf16[512,128]{1,0:T(8,128)(2,1)S(1)}, u32[]{:S(2)}, u32[]{:S(2)}) collective-permute-start(bf16[512,128]{1,0:T(8,128)(2,1)S(1)} %collective-permute-done.12.refs_4_), channel_id=1, source_target_pairs={{0,2},{2,0},{4,6},{6,4},{8,10},{10,8},{12,14},{14,12},{1,3},{3,1},... | collective-permute-start | bytes 393224 | tf_op jit(solution)/shard_map/ppermute | solution.py:19
  53.6 7.6 %copy-start.7 = (bf16[512,128]{1,0:T(8,128)(2,1)}, bf16[512,128]{1,0:T(8,128)(2,1)S(1)}, u32[]{:S(2)}) copy-start(bf16[512,128]{1,0:T(8,128)(2,1)S(1)} %collective-permute-done.10.refs_2_) | copy-start | bytes 393220
  53.6 7.6 %collective-permute-start.11 = (bf16[512,128]{1,0:T(8,128)(2,1)S(1)}, bf16[512,128]{1,0:T(8,128)(2,1)S(1)}, u32[]{:S(2)}, u32[]{:S(2)}) collective-permute-start(bf16[512,128]{1,0:T(8,128)(2,1)S(1)} %collective-permute-done.10.refs_2_), channel_id=1, source_target_pairs={{0,2},{2,0},{4,6},{6,4},{8,10},{10,8},{12,14},{14,12},{1,3},{3,1},... | collective-permute-start | bytes 393224 | tf_op jit(solution)/shard_map/ppermute | solution.py:19
  54.5 6.8 %copy-start.8 = (bf16[512,128]{1,0:T(8,128)(2,1)}, bf16[512,128]{1,0:T(8,128)(2,1)S(1)}, u32[]{:S(2)}) copy-start(bf16[512,128]{1,0:T(8,128)(2,1)S(1)} %collective-permute-done.9.refs_1_) | copy-start | bytes 393220
  57.1 4.2 %copy-start.9 = (bf16[512,128]{1,0:T(8,128)(2,1)}, bf16[512,128]{1,0:T(8,128)(2,1)S(1)}, u32[]{:S(2)}) copy-start(bf16[512,128]{1,0:T(8,128)(2,1)S(1)} %collective-permute-done.15.refs_7_) | copy-start | bytes 393220
  57.5 3.8 %copy-start.11 = (bf16[512,128]{1,0:T(8,128)(2,1)}, bf16[512,128]{1,0:T(8,128)(2,1)S(1)}, u32[]{:S(2)}) copy-start(bf16[512,128]{1,0:T(8,128)(2,1)S(1)} %collective-permute-done.14.refs_6_) | copy-start | bytes 393220
  59.6 1.7 %copy-start.13 = (bf16[512,128]{1,0:T(8,128)(2,1)}, bf16[512,128]{1,0:T(8,128)(2,1)S(1)}, u32[]{:S(2)}) copy-start(bf16[512,128]{1,0:T(8,128)(2,1)S(1)} %collective-permute-done.13.refs_5_) | copy-start | bytes 393220
  66.6 1.5 %collective-permute-start.16 = (bf16[256,128]{1,0:T(8,128)(2,1)}, bf16[256,128]{1,0:T(8,128)(2,1)S(1)}, u32[]{:S(2)}, u32[]{:S(2)}) collective-permute-start(bf16[256,128]{1,0:T(8,128)(2,1)} %get-tuple-element.16), channel_id=1, source_target_pairs={{0,1},{1,0},{2,3},{3,2},{4,5},{5,4},{6,7},{7,6},{8,9},{9,8},{10,11... | collective-permute-start | bytes 196616 | tf_op jit(solution)/shard_map/ppermute | solution.py:34
  (3 other events, 2.7 us)

commit v2 on v1

v2 whole, which is shorter than its diff:
```python
import functools
import math

import jax
import jax.numpy as jnp
from jax import lax
from jax.experimental import pallas as pl
from jax.experimental.pallas import tpu as pltpu
from jax.sharding import PartitionSpec as P

F32 = jnp.float32
BF16 = jnp.bfloat16
VMEM = pl.BlockSpec(memory_space=pltpu.VMEM)
HBM = pl.BlockSpec(memory_space=pltpu.HBM)


def params(*arrays):
    held = sum(math.prod(shape) * jnp.dtype(kind).itemsize for shape, kind in arrays)
    return pltpu.CompilerParams(vmem_limit_bytes=held + 6 * 2**20)


def in_vmem(block):
    return pltpu.with_memory_space_constraint(block, pltpu.VMEM)


def in_hbm(block):
    return pltpu.with_memory_space_constraint(block, pltpu.HBM)


def xor_permute(block, axis, distance):
    return lax.ppermute(block, axis, [(i, i ^ distance) for i in range(lax.axis_size(axis))])


def gathered(block, axis, size):
    if size == 1:
        return [block]
    if size == 2:
        return [block, xor_permute(block, axis, 1)]
    half = size // 2
    near = gathered(block, axis, half)
    far = xor_permute(block, axis, half)
    far, *near = lax.optimization_barrier((far, *near))
    return near + [far] + [xor_permute(far, axis, d) for d in range(1, half)]


def swapped(block, axis):
    return lax.ppermute(block, axis, [(0, 1), (1, 0)])


def place_kernel(
    place_hbm, count_hbm, tiles_ref, dense_ref, degree_ref, held, place_ref, count_ref, sems
):
    section_total, slot_total = place_ref.shape
    rows_here = dense_ref.shape[1]
    tile_dim = tiles_ref.shape[1]
    tile_span = rows_here // tile_dim

    def copy(s):
        slots = pl.ds(s * slot_total, slot_total)
        return pltpu.make_async_copy(tiles_ref.at[slots], held.at[slots], sems.at[s])

    places = pltpu.make_async_copy(place_hbm, place_ref, sems.at[section_total])
    counts = pltpu.make_async_copy(count_hbm, count_ref, sems.at[section_total + 1])
    places.start()
    counts.start()
    for s in range(section_total):
        copy(s).start()
    places.wait()
    counts.wait()
    ones = jnp.ones((rows_here, degree_ref.shape[1]), BF16)
    for s in range(section_total):
        copy(s).wait()
        for k in range(slot_total):
            place = place_ref[s, k]
            row = pl.multiple_of((place // tile_span) * tile_dim, tile_dim)
            col = pl.multiple_of((place % tile_span) * tile_dim, tile_dim)
            tile = held[s * slot_total + k]
            dense_ref[s, pl.ds(row, tile_dim), pl.ds(col, tile_dim)] = jnp.where(
                k < count_ref[s], tile, jnp.zeros_like(tile)
            )
        sums = jnp.dot(dense_ref[s], ones, preferred_element_type=F32)
        if s == 0:
            degree_ref[...] = sums
        else:
            degree_ref[...] += sums


def part_of(ref, index, size):
    return ref[:, pl.ds(pl.multiple_of(index * size, size), size)]


def scale_kernel(degree_ref, other_ref, feature_ref, scale_ref, first_ref):
    scale = lax.rsqrt(1.0 + (degree_ref[...] + other_ref[...]))
    scale_ref[...] = scale
    feature = part_of(feature_ref, lax.axis_index("rep"), scale.shape[1])
    first_ref[...] = (scale * feature.astype(F32)).astype(BF16)


def image(own_ref, other_ref, block_refs, held, finish, chunk=256):
    row_total = len(block_refs)
    rep_total = row_total // own_ref.shape[0]
    row_index = lax.axis_index("rows")
    replica = lax.axis_index("rep")
    for d, block_ref in enumerate(block_refs):
        held[d] = block_ref[...]
    for low in range(0, own_ref.shape[1], chunk):
        rows = pl.ds(low, chunk)
        total = held[0, rows].astype(F32)
        for dense_ref, core in ((own_ref, replica), (other_ref, 1 - replica)):
            for s in range(dense_ref.shape[0]):
                column = lax.rem(row_index - core - rep_total * s + row_total, row_total)
                total += jnp.dot(
                    dense_ref[s, rows], held[row_index ^ column], preferred_element_type=F32
                )
        finish(rows, total)


def first_kernel(own_ref, other_ref, scale_ref, *refs):
    *block_refs, heat_ref, second_ref, held = refs

    def finish(rows, total):
        scale = scale_ref[rows]
        heat = scale * total
        heat_ref[rows] = heat
        second_ref[rows] = (scale * heat).astype(BF16)

    image(own_ref, other_ref, block_refs, held, finish)


def second_kernel(own_ref, other_ref, scale_ref, heat_ref, feature_ref, *refs):
    *block_refs, keep_ref, send_ref, held, mixed = refs
    replica = lax.axis_index("rep")
    part = mixed.shape[1]

    def finish(rows, total):
        feature = feature_ref[rows, pl.ds(pl.multiple_of(replica * part, part), part)]
        heat_two = scale_ref[rows] * total
        mixed[rows] = (feature.astype(F32) + 5.0 * heat_ref[rows] + 12.5 * heat_two).astype(BF16)

    image(own_ref, other_ref, block_refs, held, finish)
    half = keep_ref.shape[0]
    keep_ref[...] = mixed[pl.ds(pl.multiple_of(replica * half, half), half), :]
    send_ref[...] = mixed[pl.ds(pl.multiple_of((1 - replica) * half, half), half), :]


def project_kernel(keep_ref, got_ref, weight_ref, out_ref):
    replica = lax.axis_index("rep")
    part = keep_ref.shape[1]
    total = 0.0
    for mixed_ref, core in ((keep_ref, replica), (got_ref, 1 - replica)):
        weight = weight_ref[pl.ds(pl.multiple_of(core * part, part), part), :]
        total += jnp.dot(mixed_ref[...], weight, preferred_element_type=F32)
    out_ref[...] = total.astype(BF16)


def per_device(features, weight, tiles, tile_place, panel_count):
    rows_here, width = features.shape
    section_total = panel_count.shape[0]
    row_total = lax.axis_size("rows")
    rep_total = lax.axis_size("rep")
    half_rows = rows_here // rep_total
    part = width // rep_total
    shape = pltpu.VMEM
    panels = (section_total, rows_here, rows_here), BF16
    column = (rows_here, part), F32
    field = (rows_here, part), BF16
    held = (row_total, rows_here, part), BF16
    half = (half_rows, part), BF16

    dense, degree = pl.pallas_call(
        place_kernel,
        out_shape=(shape(*panels), shape(*column)),
        in_specs=[HBM, HBM, HBM],
        out_specs=(VMEM, VMEM),
        scratch_shapes=[
            pltpu.VMEM(tiles.shape, BF16),
            pltpu.SMEM(tile_place.shape, jnp.int32),
            pltpu.SMEM(panel_count.shape, jnp.int32),
            pltpu.SemaphoreType.DMA((section_total + 2,)),
        ],
        compiler_params=params(panels, panels, column),
    )(in_hbm(tile_place), in_hbm(panel_count), in_hbm(tiles))
    degree_other = swapped(degree, "rep")
    scale, first = pl.pallas_call(
        scale_kernel,
        out_shape=(shape(*column), shape(*field)),
        in_specs=[VMEM] * 3,
        out_specs=(VMEM, VMEM),
        compiler_params=params(column, column, column, column),
    )(degree, degree_other, features)

    blocks = gathered(first, "rows", row_total)
    dense_late, blocks[1] = lax.optimization_barrier((dense, blocks[1]))
    dense_other = in_vmem(swapped(dense_late, "rep"))
    heat_one, second = pl.pallas_call(
        first_kernel,
        out_shape=(shape(*column), shape(*field)),
        in_specs=[VMEM] * (3 + row_total),
        out_specs=(VMEM, VMEM),
        scratch_shapes=[pltpu.VMEM(*held)],
        compiler_params=params(panels, panels, column, column, held, held),
    )(dense, dense_other, scale, *blocks)

    blocks = gathered(second, "rows", row_total)
    keep, send = pl.pallas_call(
        second_kernel,
        out_shape=(shape(*half), shape(*half)),
        in_specs=[VMEM] * (5 + row_total),
        out_specs=(VMEM, VMEM),
        scratch_shapes=[pltpu.VMEM(*held), pltpu.VMEM(*field)],
        compiler_params=params(panels, panels, column, column, column, held, held),
    )(dense, dense_other, scale, heat_one, features, *blocks)
    got = swapped(send, "rep")
    return pl.pallas_call(
        project_kernel,
        out_shape=jax.ShapeDtypeStruct((half_rows, width), BF16),
        in_specs=[VMEM] * 3,
        out_specs=VMEM,
        compiler_params=params(column, column),
    )(keep, got, in_vmem(weight))


def solution(mesh):
    in_specs = (
        P(("groups", "rows"), None),
        P(),
        P(("groups", "rows", "rep"), None, None),
        P(("groups", "rows", "rep"), None),
        P(("groups", "rows", "rep")),
    )
    out_specs = P(("groups", "rows", "rep"), None)
    return jax.shard_map(
        per_device, mesh=mesh, in_specs=in_specs, out_specs=out_specs, check_vma=False
    )
```

time: 69.5 us -> 58.3 us (0.84)
  Pallas kernels: 15.3 us -> 6.66 us
  waiting for transfers between devices: 25 us -> 30.1 us
  other arithmetic: 2.5 us -> 0 us
  local copies, waits for them, and re-layouts: 1.98 us -> 0.01 us
  matrix products: 1.85 us -> 0 us
  starting transfers between devices: 23.1 us -> 21.3 us
    pallas_call x3 -> x5, Pallas kernels: 15.3 us -> 6.66 us  [the longest x1 3.08 us: per_device(): pl.pallas_call(place_kernel, out_shape=(shape(*panels), shape(*column)),...]
    ppermute x14, waiting for transfers between devices: 19.3 us -> 27.7 us  [xor_permute(): lax.ppermute(block, axis, [(i, i ^ distance) for i in range(lax.axis_size...]
    ppermute x3, waiting for transfers between devices: 5.76 us -> 2.41 us  [swapped(): return lax.ppermute(block, axis, [(0, 1), (1, 0)])]
    unnamed x36 -> x4, local copies, waits for them, and re-layouts: 1.98 us -> 0.01 us
    dot_general x2 -> x0, matrix products: 1.85 us -> none  [the longest x1 1.68 us: per_device(): jnp.dot(keep, weight_own, preferred_element_type=F32)]
    convert_element_type x1 -> x0, other arithmetic: 1.77 us -> none  [per_device(): first = (scale * features_part).astype(BF16)]
    ppermute x14, starting transfers between devices: 22.4 us -> 20.8 us  [xor_permute(): lax.ppermute(block, axis, [(i, i ^ distance) for i in range(lax.axis_size...]
  transfers between devices with their start and end apart: 17 -> 17, of which waited for: 12 -> 15; matrix products, arithmetic and copies ran while one was open for 4% -> 0% of each run, Pallas kernels for 0% -> 0%
where the time goes in v2:
time: 58.3 us; the launch traced here: 58.1 us
  waiting for transfers between devices  30.1 us (52%)
  starting transfers between devices  21.3 us (37%)
  Pallas kernels  6.66 us (11%)
    ppermute x14, waiting for transfers between devices, xor_permute(): lax.ppermute(block, axis, [(i, i ^ distance) for i in range(lax.axis_size...  27.7 us
    ppermute x14, starting transfers between devices, xor_permute(): lax.ppermute(block, axis, [(i, i ^ distance) for i in range(lax.axis_size...  20.8 us
    pallas_call x1, Pallas kernels, per_device(): pl.pallas_call(place_kernel, out_shape=(shape(*panels), shape(*column)),...  3.08 us
    ppermute x3, waiting for transfers between devices, swapped(): return lax.ppermute(block, axis, [(0, 1), (1, 0)])  2.41 us
    pallas_call x1, Pallas kernels, per_device(): pl.pallas_call(second_kernel, out_shape=(shape(*half), shape(*half)), in_...  1.35 us
    pallas_call x1, Pallas kernels, per_device(): pl.pallas_call(first_kernel, out_shape=(shape(*column), shape(*field)), i...  1.32 us
  transfers between devices with their start and end apart: 17, of which 15 were waited for; matrix products, arithmetic and copies ran while one was open for 0% of the time, Pallas kernels for 0%

profile of v2, /device:TPU:0, one launch (start us, length us, event | category | flops | bytes accessed | tf_op | source)
XLA Modules:
  0.0 58.1 jit_solution(1350098597134943515)
XLA Ops:
  0.0 3.1 %shard_map.55 = (bf16[4,512,512]{2,1,0:T(8,128)(2,1)S(1)}, f32[512,128]{1,0:T(8,128)S(1)}) custom-call(s32[4,16]{1,0:T(4,128)} %place_hbm.1, s32[4]{0:T(128)} %count_hbm.1, bf16[64,128,128]{2,1,0:T(8,128)(2,1)} %tiles_ref.1), custom_call_target="tpu_custom_call" | custom-call | tf_op jit(solution)/shard_map/pallas_call | solution.py:170
  3.1 0.5 collective-permute-start
  3.6 1.2 %collective-permute-done.other_ref = f32[512,128]{1,0:T(8,128)S(1)} collective-permute-done((f32[512,128]{1,0:T(8,128)S(1)}, f32[512,128]{1,0:T(8,128)S(1)}, u32[]{:S(2)}, u32[]{:S(2)}) %collective-permute-start) | collective-permute-done | bytes 262176 | tf_op jit(solution)/shard_map/ppermute | solution.py:47
  4.8 3.0 %collective-permute-start.3 = (bf16[512,128]{1,0:T(8,128)(2,1)S(1)}, bf16[512,128]{1,0:T(8,128)(2,1)S(1)}, u32[]{:S(2)}, u32[]{:S(2)}) collective-permute-start(bf16[512,128]{1,0:T(8,128)(2,1)S(1)} %get-tuple-element.40.refs_0_), channel_id=1, source_target_pairs={{0,2},{2,0},{4,6},{6,4},{8,10},{10,8},{12,14},{14,12},{1,3},{3,1},... | collective-permute-start | bytes 393224 | tf_op jit(solution)/shard_map/ppermute | solution.py:31
  7.8 1.6 %collective-permute-start.2 = (bf16[512,128]{1,0:T(8,128)(2,1)S(1)}, bf16[512,128]{1,0:T(8,128)(2,1)S(1)}, u32[]{:S(2)}, u32[]{:S(2)}) collective-permute-start(bf16[512,128]{1,0:T(8,128)(2,1)S(1)} %get-tuple-element.40.refs_0_), channel_id=1, source_target_pairs={{0,4},{2,6},{4,0},{6,2},{8,12},{10,14},{12,8},{14,10},{1,5},{3,7},... | collective-permute-start | bytes 393224 | tf_op jit(solution)/shard_map/ppermute | solution.py:31
  9.4 2.6 %collective-permute-start.1 = (bf16[512,128]{1,0:T(8,128)(2,1)S(1)}, bf16[512,128]{1,0:T(8,128)(2,1)S(1)}, u32[]{:S(2)}, u32[]{:S(2)}) collective-permute-start(bf16[512,128]{1,0:T(8,128)(2,1)S(1)} %get-tuple-element.40.refs_0_), channel_id=1, source_target_pairs={{0,8},{2,10},{4,12},{6,14},{8,0},{10,2},{12,4},{14,6},{1,9},{3,11}... | collective-permute-start | bytes 393224 | tf_op jit(solution)/shard_map/ppermute | solution.py:31
  12.0 3.1 %collective-permute-done.2.refs_2_ = bf16[512,128]{1,0:T(8,128)(2,1)S(1)} collective-permute-done((bf16[512,128]{1,0:T(8,128)(2,1)S(1)}, bf16[512,128]{1,0:T(8,128)(2,1)S(1)}, u32[]{:S(2)}, u32[]{:S(2)}) %collective-permute-start.2) | collective-permute-done | bytes 131104 | tf_op jit(solution)/shard_map/ppermute | solution.py:31
  15.1 0.2 collective-permute-start.4
  15.3 2.8 %collective-permute-done.1.refs_4_ = bf16[512,128]{1,0:T(8,128)(2,1)S(1)} collective-permute-done((bf16[512,128]{1,0:T(8,128)(2,1)S(1)}, bf16[512,128]{1,0:T(8,128)(2,1)S(1)}, u32[]{:S(2)}, u32[]{:S(2)}) %collective-permute-start.1) | collective-permute-done | bytes 131104 | tf_op jit(solution)/shard_map/ppermute | solution.py:31
  18.1 1.9 %collective-permute-done.4.refs_3_ = bf16[512,128]{1,0:T(8,128)(2,1)S(1)} collective-permute-done((bf16[512,128]{1,0:T(8,128)(2,1)S(1)}, bf16[512,128]{1,0:T(8,128)(2,1)S(1)}, u32[]{:S(2)}, u32[]{:S(2)}) %collective-permute-start.4) | collective-permute-done | bytes 131104 | tf_op jit(solution)/shard_map/ppermute | solution.py:31
  20.0 1.7 %collective-permute-start.7 = (bf16[512,128]{1,0:T(8,128)(2,1)S(1)}, bf16[512,128]{1,0:T(8,128)(2,1)S(1)}, u32[]{:S(2)}, u32[]{:S(2)}) collective-permute-start(bf16[512,128]{1,0:T(8,128)(2,1)S(1)} %collective-permute-done.1.refs_4_), channel_id=1, source_target_pairs={{0,4},{2,6},{4,0},{6,2},{8,12},{10,14},{12,8},{14,10},{1,5},{3,7},... | collective-permute-start | bytes 393224 | tf_op jit(solution)/shard_map/ppermute | solution.py:31
  21.7 1.8 %collective-permute-start.6 = (bf16[512,128]{1,0:T(8,128)(2,1)S(1)}, bf16[512,128]{1,0:T(8,128)(2,1)S(1)}, u32[]{:S(2)}, u32[]{:S(2)}) collective-permute-start(bf16[512,128]{1,0:T(8,128)(2,1)S(1)} %collective-permute-done.1.refs_4_), channel_id=1, source_target_pairs={{0,2},{2,0},{4,6},{6,4},{8,10},{10,8},{12,14},{14,12},{1,3},{3,1},... | collective-permute-start | bytes 393224 | tf_op jit(solution)/shard_map/ppermute | solution.py:31
  23.5 3.7 %collective-permute-done.8.refs_7_ = bf16[512,128]{1,0:T(8,128)(2,1)S(1)} collective-permute-done((bf16[512,128]{1,0:T(8,128)(2,1)S(1)}, bf16[512,128]{1,0:T(8,128)(2,1)S(1)}, u32[]{:S(2)}, u32[]{:S(2)}) %collective-permute-start.8) | collective-permute-done | bytes 131104 | tf_op jit(solution)/shard_map/ppermute | solution.py:31
  27.3 1.1 %collective-permute-done.7.refs_6_ = bf16[512,128]{1,0:T(8,128)(2,1)S(1)} collective-permute-done((bf16[512,128]{1,0:T(8,128)(2,1)S(1)}, bf16[512,128]{1,0:T(8,128)(2,1)S(1)}, u32[]{:S(2)}, u32[]{:S(2)}) %collective-permute-start.7) | collective-permute-done | bytes 131104 | tf_op jit(solution)/shard_map/ppermute | solution.py:31
  28.4 1.3 %collective-permute-done.6.refs_5_ = bf16[512,128]{1,0:T(8,128)(2,1)S(1)} collective-permute-done((bf16[512,128]{1,0:T(8,128)(2,1)S(1)}, bf16[512,128]{1,0:T(8,128)(2,1)S(1)}, u32[]{:S(2)}, u32[]{:S(2)}) %collective-permute-start.6) | collective-permute-done | bytes 131104 | tf_op jit(solution)/shard_map/ppermute | solution.py:31
  29.7 1.3 %shard_map.57 = (f32[512,128]{1,0:T(8,128)S(1)}, bf16[512,128]{1,0:T(8,128)(2,1)S(1)}) custom-call(bf16[4,512,512]{2,1,0:T(8,128)(2,1)S(1)} %get-tuple-element.38.own_ref, bf16[4,512,512]{2,1,0:T(8,128)(2,1)S(1)} %collective-permute-done.5.other_ref, f32[512,128]{1,0:T(8,128)S(1)} %get-tuple-element.39.scale_ref, ...), custom_call_target="tpu_custom_call" | custom-call | tf_op jit(solution)/shard_map/pallas_call | solution.py:195
  31.0 0.7 %collective-permute-start.11 = (bf16[512,128]{1,0:T(8,128)(2,1)S(1)}, bf16[512,128]{1,0:T(8,128)(2,1)S(1)}, u32[]{:S(2)}, u32[]{:S(2)}) collective-permute-start(bf16[512,128]{1,0:T(8,128)(2,1)S(1)} %get-tuple-element.50.refs_0_), channel_id=1, source_target_pairs={{0,2},{2,0},{4,6},{6,4},{8,10},{10,8},{12,14},{14,12},{1,3},{3,1},... | collective-permute-start | bytes 393224 | tf_op jit(solution)/shard_map/ppermute | solution.py:31
  31.7 0.2 collective-permute-start.10
  31.9 3.5 %collective-permute-start.9 = (bf16[512,128]{1,0:T(8,128)(2,1)S(1)}, bf16[512,128]{1,0:T(8,128)(2,1)S(1)}, u32[]{:S(2)}, u32[]{:S(2)}) collective-permute-start(bf16[512,128]{1,0:T(8,128)(2,1)S(1)} %get-tuple-element.50.refs_0_), channel_id=1, source_target_pairs={{0,8},{2,10},{4,12},{6,14},{8,0},{10,2},{12,4},{14,6},{1,9},{3,11}... | collective-permute-start | bytes 393224 | tf_op jit(solution)/shard_map/ppermute | solution.py:31
  35.4 1.1 %collective-permute-done.11.refs_1_ = bf16[512,128]{1,0:T(8,128)(2,1)S(1)} collective-permute-done((bf16[512,128]{1,0:T(8,128)(2,1)S(1)}, bf16[512,128]{1,0:T(8,128)(2,1)S(1)}, u32[]{:S(2)}, u32[]{:S(2)}) %collective-permute-start.11) | collective-permute-done | bytes 131104 | tf_op jit(solution)/shard_map/ppermute | solution.py:31
  36.5 2.5 %collective-permute-done.10.refs_2_ = bf16[512,128]{1,0:T(8,128)(2,1)S(1)} collective-permute-done((bf16[512,128]{1,0:T(8,128)(2,1)S(1)}, bf16[512,128]{1,0:T(8,128)(2,1)S(1)}, u32[]{:S(2)}, u32[]{:S(2)}) %collective-permute-start.10) | collective-permute-done | bytes 131104 | tf_op jit(solution)/shard_map/ppermute | solution.py:31
  39.0 1.8 %collective-permute-start.12 = (bf16[512,128]{1,0:T(8,128)(2,1)S(1)}, bf16[512,128]{1,0:T(8,128)(2,1)S(1)}, u32[]{:S(2)}, u32[]{:S(2)}) collective-permute-start(bf16[512,128]{1,0:T(8,128)(2,1)S(1)} %collective-permute-done.10.refs_2_), channel_id=1, source_target_pairs={{0,2},{2,0},{4,6},{6,4},{8,10},{10,8},{12,14},{14,12},{1,3},{3,1},... | collective-permute-start | bytes 393224 | tf_op jit(solution)/shard_map/ppermute | solution.py:31
  40.8 0.4 collective-permute-done.9.refs_4_
  41.2 4.7 %collective-permute-done.12.refs_3_ = bf16[512,128]{1,0:T(8,128)(2,1)S(1)} collective-permute-done((bf16[512,128]{1,0:T(8,128)(2,1)S(1)}, bf16[512,128]{1,0:T(8,128)(2,1)S(1)}, u32[]{:S(2)}, u32[]{:S(2)}) %collective-permute-start.12) | collective-permute-done | bytes 131104 | tf_op jit(solution)/shard_map/ppermute | solution.py:31
  45.9 3.7 %collective-permute-start.14 = (bf16[512,128]{1,0:T(8,128)(2,1)S(1)}, bf16[512,128]{1,0:T(8,128)(2,1)S(1)}, u32[]{:S(2)}, u32[]{:S(2)}) collective-permute-start(bf16[512,128]{1,0:T(8,128)(2,1)S(1)} %collective-permute-done.9.refs_4_), channel_id=1, source_target_pairs={{0,4},{2,6},{4,0},{6,2},{8,12},{10,14},{12,8},{14,10},{1,5},{3,7},... | collective-permute-start | bytes 393224 | tf_op jit(solution)/shard_map/ppermute | solution.py:31
  49.6 2.1 %collective-permute-done.15.refs_7_ = bf16[512,128]{1,0:T(8,128)(2,1)S(1)} collective-permute-done((bf16[512,128]{1,0:T(8,128)(2,1)S(1)}, bf16[512,128]{1,0:T(8,128)(2,1)S(1)}, u32[]{:S(2)}, u32[]{:S(2)}) %collective-permute-start.15) | collective-permute-done | bytes 131104 | tf_op jit(solution)/shard_map/ppermute | solution.py:31
  51.8 2.2 %collective-permute-done.14.refs_6_ = bf16[512,128]{1,0:T(8,128)(2,1)S(1)} collective-permute-done((bf16[512,128]{1,0:T(8,128)(2,1)S(1)}, bf16[512,128]{1,0:T(8,128)(2,1)S(1)}, u32[]{:S(2)}, u32[]{:S(2)}) %collective-permute-start.14) | collective-permute-done | bytes 131104 | tf_op jit(solution)/shard_map/ppermute | solution.py:31
  54.0 0.6 %collective-permute-done.13.refs_5_ = bf16[512,128]{1,0:T(8,128)(2,1)S(1)} collective-permute-done((bf16[512,128]{1,0:T(8,128)(2,1)S(1)}, bf16[512,128]{1,0:T(8,128)(2,1)S(1)}, u32[]{:S(2)}, u32[]{:S(2)}) %collective-permute-start.13) | collective-permute-done | bytes 131104 | tf_op jit(solution)/shard_map/ppermute | solution.py:31
  54.6 1.3 %shard_map.58 = (bf16[256,128]{1,0:T(8,128)(2,1)S(1)}, bf16[256,128]{1,0:T(8,128)(2,1)S(1)}) custom-call(bf16[4,512,512]{2,1,0:T(8,128)(2,1)S(1)} %get-tuple-element.38.own_ref, bf16[4,512,512]{2,1,0:T(8,128)(2,1)S(1)} %collective-permute-done.5.other_ref, f32[512,128]{1,0:T(8,128)S(1)} %get-tuple-element.39.scale_ref, ...), custom_call_target="tpu_custom_call" | custom-call | tf_op jit(solution)/shard_map/pallas_call | solution.py:205
  55.9 0.1 collective-permute-start.16
  56.0 1.2 %collective-permute-done.16.got_ref = bf16[256,128]{1,0:T(8,128)(2,1)S(1)} collective-permute-done((bf16[256,128]{1,0:T(8,128)(2,1)S(1)}, bf16[256,128]{1,0:T(8,128)(2,1)S(1)}, u32[]{:S(2)}, u32[]{:S(2)}) %collective-permute-start.16) | collective-permute-done | bytes 65568 | tf_op jit(solution)/shard_map/ppermute | solution.py:47
  57.3 0.9 %shard_map.59 = bf16[256,256]{1,0:T(8,128)(2,1)} custom-call(bf16[256,128]{1,0:T(8,128)(2,1)S(1)} %get-tuple-element.55.keep_ref, bf16[256,128]{1,0:T(8,128)(2,1)S(1)} %collective-permute-done.16.got_ref, bf16[256,256]{1,0:T(8,128)(2,1)S(1)} %copy-done.1), custom_call_target="tpu_custom_call" | custom-call | tf_op jit(solution)/shard_map/pallas_call | solution.py:214
  (11 shorter events, 0.1 us)
Async XLA Ops:
  0.0 4.8 %copy-start = (bf16[512,256]{1,0:T(8,128)(2,1)S(1)}, bf16[512,256]{1,0:T(8,128)(2,1)}, u32[]{:S(2)}) copy-start(bf16[512,256]{1,0:T(8,128)(2,1)} %feature_ref.3) | copy-start | bytes 786436
  3.1 1.7 %collective-permute-start = (f32[512,128]{1,0:T(8,128)S(1)}, f32[512,128]{1,0:T(8,128)S(1)}, u32[]{:S(2)}, u32[]{:S(2)}) collective-permute-start(f32[512,128]{1,0:T(8,128)S(1)} %get-tuple-element.32.degree_ref), channel_id=1, source_target_pairs={{0,1},{1,0},{2,3},{3,2},{4,5},{5,4},{6,7},{7,6},{8,9},{9,8},{10,11... | collective-permute-start | bytes 786440 | tf_op jit(solution)/shard_map/ppermute | solution.py:47
  4.8 7.1 %collective-permute-start.3 = (bf16[512,128]{1,0:T(8,128)(2,1)S(1)}, bf16[512,128]{1,0:T(8,128)(2,1)S(1)}, u32[]{:S(2)}, u32[]{:S(2)}) collective-permute-start(bf16[512,128]{1,0:T(8,128)(2,1)S(1)} %get-tuple-element.40.refs_0_), channel_id=1, source_target_pairs={{0,2},{2,0},{4,6},{6,4},{8,10},{10,8},{12,14},{14,12},{1,3},{3,1},... | collective-permute-start | bytes 393224 | tf_op jit(solution)/shard_map/ppermute | solution.py:31
  7.8 7.3 %collective-permute-start.2 = (bf16[512,128]{1,0:T(8,128)(2,1)S(1)}, bf16[512,128]{1,0:T(8,128)(2,1)S(1)}, u32[]{:S(2)}, u32[]{:S(2)}) collective-permute-start(bf16[512,128]{1,0:T(8,128)(2,1)S(1)} %get-tuple-element.40.refs_0_), channel_id=1, source_target_pairs={{0,4},{2,6},{4,0},{6,2},{8,12},{10,14},{12,8},{14,10},{1,5},{3,7},... | collective-permute-start | bytes 393224 | tf_op jit(solution)/shard_map/ppermute | solution.py:31
  9.4 8.7 %collective-permute-start.1 = (bf16[512,128]{1,0:T(8,128)(2,1)S(1)}, bf16[512,128]{1,0:T(8,128)(2,1)S(1)}, u32[]{:S(2)}, u32[]{:S(2)}) collective-permute-start(bf16[512,128]{1,0:T(8,128)(2,1)S(1)} %get-tuple-element.40.refs_0_), channel_id=1, source_target_pairs={{0,8},{2,10},{4,12},{6,14},{8,0},{10,2},{12,4},{14,6},{1,9},{3,11}... | collective-permute-start | bytes 393224 | tf_op jit(solution)/shard_map/ppermute | solution.py:31
  15.1 5.0 %collective-permute-start.4 = (bf16[512,128]{1,0:T(8,128)(2,1)S(1)}, bf16[512,128]{1,0:T(8,128)(2,1)S(1)}, u32[]{:S(2)}, u32[]{:S(2)}) collective-permute-start(bf16[512,128]{1,0:T(8,128)(2,1)S(1)} %collective-permute-done.2.refs_2_), channel_id=1, source_target_pairs={{0,2},{2,0},{4,6},{6,4},{8,10},{10,8},{12,14},{14,12},{1,3},{3,1},... | collective-permute-start | bytes 393224 | tf_op jit(solution)/shard_map/ppermute | solution.py:31
  20.0 9.6 %collective-permute-start.5 = (bf16[4,512,512]{2,1,0:T(8,128)(2,1)S(1)}, bf16[4,512,512]{2,1,0:T(8,128)(2,1)S(1)}, u32[]{:S(2)}, u32[]{:S(2)}) collective-permute-start(bf16[4,512,512]{2,1,0:T(8,128)(2,1)S(1)} %get-tuple-element.38.own_ref), channel_id=1, source_target_pairs={{0,1},{1,0},{2,3},{3,2},{4,5},{5,4},{6,7},{7,6},{8,9},{9,8},{10,11... | collective-permute-start | bytes 6291464 | tf_op jit(solution)/shard_map/ppermute | solution.py:47
  20.0 7.2 %collective-permute-start.8 = (bf16[512,128]{1,0:T(8,128)(2,1)S(1)}, bf16[512,128]{1,0:T(8,128)(2,1)S(1)}, u32[]{:S(2)}, u32[]{:S(2)}) collective-permute-start(bf16[512,128]{1,0:T(8,128)(2,1)S(1)} %collective-permute-done.1.refs_4_), channel_id=1, source_target_pairs={{0,6},{2,4},{4,2},{6,0},{8,14},{10,12},{12,10},{14,8},{1,7},{3,5},... | collective-permute-start | bytes 393224 | tf_op jit(solution)/shard_map/ppermute | solution.py:31
  20.0 8.4 %collective-permute-start.7 = (bf16[512,128]{1,0:T(8,128)(2,1)S(1)}, bf16[512,128]{1,0:T(8,128)(2,1)S(1)}, u32[]{:S(2)}, u32[]{:S(2)}) collective-permute-start(bf16[512,128]{1,0:T(8,128)(2,1)S(1)} %collective-permute-done.1.refs_4_), channel_id=1, source_target_pairs={{0,4},{2,6},{4,0},{6,2},{8,12},{10,14},{12,8},{14,10},{1,5},{3,7},... | collective-permute-start | bytes 393224 | tf_op jit(solution)/shard_map/ppermute | solution.py:31
  21.7 7.9 %collective-permute-start.6 = (bf16[512,128]{1,0:T(8,128)(2,1)S(1)}, bf16[512,128]{1,0:T(8,128)(2,1)S(1)}, u32[]{:S(2)}, u32[]{:S(2)}) collective-permute-start(bf16[512,128]{1,0:T(8,128)(2,1)S(1)} %collective-permute-done.1.refs_4_), channel_id=1, source_target_pairs={{0,2},{2,0},{4,6},{6,4},{8,10},{10,8},{12,14},{14,12},{1,3},{3,1},... | collective-permute-start | bytes 393224 | tf_op jit(solution)/shard_map/ppermute | solution.py:31
  31.0 5.5 %collective-permute-start.11 = (bf16[512,128]{1,0:T(8,128)(2,1)S(1)}, bf16[512,128]{1,0:T(8,128)(2,1)S(1)}, u32[]{:S(2)}, u32[]{:S(2)}) collective-permute-start(bf16[512,128]{1,0:T(8,128)(2,1)S(1)} %get-tuple-element.50.refs_0_), channel_id=1, source_target_pairs={{0,2},{2,0},{4,6},{6,4},{8,10},{10,8},{12,14},{14,12},{1,3},{3,1},... | collective-permute-start | bytes 393224 | tf_op jit(solution)/shard_map/ppermute | solution.py:31
  31.7 7.3 %collective-permute-start.10 = (bf16[512,128]{1,0:T(8,128)(2,1)S(1)}, bf16[512,128]{1,0:T(8,128)(2,1)S(1)}, u32[]{:S(2)}, u32[]{:S(2)}) collective-permute-start(bf16[512,128]{1,0:T(8,128)(2,1)S(1)} %get-tuple-element.50.refs_0_), channel_id=1, source_target_pairs={{0,4},{2,6},{4,0},{6,2},{8,12},{10,14},{12,8},{14,10},{1,5},{3,7},... | collective-permute-start | bytes 393224 | tf_op jit(solution)/shard_map/ppermute | solution.py:31
  31.9 9.3 %collective-permute-start.9 = (bf16[512,128]{1,0:T(8,128)(2,1)S(1)}, bf16[512,128]{1,0:T(8,128)(2,1)S(1)}, u32[]{:S(2)}, u32[]{:S(2)}) collective-permute-start(bf16[512,128]{1,0:T(8,128)(2,1)S(1)} %get-tuple-element.50.refs_0_), channel_id=1, source_target_pairs={{0,8},{2,10},{4,12},{6,14},{8,0},{10,2},{12,4},{14,6},{1,9},{3,11}... | collective-permute-start | bytes 393224 | tf_op jit(solution)/shard_map/ppermute | solution.py:31
  39.0 6.9 %collective-permute-start.12 = (bf16[512,128]{1,0:T(8,128)(2,1)S(1)}, bf16[512,128]{1,0:T(8,128)(2,1)S(1)}, u32[]{:S(2)}, u32[]{:S(2)}) collective-permute-start(bf16[512,128]{1,0:T(8,128)(2,1)S(1)} %collective-permute-done.10.refs_2_), channel_id=1, source_target_pairs={{0,2},{2,0},{4,6},{6,4},{8,10},{10,8},{12,14},{14,12},{1,3},{3,1},... | collective-permute-start | bytes 393224 | tf_op jit(solution)/shard_map/ppermute | solution.py:31
  45.9 5.9 %collective-permute-start.15 = (bf16[512,128]{1,0:T(8,128)(2,1)S(1)}, bf16[512,128]{1,0:T(8,128)(2,1)S(1)}, u32[]{:S(2)}, u32[]{:S(2)}) collective-permute-start(bf16[512,128]{1,0:T(8,128)(2,1)S(1)} %collective-permute-done.9.refs_4_), channel_id=1, source_target_pairs={{0,6},{2,4},{4,2},{6,0},{8,14},{10,12},{12,10},{14,8},{1,7},{3,5},... | collective-permute-start | bytes 393224 | tf_op jit(solution)/shard_map/ppermute | solution.py:31
  45.9 8.1 %collective-permute-start.14 = (bf16[512,128]{1,0:T(8,128)(2,1)S(1)}, bf16[512,128]{1,0:T(8,128)(2,1)S(1)}, u32[]{:S(2)}, u32[]{:S(2)}) collective-permute-start(bf16[512,128]{1,0:T(8,128)(2,1)S(1)} %collective-permute-done.9.refs_4_), channel_id=1, source_target_pairs={{0,4},{2,6},{4,0},{6,2},{8,12},{10,14},{12,8},{14,10},{1,5},{3,7},... | collective-permute-start | bytes 393224 | tf_op jit(solution)/shard_map/ppermute | solution.py:31
  49.6 5.0 %collective-permute-start.13 = (bf16[512,128]{1,0:T(8,128)(2,1)S(1)}, bf16[512,128]{1,0:T(8,128)(2,1)S(1)}, u32[]{:S(2)}, u32[]{:S(2)}) collective-permute-start(bf16[512,128]{1,0:T(8,128)(2,1)S(1)} %collective-permute-done.9.refs_4_), channel_id=1, source_target_pairs={{0,2},{2,0},{4,6},{6,4},{8,10},{10,8},{12,14},{14,12},{1,3},{3,1},... | collective-permute-start | bytes 393224 | tf_op jit(solution)/shard_map/ppermute | solution.py:31
  54.6 2.7 %copy-start.1 = (bf16[256,256]{1,0:T(8,128)(2,1)S(1)}, bf16[256,256]{1,0:T(8,128)(2,1)}, u32[]{:S(2)}) copy-start(bf16[256,256]{1,0:T(8,128)(2,1)} %weight_ref.1) | copy-start | bytes 393220
  55.9 1.3 %collective-permute-start.16 = (bf16[256,128]{1,0:T(8,128)(2,1)S(1)}, bf16[256,128]{1,0:T(8,128)(2,1)S(1)}, u32[]{:S(2)}, u32[]{:S(2)}) collective-permute-start(bf16[256,128]{1,0:T(8,128)(2,1)S(1)} %get-tuple-element.56), channel_id=1, source_target_pairs={{0,1},{1,0},{2,3},{3,2},{4,5},{5,4},{6,7},{7,6},{8,9},{9,8},{10,11... | collective-permute-start | bytes 196616 | tf_op jit(solution)/shard_map/ppermute | solution.py:47

commit v3 on v2

--- a/solution.py
+++ b/solution.py
@@ -34,13 +34,11 @@
 def gathered(block, axis, size):
     if size == 1:
         return [block]
-    if size == 2:
-        return [block, xor_permute(block, axis, 1)]
     half = size // 2
-    near = gathered(block, axis, half)
     far = xor_permute(block, axis, half)
-    far, *near = lax.optimization_barrier((far, *near))
-    return near + [far] + [xor_permute(far, axis, d) for d in range(1, half)]
+    near = [xor_permute(block, axis, d) for d in range(half - 1, 0, -1)]
+    far_near = [xor_permute(far, axis, d) for d in range(half - 1, 0, -1)]
+    return [block, *near[::-1], far, *far_near[::-1]]
 
 
 def swapped(block, axis):
@@ -190,7 +188,7 @@
     )(degree, degree_other, features)
 
     blocks = gathered(first, "rows", row_total)
-    dense_late, blocks[1] = lax.optimization_barrier((dense, blocks[1]))
+    dense_late, _ = lax.optimization_barrier((dense, scale))
     dense_other = in_vmem(swapped(dense_late, "rep"))
     heat_one, second = pl.pallas_call(
         first_kernel,

time: 58.3 us -> 47.7 us (0.82)
  waiting for transfers between devices: 30.1 us -> 20.6 us
  starting transfers between devices: 21.3 us -> 20.3 us
    ppermute x14, waiting for transfers between devices: 27.7 us -> 18.2 us  [xor_permute(): lax.ppermute(block, axis, [(i, i ^ distance) for i in range(lax.axis_size...]
    ppermute x14, starting transfers between devices: 20.8 us -> 19.2 us  [xor_permute(): lax.ppermute(block, axis, [(i, i ^ distance) for i in range(lax.axis_size...]
  transfers between devices with their start and end apart: 17 -> 17, of which waited for: 15 -> 12; matrix products, arithmetic and copies ran while one was open for 0% -> 0% of each run, Pallas kernels for 0% -> 0%
where the time goes in v3:
time: 47.7 us; the launch traced here: 47.6 us
  waiting for transfers between devices  20.6 us (43%)
  starting transfers between devices  20.3 us (43%)
  Pallas kernels  6.66 us (14%)
    ppermute x14, starting transfers between devices, xor_permute(): lax.ppermute(block, axis, [(i, i ^ distance) for i in range(lax.axis_size...  19.2 us
    ppermute x14, waiting for transfers between devices, xor_permute(): lax.ppermute(block, axis, [(i, i ^ distance) for i in range(lax.axis_size...  18.2 us
    pallas_call x1, Pallas kernels, per_device(): pl.pallas_call(place_kernel, out_shape=(shape(*panels), shape(*column)),...  3.08 us
    ppermute x3, waiting for transfers between devices, swapped(): return lax.ppermute(block, axis, [(0, 1), (1, 0)])  2.41 us
    pallas_call x1, Pallas kernels, per_device(): pl.pallas_call(second_kernel, out_shape=(shape(*half), shape(*half)), in_...  1.35 us
    pallas_call x1, Pallas kernels, per_device(): pl.pallas_call(first_kernel, out_shape=(shape(*column), shape(*field)), i...  1.32 us
    ppermute x3, starting transfers between devices, swapped(): return lax.ppermute(block, axis, [(0, 1), (1, 0)])  1.02 us
  transfers between devices with their start and end apart: 17, of which 12 were waited for; matrix products, arithmetic and copies ran while one was open for 0% of the time, Pallas kernels for 0%

profile of v3, /device:TPU:0, one launch (start us, length us, event | category | flops | bytes accessed | tf_op | source)
XLA Modules:
  0.0 47.6 jit_solution(15477175170546800482)
XLA Ops:
  0.0 3.1 %shard_map.55 = (bf16[4,512,512]{2,1,0:T(8,128)(2,1)S(1)}, f32[512,128]{1,0:T(8,128)S(1)}) custom-call(s32[4,16]{1,0:T(4,128)} %place_hbm.1, s32[4]{0:T(128)} %count_hbm.1, bf16[64,128,128]{2,1,0:T(8,128)(2,1)} %tiles_ref.1), custom_call_target="tpu_custom_call" | custom-call | tf_op jit(solution)/shard_map/pallas_call | solution.py:168
  3.1 0.5 %collective-permute-start = (f32[512,128]{1,0:T(8,128)S(1)}, f32[512,128]{1,0:T(8,128)S(1)}, u32[]{:S(2)}, u32[]{:S(2)}) collective-permute-start(f32[512,128]{1,0:T(8,128)S(1)} %get-tuple-element.15.degree_ref), channel_id=1, source_target_pairs={{0,1},{1,0},{2,3},{3,2},{4,5},{5,4},{6,7},{7,6},{8,9},{9,8},{10,11... | collective-permute-start | bytes 786440 | tf_op jit(solution)/shard_map/ppermute | solution.py:45
  3.6 1.2 %collective-permute-done.other_ref = f32[512,128]{1,0:T(8,128)S(1)} collective-permute-done((f32[512,128]{1,0:T(8,128)S(1)}, f32[512,128]{1,0:T(8,128)S(1)}, u32[]{:S(2)}, u32[]{:S(2)}) %collective-permute-start) | collective-permute-done | bytes 262176 | tf_op jit(solution)/shard_map/ppermute | solution.py:45
  4.8 0.4 collective-permute-start.1
  5.3 3.7 %collective-permute-start.5 = (bf16[512,128]{1,0:T(8,128)(2,1)S(1)}, bf16[512,128]{1,0:T(8,128)(2,1)S(1)}, u32[]{:S(2)}, u32[]{:S(2)}) collective-permute-start(bf16[512,128]{1,0:T(8,128)(2,1)S(1)} %get-tuple-element.18.refs_0_), channel_id=1, source_target_pairs={{0,8},{2,10},{4,12},{6,14},{8,0},{10,2},{12,4},{14,6},{1,9},{3,11}... | collective-permute-start | bytes 393224 | tf_op jit(solution)/shard_map/ppermute | solution.py:31
  9.0 2.5 %collective-permute-start.4 = (bf16[512,128]{1,0:T(8,128)(2,1)S(1)}, bf16[512,128]{1,0:T(8,128)(2,1)S(1)}, u32[]{:S(2)}, u32[]{:S(2)}) collective-permute-start(bf16[512,128]{1,0:T(8,128)(2,1)S(1)} %get-tuple-element.18.refs_0_), channel_id=1, source_target_pairs={{0,6},{2,4},{4,2},{6,0},{8,14},{10,12},{12,10},{14,8},{1,7},{3,5},... | collective-permute-start | bytes 393224 | tf_op jit(solution)/shard_map/ppermute | solution.py:31
  11.5 0.4 collective-permute-start.3
  12.0 0.5 %collective-permute-start.2 = (bf16[512,128]{1,0:T(8,128)(2,1)S(1)}, bf16[512,128]{1,0:T(8,128)(2,1)S(1)}, u32[]{:S(2)}, u32[]{:S(2)}) collective-permute-start(bf16[512,128]{1,0:T(8,128)(2,1)S(1)} %get-tuple-element.18.refs_0_), channel_id=1, source_target_pairs={{0,2},{2,0},{4,6},{6,4},{8,10},{10,8},{12,14},{14,12},{1,3},{3,1},... | collective-permute-start | bytes 393224 | tf_op jit(solution)/shard_map/ppermute | solution.py:31
  12.5 3.4 %collective-permute-done.5.refs_4_ = bf16[512,128]{1,0:T(8,128)(2,1)S(1)} collective-permute-done((bf16[512,128]{1,0:T(8,128)(2,1)S(1)}, bf16[512,128]{1,0:T(8,128)(2,1)S(1)}, u32[]{:S(2)}, u32[]{:S(2)}) %collective-permute-start.5) | collective-permute-done | bytes 131104 | tf_op jit(solution)/shard_map/ppermute | solution.py:31
  15.9 1.6 %collective-permute-start.8 = (bf16[512,128]{1,0:T(8,128)(2,1)S(1)}, bf16[512,128]{1,0:T(8,128)(2,1)S(1)}, u32[]{:S(2)}, u32[]{:S(2)}) collective-permute-start(bf16[512,128]{1,0:T(8,128)(2,1)S(1)} %collective-permute-done.5.refs_4_), channel_id=1, source_target_pairs={{0,6},{2,4},{4,2},{6,0},{8,14},{10,12},{12,10},{14,8},{1,7},{3,5},... | collective-permute-start | bytes 393224 | tf_op jit(solution)/shard_map/ppermute | solution.py:31
  17.6 0.4 collective-permute-done.4.refs_3_
  18.0 1.2 %collective-permute-start.7 = (bf16[512,128]{1,0:T(8,128)(2,1)S(1)}, bf16[512,128]{1,0:T(8,128)(2,1)S(1)}, u32[]{:S(2)}, u32[]{:S(2)}) collective-permute-start(bf16[512,128]{1,0:T(8,128)(2,1)S(1)} %collective-permute-done.5.refs_4_), channel_id=1, source_target_pairs={{0,4},{2,6},{4,0},{6,2},{8,12},{10,14},{12,8},{14,10},{1,5},{3,7},... | collective-permute-start | bytes 393224 | tf_op jit(solution)/shard_map/ppermute | solution.py:31
  19.2 1.6 %collective-permute-done.3.refs_2_ = bf16[512,128]{1,0:T(8,128)(2,1)S(1)} collective-permute-done((bf16[512,128]{1,0:T(8,128)(2,1)S(1)}, bf16[512,128]{1,0:T(8,128)(2,1)S(1)}, u32[]{:S(2)}, u32[]{:S(2)}) %collective-permute-start.3) | collective-permute-done | bytes 131104 | tf_op jit(solution)/shard_map/ppermute | solution.py:31
  20.8 0.4 collective-permute-start.6
  21.2 2.2 %collective-permute-done.8.refs_7_ = bf16[512,128]{1,0:T(8,128)(2,1)S(1)} collective-permute-done((bf16[512,128]{1,0:T(8,128)(2,1)S(1)}, bf16[512,128]{1,0:T(8,128)(2,1)S(1)}, u32[]{:S(2)}, u32[]{:S(2)}) %collective-permute-start.8) | collective-permute-done | bytes 131104 | tf_op jit(solution)/shard_map/ppermute | solution.py:31
  23.4 2.1 %collective-permute-done.7.refs_6_ = bf16[512,128]{1,0:T(8,128)(2,1)S(1)} collective-permute-done((bf16[512,128]{1,0:T(8,128)(2,1)S(1)}, bf16[512,128]{1,0:T(8,128)(2,1)S(1)}, u32[]{:S(2)}, u32[]{:S(2)}) %collective-permute-start.7) | collective-permute-done | bytes 131104 | tf_op jit(solution)/shard_map/ppermute | solution.py:31
  25.5 0.2 collective-permute-done.6.refs_5_
  25.7 1.3 %shard_map.57 = (f32[512,128]{1,0:T(8,128)S(1)}, bf16[512,128]{1,0:T(8,128)(2,1)S(1)}) custom-call(bf16[4,512,512]{2,1,0:T(8,128)(2,1)S(1)} %get-tuple-element.17.own_ref, bf16[4,512,512]{2,1,0:T(8,128)(2,1)S(1)} %collective-permute-done.1.other_ref, f32[512,128]{1,0:T(8,128)S(1)} %get-tuple-element.16.scale_ref, ...), custom_call_target="tpu_custom_call" | custom-call | tf_op jit(solution)/shard_map/pallas_call | solution.py:193
  27.1 1.8 %collective-permute-start.12 = (bf16[512,128]{1,0:T(8,128)(2,1)S(1)}, bf16[512,128]{1,0:T(8,128)(2,1)S(1)}, u32[]{:S(2)}, u32[]{:S(2)}) collective-permute-start(bf16[512,128]{1,0:T(8,128)(2,1)S(1)} %get-tuple-element.20.refs_0_), channel_id=1, source_target_pairs={{0,8},{2,10},{4,12},{6,14},{8,0},{10,2},{12,4},{14,6},{1,9},{3,11}... | collective-permute-start | bytes 393224 | tf_op jit(solution)/shard_map/ppermute | solution.py:31
  28.9 2.6 %collective-permute-start.11 = (bf16[512,128]{1,0:T(8,128)(2,1)S(1)}, bf16[512,128]{1,0:T(8,128)(2,1)S(1)}, u32[]{:S(2)}, u32[]{:S(2)}) collective-permute-start(bf16[512,128]{1,0:T(8,128)(2,1)S(1)} %get-tuple-element.20.refs_0_), channel_id=1, source_target_pairs={{0,6},{2,4},{4,2},{6,0},{8,14},{10,12},{12,10},{14,8},{1,7},{3,5},... | collective-permute-start | bytes 393224 | tf_op jit(solution)/shard_map/ppermute | solution.py:31
  31.5 0.8 %collective-permute-start.9 = (bf16[512,128]{1,0:T(8,128)(2,1)S(1)}, bf16[512,128]{1,0:T(8,128)(2,1)S(1)}, u32[]{:S(2)}, u32[]{:S(2)}) collective-permute-start(bf16[512,128]{1,0:T(8,128)(2,1)S(1)} %get-tuple-element.20.refs_0_), channel_id=1, source_target_pairs={{0,2},{2,0},{4,6},{6,4},{8,10},{10,8},{12,14},{14,12},{1,3},{3,1},... | collective-permute-start | bytes 393224 | tf_op jit(solution)/shard_map/ppermute | solution.py:31
  32.3 3.2 %collective-permute-done.12.refs_4_ = bf16[512,128]{1,0:T(8,128)(2,1)S(1)} collective-permute-done((bf16[512,128]{1,0:T(8,128)(2,1)S(1)}, bf16[512,128]{1,0:T(8,128)(2,1)S(1)}, u32[]{:S(2)}, u32[]{:S(2)}) %collective-permute-start.12) | collective-permute-done | bytes 131104 | tf_op jit(solution)/shard_map/ppermute | solution.py:31
  35.5 0.3 collective-permute-start.15
  35.8 2.5 %collective-permute-start.14 = (bf16[512,128]{1,0:T(8,128)(2,1)S(1)}, bf16[512,128]{1,0:T(8,128)(2,1)S(1)}, u32[]{:S(2)}, u32[]{:S(2)}) collective-permute-start(bf16[512,128]{1,0:T(8,128)(2,1)S(1)} %collective-permute-done.12.refs_4_), channel_id=1, source_target_pairs={{0,4},{2,6},{4,0},{6,2},{8,12},{10,14},{12,8},{14,10},{1,5},{3,7},... | collective-permute-start | bytes 393224 | tf_op jit(solution)/shard_map/ppermute | solution.py:31
  38.4 0.6 %collective-permute-start.13 = (bf16[512,128]{1,0:T(8,128)(2,1)S(1)}, bf16[512,128]{1,0:T(8,128)(2,1)S(1)}, u32[]{:S(2)}, u32[]{:S(2)}) collective-permute-start(bf16[512,128]{1,0:T(8,128)(2,1)S(1)} %collective-permute-done.12.refs_4_), channel_id=1, source_target_pairs={{0,2},{2,0},{4,6},{6,4},{8,10},{10,8},{12,14},{14,12},{1,3},{3,1},... | collective-permute-start | bytes 393224 | tf_op jit(solution)/shard_map/ppermute | solution.py:31
  39.0 4.3 %collective-permute-done.15.refs_7_ = bf16[512,128]{1,0:T(8,128)(2,1)S(1)} collective-permute-done((bf16[512,128]{1,0:T(8,128)(2,1)S(1)}, bf16[512,128]{1,0:T(8,128)(2,1)S(1)}, u32[]{:S(2)}, u32[]{:S(2)}) %collective-permute-start.15) | collective-permute-done | bytes 131104 | tf_op jit(solution)/shard_map/ppermute | solution.py:31
  43.3 0.4 collective-permute-done.14.refs_6_
  43.7 0.4 collective-permute-done.13.refs_5_
  44.0 1.3 %shard_map.58 = (bf16[256,128]{1,0:T(8,128)(2,1)S(1)}, bf16[256,128]{1,0:T(8,128)(2,1)S(1)}) custom-call(bf16[4,512,512]{2,1,0:T(8,128)(2,1)S(1)} %get-tuple-element.17.own_ref, bf16[4,512,512]{2,1,0:T(8,128)(2,1)S(1)} %collective-permute-done.1.other_ref, f32[512,128]{1,0:T(8,128)S(1)} %get-tuple-element.16.scale_ref, ...), custom_call_target="tpu_custom_call" | custom-call | tf_op jit(solution)/shard_map/pallas_call | solution.py:203
  45.4 0.1 collective-permute-start.16
  45.5 1.2 %collective-permute-done.16.got_ref = bf16[256,128]{1,0:T(8,128)(2,1)S(1)} collective-permute-done((bf16[256,128]{1,0:T(8,128)(2,1)S(1)}, bf16[256,128]{1,0:T(8,128)(2,1)S(1)}, u32[]{:S(2)}, u32[]{:S(2)}) %collective-permute-start.16) | collective-permute-done | bytes 65568 | tf_op jit(solution)/shard_map/ppermute | solution.py:45
  46.7 0.9 %shard_map.59 = bf16[256,256]{1,0:T(8,128)(2,1)} custom-call(bf16[256,128]{1,0:T(8,128)(2,1)S(1)} %get-tuple-element.21.keep_ref, bf16[256,128]{1,0:T(8,128)(2,1)S(1)} %collective-permute-done.16.got_ref, bf16[256,256]{1,0:T(8,128)(2,1)S(1)} %copy-done.1), custom_call_target="tpu_custom_call" | custom-call | tf_op jit(solution)/shard_map/pallas_call | solution.py:212
  (11 shorter events, 0.1 us)
Async XLA Ops:
  0.0 4.8 %copy-start = (bf16[512,256]{1,0:T(8,128)(2,1)S(1)}, bf16[512,256]{1,0:T(8,128)(2,1)}, u32[]{:S(2)}) copy-start(bf16[512,256]{1,0:T(8,128)(2,1)} %feature_ref.3) | copy-start | bytes 786436
  3.1 1.7 %collective-permute-start = (f32[512,128]{1,0:T(8,128)S(1)}, f32[512,128]{1,0:T(8,128)S(1)}, u32[]{:S(2)}, u32[]{:S(2)}) collective-permute-start(f32[512,128]{1,0:T(8,128)S(1)} %get-tuple-element.15.degree_ref), channel_id=1, source_target_pairs={{0,1},{1,0},{2,3},{3,2},{4,5},{5,4},{6,7},{7,6},{8,9},{9,8},{10,11... | collective-permute-start | bytes 786440 | tf_op jit(solution)/shard_map/ppermute | solution.py:45
  4.8 20.9 %collective-permute-start.1 = (bf16[4,512,512]{2,1,0:T(8,128)(2,1)S(1)}, bf16[4,512,512]{2,1,0:T(8,128)(2,1)S(1)}, u32[]{:S(2)}, u32[]{:S(2)}) collective-permute-start(bf16[4,512,512]{2,1,0:T(8,128)(2,1)S(1)} %get-tuple-element.17.own_ref), channel_id=1, source_target_pairs={{0,1},{1,0},{2,3},{3,2},{4,5},{5,4},{6,7},{7,6},{8,9},{9,8},{10,11... | collective-permute-start | bytes 6291464 | tf_op jit(solution)/shard_map/ppermute | solution.py:45
  5.3 10.7 %collective-permute-start.5 = (bf16[512,128]{1,0:T(8,128)(2,1)S(1)}, bf16[512,128]{1,0:T(8,128)(2,1)S(1)}, u32[]{:S(2)}, u32[]{:S(2)}) collective-permute-start(bf16[512,128]{1,0:T(8,128)(2,1)S(1)} %get-tuple-element.18.refs_0_), channel_id=1, source_target_pairs={{0,8},{2,10},{4,12},{6,14},{8,0},{10,2},{12,4},{14,6},{1,9},{3,11}... | collective-permute-start | bytes 393224 | tf_op jit(solution)/shard_map/ppermute | solution.py:31
  9.0 8.9 %collective-permute-start.4 = (bf16[512,128]{1,0:T(8,128)(2,1)S(1)}, bf16[512,128]{1,0:T(8,128)(2,1)S(1)}, u32[]{:S(2)}, u32[]{:S(2)}) collective-permute-start(bf16[512,128]{1,0:T(8,128)(2,1)S(1)} %get-tuple-element.18.refs_0_), channel_id=1, source_target_pairs={{0,6},{2,4},{4,2},{6,0},{8,14},{10,12},{12,10},{14,8},{1,7},{3,5},... | collective-permute-start | bytes 393224 | tf_op jit(solution)/shard_map/ppermute | solution.py:31
  11.5 9.2 %collective-permute-start.3 = (bf16[512,128]{1,0:T(8,128)(2,1)S(1)}, bf16[512,128]{1,0:T(8,128)(2,1)S(1)}, u32[]{:S(2)}, u32[]{:S(2)}) collective-permute-start(bf16[512,128]{1,0:T(8,128)(2,1)S(1)} %get-tuple-element.18.refs_0_), channel_id=1, source_target_pairs={{0,4},{2,6},{4,0},{6,2},{8,12},{10,14},{12,8},{14,10},{1,5},{3,7},... | collective-permute-start | bytes 393224 | tf_op jit(solution)/shard_map/ppermute | solution.py:31
  12.0 9.2 %collective-permute-start.2 = (bf16[512,128]{1,0:T(8,128)(2,1)S(1)}, bf16[512,128]{1,0:T(8,128)(2,1)S(1)}, u32[]{:S(2)}, u32[]{:S(2)}) collective-permute-start(bf16[512,128]{1,0:T(8,128)(2,1)S(1)} %get-tuple-element.18.refs_0_), channel_id=1, source_target_pairs={{0,2},{2,0},{4,6},{6,4},{8,10},{10,8},{12,14},{14,12},{1,3},{3,1},... | collective-permute-start | bytes 393224 | tf_op jit(solution)/shard_map/ppermute | solution.py:31
  15.9 7.5 %collective-permute-start.8 = (bf16[512,128]{1,0:T(8,128)(2,1)S(1)}, bf16[512,128]{1,0:T(8,128)(2,1)S(1)}, u32[]{:S(2)}, u32[]{:S(2)}) collective-permute-start(bf16[512,128]{1,0:T(8,128)(2,1)S(1)} %collective-permute-done.5.refs_4_), channel_id=1, source_target_pairs={{0,6},{2,4},{4,2},{6,0},{8,14},{10,12},{12,10},{14,8},{1,7},{3,5},... | collective-permute-start | bytes 393224 | tf_op jit(solution)/shard_map/ppermute | solution.py:31
  18.0 7.6 %collective-permute-start.7 = (bf16[512,128]{1,0:T(8,128)(2,1)S(1)}, bf16[512,128]{1,0:T(8,128)(2,1)S(1)}, u32[]{:S(2)}, u32[]{:S(2)}) collective-permute-start(bf16[512,128]{1,0:T(8,128)(2,1)S(1)} %collective-permute-done.5.refs_4_), channel_id=1, source_target_pairs={{0,4},{2,6},{4,0},{6,2},{8,12},{10,14},{12,8},{14,10},{1,5},{3,7},... | collective-permute-start | bytes 393224 | tf_op jit(solution)/shard_map/ppermute | solution.py:31
  20.8 5.0 %collective-permute-start.6 = (bf16[512,128]{1,0:T(8,128)(2,1)S(1)}, bf16[512,128]{1,0:T(8,128)(2,1)S(1)}, u32[]{:S(2)}, u32[]{:S(2)}) collective-permute-start(bf16[512,128]{1,0:T(8,128)(2,1)S(1)} %collective-permute-done.5.refs_4_), channel_id=1, source_target_pairs={{0,2},{2,0},{4,6},{6,4},{8,10},{10,8},{12,14},{14,12},{1,3},{3,1},... | collective-permute-start | bytes 393224 | tf_op jit(solution)/shard_map/ppermute | solution.py:31
  27.1 8.5 %collective-permute-start.12 = (bf16[512,128]{1,0:T(8,128)(2,1)S(1)}, bf16[512,128]{1,0:T(8,128)(2,1)S(1)}, u32[]{:S(2)}, u32[]{:S(2)}) collective-permute-start(bf16[512,128]{1,0:T(8,128)(2,1)S(1)} %get-tuple-element.20.refs_0_), channel_id=1, source_target_pairs={{0,8},{2,10},{4,12},{6,14},{8,0},{10,2},{12,4},{14,6},{1,9},{3,11}... | collective-permute-start | bytes 393224 | tf_op jit(solution)/shard_map/ppermute | solution.py:31
  28.9 9.5 %collective-permute-start.11 = (bf16[512,128]{1,0:T(8,128)(2,1)S(1)}, bf16[512,128]{1,0:T(8,128)(2,1)S(1)}, u32[]{:S(2)}, u32[]{:S(2)}) collective-permute-start(bf16[512,128]{1,0:T(8,128)(2,1)S(1)} %get-tuple-element.20.refs_0_), channel_id=1, source_target_pairs={{0,6},{2,4},{4,2},{6,0},{8,14},{10,12},{12,10},{14,8},{1,7},{3,5},... | collective-permute-start | bytes 393224 | tf_op jit(solution)/shard_map/ppermute | solution.py:31
  31.5 7.5 %collective-permute-start.10 = (bf16[512,128]{1,0:T(8,128)(2,1)S(1)}, bf16[512,128]{1,0:T(8,128)(2,1)S(1)}, u32[]{:S(2)}, u32[]{:S(2)}) collective-permute-start(bf16[512,128]{1,0:T(8,128)(2,1)S(1)} %get-tuple-element.20.refs_0_), channel_id=1, source_target_pairs={{0,4},{2,6},{4,0},{6,2},{8,12},{10,14},{12,8},{14,10},{1,5},{3,7},... | collective-permute-start | bytes 393224 | tf_op jit(solution)/shard_map/ppermute | solution.py:31
  31.5 7.5 %collective-permute-start.9 = (bf16[512,128]{1,0:T(8,128)(2,1)S(1)}, bf16[512,128]{1,0:T(8,128)(2,1)S(1)}, u32[]{:S(2)}, u32[]{:S(2)}) collective-permute-start(bf16[512,128]{1,0:T(8,128)(2,1)S(1)} %get-tuple-element.20.refs_0_), channel_id=1, source_target_pairs={{0,2},{2,0},{4,6},{6,4},{8,10},{10,8},{12,14},{14,12},{1,3},{3,1},... | collective-permute-start | bytes 393224 | tf_op jit(solution)/shard_map/ppermute | solution.py:31
  35.5 7.8 %collective-permute-start.15 = (bf16[512,128]{1,0:T(8,128)(2,1)S(1)}, bf16[512,128]{1,0:T(8,128)(2,1)S(1)}, u32[]{:S(2)}, u32[]{:S(2)}) collective-permute-start(bf16[512,128]{1,0:T(8,128)(2,1)S(1)} %collective-permute-done.12.refs_4_), channel_id=1, source_target_pairs={{0,6},{2,4},{4,2},{6,0},{8,14},{10,12},{12,10},{14,8},{1,7},{3,5},... | collective-permute-start | bytes 393224 | tf_op jit(solution)/shard_map/ppermute | solution.py:31
  35.8 7.8 %collective-permute-start.14 = (bf16[512,128]{1,0:T(8,128)(2,1)S(1)}, bf16[512,128]{1,0:T(8,128)(2,1)S(1)}, u32[]{:S(2)}, u32[]{:S(2)}) collective-permute-start(bf16[512,128]{1,0:T(8,128)(2,1)S(1)} %collective-permute-done.12.refs_4_), channel_id=1, source_target_pairs={{0,4},{2,6},{4,0},{6,2},{8,12},{10,14},{12,8},{14,10},{1,5},{3,7},... | collective-permute-start | bytes 393224 | tf_op jit(solution)/shard_map/ppermute | solution.py:31
  38.4 5.7 %collective-permute-start.13 = (bf16[512,128]{1,0:T(8,128)(2,1)S(1)}, bf16[512,128]{1,0:T(8,128)(2,1)S(1)}, u32[]{:S(2)}, u32[]{:S(2)}) collective-permute-start(bf16[512,128]{1,0:T(8,128)(2,1)S(1)} %collective-permute-done.12.refs_4_), channel_id=1, source_target_pairs={{0,2},{2,0},{4,6},{6,4},{8,10},{10,8},{12,14},{14,12},{1,3},{3,1},... | collective-permute-start | bytes 393224 | tf_op jit(solution)/shard_map/ppermute | solution.py:31
  44.0 2.7 %copy-start.1 = (bf16[256,256]{1,0:T(8,128)(2,1)S(1)}, bf16[256,256]{1,0:T(8,128)(2,1)}, u32[]{:S(2)}) copy-start(bf16[256,256]{1,0:T(8,128)(2,1)} %weight_ref.1) | copy-start | bytes 393220
  45.4 1.3 %collective-permute-start.16 = (bf16[256,128]{1,0:T(8,128)(2,1)S(1)}, bf16[256,128]{1,0:T(8,128)(2,1)S(1)}, u32[]{:S(2)}, u32[]{:S(2)}) collective-permute-start(bf16[256,128]{1,0:T(8,128)(2,1)S(1)} %get-tuple-element.22), channel_id=1, source_target_pairs={{0,1},{1,0},{2,3},{3,2},{4,5},{5,4},{6,7},{7,6},{8,9},{9,8},{10,11... | collective-permute-start | bytes 196616 | tf_op jit(solution)/shard_map/ppermute | solution.py:45

commit v4 on v3

--- a/solution.py
+++ b/solution.py
@@ -31,14 +31,17 @@
     return lax.ppermute(block, axis, [(i, i ^ distance) for i in range(lax.axis_size(axis))])
 
 
-def gathered(block, axis, size):
-    if size == 1:
-        return [block]
+def gathered(block, axis, size, also=None):
     half = size // 2
-    far = xor_permute(block, axis, half)
-    near = [xor_permute(block, axis, d) for d in range(half - 1, 0, -1)]
-    far_near = [xor_permute(far, axis, d) for d in range(half - 1, 0, -1)]
-    return [block, *near[::-1], far, *far_near[::-1]]
+    blocks = {0: block}
+    for d in [1, half, *range(2, half)]:
+        blocks[d] = xor_permute(block, axis, d)
+    early = [half, *range(1, half - 1)]
+    tied, also = lax.optimization_barrier(([blocks[d] for d in early], also))
+    blocks.update(zip(early, tied))
+    for d in range(half - 1, 0, -1):
+        blocks[half + d] = xor_permute(blocks[half], axis, d)
+    return [blocks[d] for d in range(size)], also
 
 
 def swapped(block, axis):
@@ -94,26 +97,47 @@
     first_ref[...] = (scale * feature.astype(F32)).astype(BF16)
 
 
-def image(own_ref, other_ref, block_refs, held, finish, chunk=256):
-    row_total = len(block_refs)
+def add_image(far, row_total, own_ref, other_ref, block_refs, held, start, finish, chunk=256):
     rep_total = row_total // own_ref.shape[0]
     row_index = lax.axis_index("rows")
     replica = lax.axis_index("rep")
-    for d, block_ref in enumerate(block_refs):
-        held[d] = block_ref[...]
-    for low in range(0, own_ref.shape[1], chunk):
-        rows = pl.ds(low, chunk)
-        total = held[0, rows].astype(F32)
-        for dense_ref, core in ((own_ref, replica), (other_ref, 1 - replica)):
-            for s in range(dense_ref.shape[0]):
-                column = lax.rem(row_index - core - rep_total * s + row_total, row_total)
+    for i, block_ref in enumerate(block_refs):
+        held[i] = block_ref[...]
+    for first_row in range(0, own_ref.shape[1], chunk):
+        rows = pl.ds(first_row, chunk)
+        total = start(rows)
+        for i in range(0, len(block_refs), rep_total):
+            for dense_ref, core in ((own_ref, replica), (other_ref, 1 - replica)):
+                column = row_index ^ (far[i] + core * (far[i + 1] - far[i]))
+                section = lax.rem(row_index - column + row_total, row_total) // rep_total
                 total += jnp.dot(
-                    dense_ref[s, rows], held[row_index ^ column], preferred_element_type=F32
+                    dense_ref[section, rows], held[i + core], preferred_element_type=F32
                 )
         finish(rows, total)
 
 
-def first_kernel(own_ref, other_ref, scale_ref, *refs):
+def near_kernel(far, row_total, own_ref, other_ref, *refs):
+    *block_refs, total_ref, held = refs
+
+    def start(rows):
+        return block_refs[0][rows].astype(F32)
+
+    def finish(rows, total):
+        total_ref[rows] = total
+
+    add_image(far, row_total, own_ref, other_ref, block_refs, held, start, finish)
+
+
+def more_kernel(far, row_total, own_ref, other_ref, sum_ref, *refs):
+    *block_refs, total_ref, held = refs
+
+    def finish(rows, total):
+        total_ref[rows] = total
+
+    add_image(far, row_total, own_ref, other_ref, block_refs, held, lambda rows: sum_ref[rows], finish)
+
+
+def first_kernel(far, row_total, own_ref, other_ref, sum_ref, scale_ref, *refs):
     *block_refs, heat_ref, second_ref, held = refs
 
     def finish(rows, total):
@@ -122,10 +146,12 @@
         heat_ref[rows] = heat
         second_ref[rows] = (scale * heat).astype(BF16)
 
-    image(own_ref, other_ref, block_refs, held, finish)
-
-
-def second_kernel(own_ref, other_ref, scale_ref, heat_ref, feature_ref, *refs):
+    add_image(far, row_total, own_ref, other_ref, block_refs, held, lambda rows: sum_ref[rows], finish)
+
+
+def second_kernel(
+    far, row_total, own_ref, other_ref, sum_ref, scale_ref, heat_ref, feature_ref, *refs
+):
     *block_refs, keep_ref, send_ref, held, mixed = refs
     replica = lax.axis_index("rep")
     part = mixed.shape[1]
@@ -135,7 +161,7 @@
         heat_two = scale_ref[rows] * total
         mixed[rows] = (feature.astype(F32) + 5.0 * heat_ref[rows] + 12.5 * heat_two).astype(BF16)
 
-    image(own_ref, other_ref, block_refs, held, finish)
+    add_image(far, row_total, own_ref, other_ref, block_refs, held, lambda rows: sum_ref[rows], finish)
     half = keep_ref.shape[0]
     keep_ref[...] = mixed[pl.ds(pl.multiple_of(replica * half, half), half), :]
     send_ref[...] = mixed[pl.ds(pl.multiple_of((1 - replica) * half, half), half), :]
@@ -187,27 +213,63 @@
         compiler_params=params(column, column, column, column),
     )(degree, degree_other, features)
 
-    blocks = gathered(first, "rows", row_total)
     dense_late, _ = lax.optimization_barrier((dense, scale))
-    dense_other = in_vmem(swapped(dense_late, "rep"))
-    heat_one, second = pl.pallas_call(
-        first_kernel,
-        out_shape=(shape(*column), shape(*field)),
-        in_specs=[VMEM] * (3 + row_total),
-        out_specs=(VMEM, VMEM),
-        scratch_shapes=[pltpu.VMEM(*held)],
-        compiler_params=params(panels, panels, column, column, held, held),
-    )(dense, dense_other, scale, *blocks)
-
-    blocks = gathered(second, "rows", row_total)
-    keep, send = pl.pallas_call(
-        second_kernel,
-        out_shape=(shape(*half), shape(*half)),
-        in_specs=[VMEM] * (5 + row_total),
-        out_specs=(VMEM, VMEM),
-        scratch_shapes=[pltpu.VMEM(*held), pltpu.VMEM(*field)],
-        compiler_params=params(panels, panels, column, column, column, held, held),
-    )(dense, dense_other, scale, heat_one, features, *blocks)
+    blocks, dense_other = gathered(first, "rows", row_total, swapped(dense_late, "rep"))
+    dense_other = in_vmem(dense_other)
+
+    def image(kernel, out_shape, blocks, *others, scratch=()):
+        return pl.pallas_call(
+            kernel,
+            out_shape=out_shape,
+            in_specs=[VMEM] * (2 + len(others) + len(blocks)),
+            out_specs=jax.tree.map(lambda _: VMEM, out_shape),
+            scratch_shapes=[pltpu.VMEM((len(blocks), rows_here, part), BF16), *scratch],
+            compiler_params=params(panels, panels, column, column, column, held, held),
+            cost_estimate=pl.CostEstimate(
+                flops=2 * len(blocks) * rows_here * rows_here * part,
+                bytes_accessed=0,
+                transcendentals=0,
+            ),
+        )(dense, dense_other, *others, *blocks)
+
+    cut = row_total // 2
+    early = list(range(cut))
+    arriving = [cut, *range(row_total - 1, cut, -1)]
+    middle, late = arriving[: cut // 2], arriving[cut // 2 :]
+
+    def image_start(blocks):
+        total = image(
+            functools.partial(near_kernel, early, row_total),
+            shape(*column),
+            [blocks[d] for d in early],
+        )
+        total = image(
+            functools.partial(more_kernel, middle, row_total),
+            shape(*column),
+            [blocks[d] for d in middle],
+            total,
+        )
+        return total, [blocks[d] for d in late]
+
+    total, blocks = image_start(blocks)
+    heat_one, second = image(
+        functools.partial(first_kernel, late, row_total),
+        (shape(*column), shape(*field)),
+        blocks,
+        total,
+        scale,
+    )
+    total, blocks = image_start(gathered(second, "rows", row_total)[0])
+    keep, send = image(
+        functools.partial(second_kernel, late, row_total),
+        (shape(*half), shape(*half)),
+        blocks,
+        total,
+        scale,
+        heat_one,
+        features,
+        scratch=[pltpu.VMEM(*field)],
+    )
     got = swapped(send, "rep")
     return pl.pallas_call(
         project_kernel,

time: 47.7 us -> 46.4 us (0.973)
  waiting for transfers between devices: 20.6 us -> 18.3 us
  Pallas kernels: 6.66 us -> 7.24 us
    ppermute x14, waiting for transfers between devices: 18.2 us -> 15.9 us  [xor_permute(): lax.ppermute(block, axis, [(i, i ^ distance) for i in range(lax.axis_size...]
    pallas_call x2 -> x6, Pallas kernels: 2.66 us -> 3.24 us  [image(): pl.pallas_call(kernel, out_shape=out_shape, in_specs=[VMEM] * (2 + len(ot...]
  transfers between devices with their start and end apart: 17 -> 17, of which waited for: 12 -> 10; matrix products, arithmetic and copies ran while one was open for 0% -> 0% of each run, Pallas kernels for 0% -> 5%
where the time goes in v4:
time: 46.4 us; the launch traced here: 46.2 us
  starting transfers between devices  20.6 us (44%)
  waiting for transfers between devices  18.3 us (39%)
  Pallas kernels  7.24 us (16%)
    ppermute x14, starting transfers between devices, xor_permute(): lax.ppermute(block, axis, [(i, i ^ distance) for i in range(lax.axis_size...  19.6 us
    ppermute x14, waiting for transfers between devices, xor_permute(): lax.ppermute(block, axis, [(i, i ^ distance) for i in range(lax.axis_size...  15.9 us
    pallas_call x6, Pallas kernels, image(): pl.pallas_call(kernel, out_shape=out_shape, in_specs=[VMEM] * (2 + len(ot...  3.24 us
    pallas_call x1, Pallas kernels, per_device(): pl.pallas_call(place_kernel, out_shape=(shape(*panels), shape(*column)),...  3.08 us
    ppermute x3, waiting for transfers between devices, swapped(): return lax.ppermute(block, axis, [(0, 1), (1, 0)])  2.41 us
    ppermute x3, starting transfers between devices, swapped(): return lax.ppermute(block, axis, [(0, 1), (1, 0)])  1.03 us
  transfers between devices with their start and end apart: 17, of which 10 were waited for; matrix products, arithmetic and copies ran while one was open for 0% of the time, Pallas kernels for 5%

profile of v4, /device:TPU:0, one launch (start us, length us, event | category | flops | bytes accessed | tf_op | source)
XLA Modules:
  0.0 46.2 jit_solution(5148691139800575737)
XLA Ops:
  0.0 3.1 %shard_map.55 = (bf16[4,512,512]{2,1,0:T(8,128)(2,1)S(1)}, f32[512,128]{1,0:T(8,128)S(1)}) custom-call(s32[4,16]{1,0:T(4,128)} %place_hbm.1, s32[4]{0:T(128)} %count_hbm.1, bf16[64,128,128]{2,1,0:T(8,128)(2,1)} %tiles_ref.1), custom_call_target="tpu_custom_call" | custom-call | tf_op jit(solution)/shard_map/pallas_call | solution.py:194
  3.1 0.5 %collective-permute-start = (f32[512,128]{1,0:T(8,128)S(1)}, f32[512,128]{1,0:T(8,128)S(1)}, u32[]{:S(2)}, u32[]{:S(2)}) collective-permute-start(f32[512,128]{1,0:T(8,128)S(1)} %get-tuple-element.22.degree_ref), channel_id=1, source_target_pairs={{0,1},{1,0},{2,3},{3,2},{4,5},{5,4},{6,7},{7,6},{8,9},{9,8},{10,11... | collective-permute-start | bytes 786440 | tf_op jit(solution)/shard_map/ppermute | solution.py:48
  3.6 1.2 %collective-permute-done.other_ref = f32[512,128]{1,0:T(8,128)S(1)} collective-permute-done((f32[512,128]{1,0:T(8,128)S(1)}, f32[512,128]{1,0:T(8,128)S(1)}, u32[]{:S(2)}, u32[]{:S(2)}) %collective-permute-start) | collective-permute-done | bytes 262176 | tf_op jit(solution)/shard_map/ppermute | solution.py:48
  4.8 0.4 collective-permute-start.4
  5.3 3.7 %collective-permute-start.1 = (bf16[512,128]{1,0:T(8,128)(2,1)S(1)}, bf16[512,128]{1,0:T(8,128)(2,1)S(1)}, u32[]{:S(2)}, u32[]{:S(2)}) collective-permute-start(bf16[512,128]{1,0:T(8,128)(2,1)S(1)} %get-tuple-element.23.refs_0_), channel_id=1, source_target_pairs={{0,8},{2,10},{4,12},{6,14},{8,0},{10,2},{12,4},{14,6},{1,9},{3,11}... | collective-permute-start | bytes 393224 | tf_op jit(solution)/shard_map/ppermute | solution.py:31
  9.0 1.5 %collective-permute-start.2 = (bf16[512,128]{1,0:T(8,128)(2,1)S(1)}, bf16[512,128]{1,0:T(8,128)(2,1)S(1)}, u32[]{:S(2)}, u32[]{:S(2)}) collective-permute-start(bf16[512,128]{1,0:T(8,128)(2,1)S(1)} %get-tuple-element.23.refs_0_), channel_id=1, source_target_pairs={{0,2},{2,0},{4,6},{6,4},{8,10},{10,8},{12,14},{14,12},{1,3},{3,1},... | collective-permute-start | bytes 393224 | tf_op jit(solution)/shard_map/ppermute | solution.py:31
  10.5 1.6 %collective-permute-start.3 = (bf16[512,128]{1,0:T(8,128)(2,1)S(1)}, bf16[512,128]{1,0:T(8,128)(2,1)S(1)}, u32[]{:S(2)}, u32[]{:S(2)}) collective-permute-start(bf16[512,128]{1,0:T(8,128)(2,1)S(1)} %get-tuple-element.23.refs_0_), channel_id=1, source_target_pairs={{0,4},{2,6},{4,0},{6,2},{8,12},{10,14},{12,8},{14,10},{1,5},{3,7},... | collective-permute-start | bytes 393224 | tf_op jit(solution)/shard_map/ppermute | solution.py:31
  12.1 0.4 collective-permute-start.5
  12.5 3.4 %collective-permute-done.1.refs_0_ = bf16[512,128]{1,0:T(8,128)(2,1)S(1)} collective-permute-done((bf16[512,128]{1,0:T(8,128)(2,1)S(1)}, bf16[512,128]{1,0:T(8,128)(2,1)S(1)}, u32[]{:S(2)}, u32[]{:S(2)}) %collective-permute-start.1) | collective-permute-done | bytes 131104 | tf_op jit(solution)/shard_map/ppermute | solution.py:31
  15.9 2.4 %collective-permute-done.3.refs_2_ = bf16[512,128]{1,0:T(8,128)(2,1)S(1)} collective-permute-done((bf16[512,128]{1,0:T(8,128)(2,1)S(1)}, bf16[512,128]{1,0:T(8,128)(2,1)S(1)}, u32[]{:S(2)}, u32[]{:S(2)}) %collective-permute-start.3) | collective-permute-done | bytes 131104 | tf_op jit(solution)/shard_map/ppermute | solution.py:31
  18.4 0.8 %collective-permute-start.6 = (bf16[512,128]{1,0:T(8,128)(2,1)S(1)}, bf16[512,128]{1,0:T(8,128)(2,1)S(1)}, u32[]{:S(2)}, u32[]{:S(2)}) collective-permute-start(bf16[512,128]{1,0:T(8,128)(2,1)S(1)} %collective-permute-done.1.refs_0_), channel_id=1, source_target_pairs={{0,6},{2,4},{4,2},{6,0},{8,14},{10,12},{12,10},{14,8},{1,7},{3,5},... | collective-permute-start | bytes 393224 | tf_op jit(solution)/shard_map/ppermute | solution.py:31
  19.1 1.0 %collective-permute-start.7 = (bf16[512,128]{1,0:T(8,128)(2,1)S(1)}, bf16[512,128]{1,0:T(8,128)(2,1)S(1)}, u32[]{:S(2)}, u32[]{:S(2)}) collective-permute-start(bf16[512,128]{1,0:T(8,128)(2,1)S(1)} %collective-permute-done.1.refs_0_), channel_id=1, source_target_pairs={{0,4},{2,6},{4,0},{6,2},{8,12},{10,14},{12,8},{14,10},{1,5},{3,7},... | collective-permute-start | bytes 393224 | tf_op jit(solution)/shard_map/ppermute | solution.py:31
  20.2 1.7 %collective-permute-start.8 = (bf16[512,128]{1,0:T(8,128)(2,1)S(1)}, bf16[512,128]{1,0:T(8,128)(2,1)S(1)}, u32[]{:S(2)}, u32[]{:S(2)}) collective-permute-start(bf16[512,128]{1,0:T(8,128)(2,1)S(1)} %collective-permute-done.1.refs_0_), channel_id=1, source_target_pairs={{0,2},{2,0},{4,6},{6,4},{8,10},{10,8},{12,14},{14,12},{1,3},{3,1},... | collective-permute-start | bytes 393224 | tf_op jit(solution)/shard_map/ppermute | solution.py:31
  21.9 0.7 %shard_map.57.sum_ref = f32[512,128]{1,0:T(8,128)S(1)} custom-call(bf16[4,512,512]{2,1,0:T(8,128)(2,1)S(1)} %get-tuple-element.25.own_ref, bf16[4,512,512]{2,1,0:T(8,128)(2,1)S(1)} %collective-permute-done.4.other_ref, bf16[512,128]{1,0:T(8,128)(2,1)S(1)} %get-tuple-element.23.refs_0_, bf16[512,128]{1,0:T(8,128)(2,1)S(1)} %collective-permute-done.2.refs_1_, ...), custom_call_target="tpu_custom_call" | custom-call | flops 268435456 | tf_op jit(solution)/shard_map/pallas_call | solution.py:221
  22.6 1.9 %collective-permute-done.6.refs_1_ = bf16[512,128]{1,0:T(8,128)(2,1)S(1)} collective-permute-done((bf16[512,128]{1,0:T(8,128)(2,1)S(1)}, bf16[512,128]{1,0:T(8,128)(2,1)S(1)}, u32[]{:S(2)}, u32[]{:S(2)}) %collective-permute-start.6) | collective-permute-done | bytes 131104 | tf_op jit(solution)/shard_map/ppermute | solution.py:31
  24.5 0.4 shard_map.58.sum_ref
  24.9 0.9 %collective-permute-done.7.refs_0_ = bf16[512,128]{1,0:T(8,128)(2,1)S(1)} collective-permute-done((bf16[512,128]{1,0:T(8,128)(2,1)S(1)}, bf16[512,128]{1,0:T(8,128)(2,1)S(1)}, u32[]{:S(2)}, u32[]{:S(2)}) %collective-permute-start.7) | collective-permute-done | bytes 131104 | tf_op jit(solution)/shard_map/ppermute | solution.py:31
  25.8 0.4 shard_map.59
  26.2 1.5 %collective-permute-start.10 = (bf16[512,128]{1,0:T(8,128)(2,1)S(1)}, bf16[512,128]{1,0:T(8,128)(2,1)S(1)}, u32[]{:S(2)}, u32[]{:S(2)}) collective-permute-start(bf16[512,128]{1,0:T(8,128)(2,1)S(1)} %get-tuple-element.30.refs_0_), channel_id=1, source_target_pairs={{0,2},{2,0},{4,6},{6,4},{8,10},{10,8},{12,14},{14,12},{1,3},{3,1},... | collective-permute-start | bytes 393224 | tf_op jit(solution)/shard_map/ppermute | solution.py:31
  27.8 0.6 %collective-permute-start.11 = (bf16[512,128]{1,0:T(8,128)(2,1)S(1)}, bf16[512,128]{1,0:T(8,128)(2,1)S(1)}, u32[]{:S(2)}, u32[]{:S(2)}) collective-permute-start(bf16[512,128]{1,0:T(8,128)(2,1)S(1)} %get-tuple-element.30.refs_0_), channel_id=1, source_target_pairs={{0,4},{2,6},{4,0},{6,2},{8,12},{10,14},{12,8},{14,10},{1,5},{3,7},... | collective-permute-start | bytes 393224 | tf_op jit(solution)/shard_map/ppermute | solution.py:31
  28.3 2.9 %collective-permute-start.9 = (bf16[512,128]{1,0:T(8,128)(2,1)S(1)}, bf16[512,128]{1,0:T(8,128)(2,1)S(1)}, u32[]{:S(2)}, u32[]{:S(2)}) collective-permute-start(bf16[512,128]{1,0:T(8,128)(2,1)S(1)} %get-tuple-element.30.refs_0_), channel_id=1, source_target_pairs={{0,8},{2,10},{4,12},{6,14},{8,0},{10,2},{12,4},{14,6},{1,9},{3,11}... | collective-permute-start | bytes 393224 | tf_op jit(solution)/shard_map/ppermute | solution.py:31
  31.6 4.5 %collective-permute-done.11.refs_2_ = bf16[512,128]{1,0:T(8,128)(2,1)S(1)} collective-permute-done((bf16[512,128]{1,0:T(8,128)(2,1)S(1)}, bf16[512,128]{1,0:T(8,128)(2,1)S(1)}, u32[]{:S(2)}, u32[]{:S(2)}) %collective-permute-start.11) | collective-permute-done | bytes 131104 | tf_op jit(solution)/shard_map/ppermute | solution.py:31
  36.1 1.9 %collective-permute-start.13 = (bf16[512,128]{1,0:T(8,128)(2,1)S(1)}, bf16[512,128]{1,0:T(8,128)(2,1)S(1)}, u32[]{:S(2)}, u32[]{:S(2)}) collective-permute-start(bf16[512,128]{1,0:T(8,128)(2,1)S(1)} %collective-permute-done.9.refs_0_), channel_id=1, source_target_pairs={{0,6},{2,4},{4,2},{6,0},{8,14},{10,12},{12,10},{14,8},{1,7},{3,5},... | collective-permute-start | bytes 393224 | tf_op jit(solution)/shard_map/ppermute | solution.py:31
  38.0 1.6 %collective-permute-start.15 = (bf16[512,128]{1,0:T(8,128)(2,1)S(1)}, bf16[512,128]{1,0:T(8,128)(2,1)S(1)}, u32[]{:S(2)}, u32[]{:S(2)}) collective-permute-start(bf16[512,128]{1,0:T(8,128)(2,1)S(1)} %collective-permute-done.9.refs_0_), channel_id=1, source_target_pairs={{0,2},{2,0},{4,6},{6,4},{8,10},{10,8},{12,14},{14,12},{1,3},{3,1},... | collective-permute-start | bytes 393224 | tf_op jit(solution)/shard_map/ppermute | solution.py:31
  39.6 0.7 %shard_map.60.sum_ref = f32[512,128]{1,0:T(8,128)S(1)} custom-call(bf16[4,512,512]{2,1,0:T(8,128)(2,1)S(1)} %get-tuple-element.25.own_ref, bf16[4,512,512]{2,1,0:T(8,128)(2,1)S(1)} %collective-permute-done.4.other_ref, bf16[512,128]{1,0:T(8,128)(2,1)S(1)} %get-tuple-element.30.refs_0_, bf16[512,128]{1,0:T(8,128)(2,1)S(1)} %collective-permute-done.10.refs_1_, ...), custom_call_target="tpu_custom_call" | custom-call | flops 268435456 | tf_op jit(solution)/shard_map/pallas_call | solution.py:221
  40.3 1.9 %collective-permute-done.13.refs_1_ = bf16[512,128]{1,0:T(8,128)(2,1)S(1)} collective-permute-done((bf16[512,128]{1,0:T(8,128)(2,1)S(1)}, bf16[512,128]{1,0:T(8,128)(2,1)S(1)}, u32[]{:S(2)}, u32[]{:S(2)}) %collective-permute-start.13) | collective-permute-done | bytes 131104 | tf_op jit(solution)/shard_map/ppermute | solution.py:31
  42.2 0.4 shard_map.61.sum_ref
  42.7 0.5 %collective-permute-done.14.refs_0_ = bf16[512,128]{1,0:T(8,128)(2,1)S(1)} collective-permute-done((bf16[512,128]{1,0:T(8,128)(2,1)S(1)}, bf16[512,128]{1,0:T(8,128)(2,1)S(1)}, u32[]{:S(2)}, u32[]{:S(2)}) %collective-permute-start.14) | collective-permute-done | bytes 131104 | tf_op jit(solution)/shard_map/ppermute | solution.py:31
  43.2 0.4 collective-permute-done.15.refs_1_
  43.6 0.5 %shard_map.62 = (bf16[256,128]{1,0:T(8,128)(2,1)S(1)}, bf16[256,128]{1,0:T(8,128)(2,1)S(1)}) custom-call(bf16[4,512,512]{2,1,0:T(8,128)(2,1)S(1)} %get-tuple-element.25.own_ref, bf16[4,512,512]{2,1,0:T(8,128)(2,1)S(1)} %collective-permute-done.4.other_ref, f32[512,128]{1,0:T(8,128)S(1)} %shard_map.61.sum_ref, f32[512,128]{1,0:T(8,128)S(1)} %get-tuple-element.24.scale_ref, ...), custom_call_target="tpu_custom_call" | custom-call | flops 134217728 | tf_op jit(solution)/shard_map/pallas_call | solution.py:221
  44.1 1.2 %collective-permute-done.16.got_ref = bf16[256,128]{1,0:T(8,128)(2,1)S(1)} collective-permute-done((bf16[256,128]{1,0:T(8,128)(2,1)S(1)}, bf16[256,128]{1,0:T(8,128)(2,1)S(1)}, u32[]{:S(2)}, u32[]{:S(2)}) %collective-permute-start.16) | collective-permute-done | bytes 65568 | tf_op jit(solution)/shard_map/ppermute | solution.py:48
  45.4 0.9 %shard_map.63 = bf16[256,256]{1,0:T(8,128)(2,1)} custom-call(bf16[256,128]{1,0:T(8,128)(2,1)S(1)} %get-tuple-element.35.keep_ref, bf16[256,128]{1,0:T(8,128)(2,1)S(1)} %collective-permute-done.16.got_ref, bf16[256,256]{1,0:T(8,128)(2,1)S(1)} %copy-done.1), custom_call_target="tpu_custom_call" | custom-call | tf_op jit(solution)/shard_map/pallas_call | solution.py:274
  (15 shorter events, 0.5 us)
Async XLA Ops:
  0.0 4.8 %copy-start = (bf16[512,256]{1,0:T(8,128)(2,1)S(1)}, bf16[512,256]{1,0:T(8,128)(2,1)}, u32[]{:S(2)}) copy-start(bf16[512,256]{1,0:T(8,128)(2,1)} %feature_ref.3) | copy-start | bytes 786436
  3.1 1.7 %collective-permute-start = (f32[512,128]{1,0:T(8,128)S(1)}, f32[512,128]{1,0:T(8,128)S(1)}, u32[]{:S(2)}, u32[]{:S(2)}) collective-permute-start(f32[512,128]{1,0:T(8,128)S(1)} %get-tuple-element.22.degree_ref), channel_id=1, source_target_pairs={{0,1},{1,0},{2,3},{3,2},{4,5},{5,4},{6,7},{7,6},{8,9},{9,8},{10,11... | collective-permute-start | bytes 786440 | tf_op jit(solution)/shard_map/ppermute | solution.py:48
  4.8 13.5 %collective-permute-start.4 = (bf16[4,512,512]{2,1,0:T(8,128)(2,1)S(1)}, bf16[4,512,512]{2,1,0:T(8,128)(2,1)S(1)}, u32[]{:S(2)}, u32[]{:S(2)}) collective-permute-start(bf16[4,512,512]{2,1,0:T(8,128)(2,1)S(1)} %get-tuple-element.25.own_ref), channel_id=1, source_target_pairs={{0,1},{1,0},{2,3},{3,2},{4,5},{5,4},{6,7},{7,6},{8,9},{9,8},{10,11... | collective-permute-start | bytes 6291464 | tf_op jit(solution)/shard_map/ppermute | solution.py:48
  5.3 10.7 %collective-permute-start.1 = (bf16[512,128]{1,0:T(8,128)(2,1)S(1)}, bf16[512,128]{1,0:T(8,128)(2,1)S(1)}, u32[]{:S(2)}, u32[]{:S(2)}) collective-permute-start(bf16[512,128]{1,0:T(8,128)(2,1)S(1)} %get-tuple-element.23.refs_0_), channel_id=1, source_target_pairs={{0,8},{2,10},{4,12},{6,14},{8,0},{10,2},{12,4},{14,6},{1,9},{3,11}... | collective-permute-start | bytes 393224 | tf_op jit(solution)/shard_map/ppermute | solution.py:31
  9.0 6.9 %collective-permute-start.2 = (bf16[512,128]{1,0:T(8,128)(2,1)S(1)}, bf16[512,128]{1,0:T(8,128)(2,1)S(1)}, u32[]{:S(2)}, u32[]{:S(2)}) collective-permute-start(bf16[512,128]{1,0:T(8,128)(2,1)S(1)} %get-tuple-element.23.refs_0_), channel_id=1, source_target_pairs={{0,2},{2,0},{4,6},{6,4},{8,10},{10,8},{12,14},{14,12},{1,3},{3,1},... | collective-permute-start | bytes 393224 | tf_op jit(solution)/shard_map/ppermute | solution.py:31
  10.5 7.8 %collective-permute-start.3 = (bf16[512,128]{1,0:T(8,128)(2,1)S(1)}, bf16[512,128]{1,0:T(8,128)(2,1)S(1)}, u32[]{:S(2)}, u32[]{:S(2)}) collective-permute-start(bf16[512,128]{1,0:T(8,128)(2,1)S(1)} %get-tuple-element.23.refs_0_), channel_id=1, source_target_pairs={{0,4},{2,6},{4,0},{6,2},{8,12},{10,14},{12,8},{14,10},{1,5},{3,7},... | collective-permute-start | bytes 393224 | tf_op jit(solution)/shard_map/ppermute | solution.py:31
  12.1 9.8 %collective-permute-start.5 = (bf16[512,128]{1,0:T(8,128)(2,1)S(1)}, bf16[512,128]{1,0:T(8,128)(2,1)S(1)}, u32[]{:S(2)}, u32[]{:S(2)}) collective-permute-start(bf16[512,128]{1,0:T(8,128)(2,1)S(1)} %get-tuple-element.23.refs_0_), channel_id=1, source_target_pairs={{0,6},{2,4},{4,2},{6,0},{8,14},{10,12},{12,10},{14,8},{1,7},{3,5},... | collective-permute-start | bytes 393224 | tf_op jit(solution)/shard_map/ppermute | solution.py:31
  18.4 6.1 %collective-permute-start.6 = (bf16[512,128]{1,0:T(8,128)(2,1)S(1)}, bf16[512,128]{1,0:T(8,128)(2,1)S(1)}, u32[]{:S(2)}, u32[]{:S(2)}) collective-permute-start(bf16[512,128]{1,0:T(8,128)(2,1)S(1)} %collective-permute-done.1.refs_0_), channel_id=1, source_target_pairs={{0,6},{2,4},{4,2},{6,0},{8,14},{10,12},{12,10},{14,8},{1,7},{3,5},... | collective-permute-start | bytes 393224 | tf_op jit(solution)/shard_map/ppermute | solution.py:31
  19.1 6.7 %collective-permute-start.7 = (bf16[512,128]{1,0:T(8,128)(2,1)S(1)}, bf16[512,128]{1,0:T(8,128)(2,1)S(1)}, u32[]{:S(2)}, u32[]{:S(2)}) collective-permute-start(bf16[512,128]{1,0:T(8,128)(2,1)S(1)} %collective-permute-done.1.refs_0_), channel_id=1, source_target_pairs={{0,4},{2,6},{4,0},{6,2},{8,12},{10,14},{12,8},{14,10},{1,5},{3,7},... | collective-permute-start | bytes 393224 | tf_op jit(solution)/shard_map/ppermute | solution.py:31
  20.2 5.6 %collective-permute-start.8 = (bf16[512,128]{1,0:T(8,128)(2,1)S(1)}, bf16[512,128]{1,0:T(8,128)(2,1)S(1)}, u32[]{:S(2)}, u32[]{:S(2)}) collective-permute-start(bf16[512,128]{1,0:T(8,128)(2,1)S(1)} %collective-permute-done.1.refs_0_), channel_id=1, source_target_pairs={{0,2},{2,0},{4,6},{6,4},{8,10},{10,8},{12,14},{14,12},{1,3},{3,1},... | collective-permute-start | bytes 393224 | tf_op jit(solution)/shard_map/ppermute | solution.py:31
  26.2 5.4 %collective-permute-start.10 = (bf16[512,128]{1,0:T(8,128)(2,1)S(1)}, bf16[512,128]{1,0:T(8,128)(2,1)S(1)}, u32[]{:S(2)}, u32[]{:S(2)}) collective-permute-start(bf16[512,128]{1,0:T(8,128)(2,1)S(1)} %get-tuple-element.30.refs_0_), channel_id=1, source_target_pairs={{0,2},{2,0},{4,6},{6,4},{8,10},{10,8},{12,14},{14,12},{1,3},{3,1},... | collective-permute-start | bytes 393224 | tf_op jit(solution)/shard_map/ppermute | solution.py:31
  27.8 8.3 %collective-permute-start.11 = (bf16[512,128]{1,0:T(8,128)(2,1)S(1)}, bf16[512,128]{1,0:T(8,128)(2,1)S(1)}, u32[]{:S(2)}, u32[]{:S(2)}) collective-permute-start(bf16[512,128]{1,0:T(8,128)(2,1)S(1)} %get-tuple-element.30.refs_0_), channel_id=1, source_target_pairs={{0,4},{2,6},{4,0},{6,2},{8,12},{10,14},{12,8},{14,10},{1,5},{3,7},... | collective-permute-start | bytes 393224 | tf_op jit(solution)/shard_map/ppermute | solution.py:31
  28.3 7.8 %collective-permute-start.9 = (bf16[512,128]{1,0:T(8,128)(2,1)S(1)}, bf16[512,128]{1,0:T(8,128)(2,1)S(1)}, u32[]{:S(2)}, u32[]{:S(2)}) collective-permute-start(bf16[512,128]{1,0:T(8,128)(2,1)S(1)} %get-tuple-element.30.refs_0_), channel_id=1, source_target_pairs={{0,8},{2,10},{4,12},{6,14},{8,0},{10,2},{12,4},{14,6},{1,9},{3,11}... | collective-permute-start | bytes 393224 | tf_op jit(solution)/shard_map/ppermute | solution.py:31
  31.3 8.3 %collective-permute-start.12 = (bf16[512,128]{1,0:T(8,128)(2,1)S(1)}, bf16[512,128]{1,0:T(8,128)(2,1)S(1)}, u32[]{:S(2)}, u32[]{:S(2)}) collective-permute-start(bf16[512,128]{1,0:T(8,128)(2,1)S(1)} %get-tuple-element.30.refs_0_), channel_id=1, source_target_pairs={{0,6},{2,4},{4,2},{6,0},{8,14},{10,12},{12,10},{14,8},{1,7},{3,5},... | collective-permute-start | bytes 393224 | tf_op jit(solution)/shard_map/ppermute | solution.py:31
  36.1 6.1 %collective-permute-start.13 = (bf16[512,128]{1,0:T(8,128)(2,1)S(1)}, bf16[512,128]{1,0:T(8,128)(2,1)S(1)}, u32[]{:S(2)}, u32[]{:S(2)}) collective-permute-start(bf16[512,128]{1,0:T(8,128)(2,1)S(1)} %collective-permute-done.9.refs_0_), channel_id=1, source_target_pairs={{0,6},{2,4},{4,2},{6,0},{8,14},{10,12},{12,10},{14,8},{1,7},{3,5},... | collective-permute-start | bytes 393224 | tf_op jit(solution)/shard_map/ppermute | solution.py:31
  38.0 5.2 %collective-permute-start.14 = (bf16[512,128]{1,0:T(8,128)(2,1)S(1)}, bf16[512,128]{1,0:T(8,128)(2,1)S(1)}, u32[]{:S(2)}, u32[]{:S(2)}) collective-permute-start(bf16[512,128]{1,0:T(8,128)(2,1)S(1)} %collective-permute-done.9.refs_0_), channel_id=1, source_target_pairs={{0,4},{2,6},{4,0},{6,2},{8,12},{10,14},{12,8},{14,10},{1,5},{3,7},... | collective-permute-start | bytes 393224 | tf_op jit(solution)/shard_map/ppermute | solution.py:31
  38.0 5.5 %collective-permute-start.15 = (bf16[512,128]{1,0:T(8,128)(2,1)S(1)}, bf16[512,128]{1,0:T(8,128)(2,1)S(1)}, u32[]{:S(2)}, u32[]{:S(2)}) collective-permute-start(bf16[512,128]{1,0:T(8,128)(2,1)S(1)} %collective-permute-done.9.refs_0_), channel_id=1, source_target_pairs={{0,2},{2,0},{4,6},{6,4},{8,10},{10,8},{12,14},{14,12},{1,3},{3,1},... | collective-permute-start | bytes 393224 | tf_op jit(solution)/shard_map/ppermute | solution.py:31
  43.6 1.8 %copy-start.1 = (bf16[256,256]{1,0:T(8,128)(2,1)S(1)}, bf16[256,256]{1,0:T(8,128)(2,1)}, u32[]{:S(2)}) copy-start(bf16[256,256]{1,0:T(8,128)(2,1)} %weight_ref.1) | copy-start | bytes 393220
  44.0 1.3 %collective-permute-start.16 = (bf16[256,128]{1,0:T(8,128)(2,1)S(1)}, bf16[256,128]{1,0:T(8,128)(2,1)S(1)}, u32[]{:S(2)}, u32[]{:S(2)}) collective-permute-start(bf16[256,128]{1,0:T(8,128)(2,1)S(1)} %get-tuple-element.36), channel_id=1, source_target_pairs={{0,1},{1,0},{2,3},{3,2},{4,5},{5,4},{6,7},{7,6},{8,9},{9,8},{10,11... | collective-permute-start | bytes 196616 | tf_op jit(solution)/shard_map/ppermute | solution.py:48

commit v5 on v4

--- a/solution.py
+++ b/solution.py
@@ -68,7 +68,6 @@
         copy(s).start()
     places.wait()
     counts.wait()
-    ones = jnp.ones((rows_here, degree_ref.shape[1]), BF16)
     for s in range(section_total):
         copy(s).wait()
         for k in range(slot_total):
@@ -79,11 +78,14 @@
             dense_ref[s, pl.ds(row, tile_dim), pl.ds(col, tile_dim)] = jnp.where(
                 k < count_ref[s], tile, jnp.zeros_like(tile)
             )
-        sums = jnp.dot(dense_ref[s], ones, preferred_element_type=F32)
-        if s == 0:
-            degree_ref[...] = sums
-        else:
-            degree_ref[...] += sums
+    ones = jnp.ones((rows_here, degree_ref.shape[1]), BF16)
+    chunk = rows_here // 2
+    for low in range(0, rows_here, chunk):
+        rows = pl.ds(low, chunk)
+        total = 0.0
+        for s in range(section_total):
+            total += jnp.dot(dense_ref[s, rows], ones, preferred_element_type=F32)
+        degree_ref[rows] = total
 
 
 def part_of(ref, index, size):
@@ -214,7 +216,8 @@
     )(degree, degree_other, features)
 
     dense_late, _ = lax.optimization_barrier((dense, scale))
-    blocks, dense_other = gathered(first, "rows", row_total, swapped(dense_late, "rep"))
+    blocks, _ = gathered(first, "rows", row_total)
+    dense_other = swapped(dense_late, "rep")
     dense_other = in_vmem(dense_other)
 
     def image(kernel, out_shape, blocks, *others, scratch=()):

time: 46.4 us -> 45.7 us (0.985)
  Pallas kernels: 7.24 us -> 6.61 us
    pallas_call x1, Pallas kernels: 3.08 us -> 2.45 us  [per_device(): pl.pallas_call(place_kernel, out_shape=(shape(*panels), shape(*column)),...]
where the time goes in v5:
time: 45.7 us; the launch traced here: 45.6 us
  starting transfers between devices  20.5 us (45%)
  waiting for transfers between devices  18.4 us (40%)
  Pallas kernels  6.61 us (14%)
    ppermute x14, starting transfers between devices, xor_permute(): lax.ppermute(block, axis, [(i, i ^ distance) for i in range(lax.axis_size...  19.5 us
    ppermute x14, waiting for transfers between devices, xor_permute(): lax.ppermute(block, axis, [(i, i ^ distance) for i in range(lax.axis_size...  15.9 us
    pallas_call x6, Pallas kernels, image(): pl.pallas_call(kernel, out_shape=out_shape, in_specs=[VMEM] * (2 + len(ot...  3.25 us
    pallas_call x1, Pallas kernels, per_device(): pl.pallas_call(place_kernel, out_shape=(shape(*panels), shape(*column)),...  2.45 us
    ppermute x3, waiting for transfers between devices, swapped(): return lax.ppermute(block, axis, [(0, 1), (1, 0)])  2.41 us
    ppermute x3, starting transfers between devices, swapped(): return lax.ppermute(block, axis, [(0, 1), (1, 0)])  1.03 us
  transfers between devices with their start and end apart: 17, of which 10 were waited for; matrix products, arithmetic and copies ran while one was open for 0% of the time, Pallas kernels for 5%

profile of v5, /device:TPU:0, one launch (start us, length us, event | category | flops | bytes accessed | tf_op | source)
XLA Modules:
  0.0 45.6 jit_solution(16544915622750524840)
XLA Ops:
  0.0 2.4 %shard_map.55 = (bf16[4,512,512]{2,1,0:T(8,128)(2,1)S(1)}, f32[512,128]{1,0:T(8,128)S(1)}) custom-call(s32[4,16]{1,0:T(4,128)} %place_hbm.1, s32[4]{0:T(128)} %count_hbm.1, bf16[64,128,128]{2,1,0:T(8,128)(2,1)} %tiles_ref.1), custom_call_target="tpu_custom_call" | custom-call | tf_op jit(solution)/shard_map/pallas_call | solution.py:196
  2.5 0.5 %collective-permute-start = (f32[512,128]{1,0:T(8,128)S(1)}, f32[512,128]{1,0:T(8,128)S(1)}, u32[]{:S(2)}, u32[]{:S(2)}) collective-permute-start(f32[512,128]{1,0:T(8,128)S(1)} %get-tuple-element.21.degree_ref), channel_id=1, source_target_pairs={{0,1},{1,0},{2,3},{3,2},{4,5},{5,4},{6,7},{7,6},{8,9},{9,8},{10,11... | collective-permute-start | bytes 786440 | tf_op jit(solution)/shard_map/ppermute | solution.py:48
  3.0 1.2 %collective-permute-done.other_ref = f32[512,128]{1,0:T(8,128)S(1)} collective-permute-done((f32[512,128]{1,0:T(8,128)S(1)}, f32[512,128]{1,0:T(8,128)S(1)}, u32[]{:S(2)}, u32[]{:S(2)}) %collective-permute-start) | collective-permute-done | bytes 262176 | tf_op jit(solution)/shard_map/ppermute | solution.py:48
  4.2 0.4 collective-permute-start.1
  4.6 3.7 %collective-permute-start.2 = (bf16[512,128]{1,0:T(8,128)(2,1)S(1)}, bf16[512,128]{1,0:T(8,128)(2,1)S(1)}, u32[]{:S(2)}, u32[]{:S(2)}) collective-permute-start(bf16[512,128]{1,0:T(8,128)(2,1)S(1)} %get-tuple-element.24.refs_0_), channel_id=1, source_target_pairs={{0,8},{2,10},{4,12},{6,14},{8,0},{10,2},{12,4},{14,6},{1,9},{3,11}... | collective-permute-start | bytes 393224 | tf_op jit(solution)/shard_map/ppermute | solution.py:31
  8.4 1.5 %collective-permute-start.3 = (bf16[512,128]{1,0:T(8,128)(2,1)S(1)}, bf16[512,128]{1,0:T(8,128)(2,1)S(1)}, u32[]{:S(2)}, u32[]{:S(2)}) collective-permute-start(bf16[512,128]{1,0:T(8,128)(2,1)S(1)} %get-tuple-element.24.refs_0_), channel_id=1, source_target_pairs={{0,2},{2,0},{4,6},{6,4},{8,10},{10,8},{12,14},{14,12},{1,3},{3,1},... | collective-permute-start | bytes 393224 | tf_op jit(solution)/shard_map/ppermute | solution.py:31
  9.9 1.6 %collective-permute-start.4 = (bf16[512,128]{1,0:T(8,128)(2,1)S(1)}, bf16[512,128]{1,0:T(8,128)(2,1)S(1)}, u32[]{:S(2)}, u32[]{:S(2)}) collective-permute-start(bf16[512,128]{1,0:T(8,128)(2,1)S(1)} %get-tuple-element.24.refs_0_), channel_id=1, source_target_pairs={{0,4},{2,6},{4,0},{6,2},{8,12},{10,14},{12,8},{14,10},{1,5},{3,7},... | collective-permute-start | bytes 393224 | tf_op jit(solution)/shard_map/ppermute | solution.py:31
  11.5 0.4 collective-permute-start.5
  11.9 3.4 %collective-permute-done.2.refs_0_ = bf16[512,128]{1,0:T(8,128)(2,1)S(1)} collective-permute-done((bf16[512,128]{1,0:T(8,128)(2,1)S(1)}, bf16[512,128]{1,0:T(8,128)(2,1)S(1)}, u32[]{:S(2)}, u32[]{:S(2)}) %collective-permute-start.2) | collective-permute-done | bytes 131104 | tf_op jit(solution)/shard_map/ppermute | solution.py:31
  15.3 2.4 %collective-permute-done.4.refs_2_ = bf16[512,128]{1,0:T(8,128)(2,1)S(1)} collective-permute-done((bf16[512,128]{1,0:T(8,128)(2,1)S(1)}, bf16[512,128]{1,0:T(8,128)(2,1)S(1)}, u32[]{:S(2)}, u32[]{:S(2)}) %collective-permute-start.4) | collective-permute-done | bytes 131104 | tf_op jit(solution)/shard_map/ppermute | solution.py:31
  17.7 0.8 %collective-permute-start.6 = (bf16[512,128]{1,0:T(8,128)(2,1)S(1)}, bf16[512,128]{1,0:T(8,128)(2,1)S(1)}, u32[]{:S(2)}, u32[]{:S(2)}) collective-permute-start(bf16[512,128]{1,0:T(8,128)(2,1)S(1)} %collective-permute-done.2.refs_0_), channel_id=1, source_target_pairs={{0,6},{2,4},{4,2},{6,0},{8,14},{10,12},{12,10},{14,8},{1,7},{3,5},... | collective-permute-start | bytes 393224 | tf_op jit(solution)/shard_map/ppermute | solution.py:31
  18.5 1.0 %collective-permute-start.7 = (bf16[512,128]{1,0:T(8,128)(2,1)S(1)}, bf16[512,128]{1,0:T(8,128)(2,1)S(1)}, u32[]{:S(2)}, u32[]{:S(2)}) collective-permute-start(bf16[512,128]{1,0:T(8,128)(2,1)S(1)} %collective-permute-done.2.refs_0_), channel_id=1, source_target_pairs={{0,4},{2,6},{4,0},{6,2},{8,12},{10,14},{12,8},{14,10},{1,5},{3,7},... | collective-permute-start | bytes 393224 | tf_op jit(solution)/shard_map/ppermute | solution.py:31
  19.5 1.7 %collective-permute-start.8 = (bf16[512,128]{1,0:T(8,128)(2,1)S(1)}, bf16[512,128]{1,0:T(8,128)(2,1)S(1)}, u32[]{:S(2)}, u32[]{:S(2)}) collective-permute-start(bf16[512,128]{1,0:T(8,128)(2,1)S(1)} %collective-permute-done.2.refs_0_), channel_id=1, source_target_pairs={{0,2},{2,0},{4,6},{6,4},{8,10},{10,8},{12,14},{14,12},{1,3},{3,1},... | collective-permute-start | bytes 393224 | tf_op jit(solution)/shard_map/ppermute | solution.py:31
  21.2 0.7 %shard_map.57.sum_ref = f32[512,128]{1,0:T(8,128)S(1)} custom-call(bf16[4,512,512]{2,1,0:T(8,128)(2,1)S(1)} %get-tuple-element.23.own_ref, bf16[4,512,512]{2,1,0:T(8,128)(2,1)S(1)} %collective-permute-done.1.other_ref, bf16[512,128]{1,0:T(8,128)(2,1)S(1)} %get-tuple-element.24.refs_0_, bf16[512,128]{1,0:T(8,128)(2,1)S(1)} %collective-permute-done.3.refs_1_, ...), custom_call_target="tpu_custom_call" | custom-call | flops 268435456 | tf_op jit(solution)/shard_map/pallas_call | solution.py:224
  21.9 1.9 %collective-permute-done.6.refs_1_ = bf16[512,128]{1,0:T(8,128)(2,1)S(1)} collective-permute-done((bf16[512,128]{1,0:T(8,128)(2,1)S(1)}, bf16[512,128]{1,0:T(8,128)(2,1)S(1)}, u32[]{:S(2)}, u32[]{:S(2)}) %collective-permute-start.6) | collective-permute-done | bytes 131104 | tf_op jit(solution)/shard_map/ppermute | solution.py:31
  23.8 0.4 shard_map.58.sum_ref
  24.3 0.9 %collective-permute-done.7.refs_0_ = bf16[512,128]{1,0:T(8,128)(2,1)S(1)} collective-permute-done((bf16[512,128]{1,0:T(8,128)(2,1)S(1)}, bf16[512,128]{1,0:T(8,128)(2,1)S(1)}, u32[]{:S(2)}, u32[]{:S(2)}) %collective-permute-start.7) | collective-permute-done | bytes 131104 | tf_op jit(solution)/shard_map/ppermute | solution.py:31
  25.2 0.4 shard_map.59
  25.6 1.5 %collective-permute-start.10 = (bf16[512,128]{1,0:T(8,128)(2,1)S(1)}, bf16[512,128]{1,0:T(8,128)(2,1)S(1)}, u32[]{:S(2)}, u32[]{:S(2)}) collective-permute-start(bf16[512,128]{1,0:T(8,128)(2,1)S(1)} %get-tuple-element.28.refs_0_), channel_id=1, source_target_pairs={{0,2},{2,0},{4,6},{6,4},{8,10},{10,8},{12,14},{14,12},{1,3},{3,1},... | collective-permute-start | bytes 393224 | tf_op jit(solution)/shard_map/ppermute | solution.py:31
  27.1 0.5 %collective-permute-start.11 = (bf16[512,128]{1,0:T(8,128)(2,1)S(1)}, bf16[512,128]{1,0:T(8,128)(2,1)S(1)}, u32[]{:S(2)}, u32[]{:S(2)}) collective-permute-start(bf16[512,128]{1,0:T(8,128)(2,1)S(1)} %get-tuple-element.28.refs_0_), channel_id=1, source_target_pairs={{0,4},{2,6},{4,0},{6,2},{8,12},{10,14},{12,8},{14,10},{1,5},{3,7},... | collective-permute-start | bytes 393224 | tf_op jit(solution)/shard_map/ppermute | solution.py:31
  27.7 2.9 %collective-permute-start.9 = (bf16[512,128]{1,0:T(8,128)(2,1)S(1)}, bf16[512,128]{1,0:T(8,128)(2,1)S(1)}, u32[]{:S(2)}, u32[]{:S(2)}) collective-permute-start(bf16[512,128]{1,0:T(8,128)(2,1)S(1)} %get-tuple-element.28.refs_0_), channel_id=1, source_target_pairs={{0,8},{2,10},{4,12},{6,14},{8,0},{10,2},{12,4},{14,6},{1,9},{3,11}... | collective-permute-start | bytes 393224 | tf_op jit(solution)/shard_map/ppermute | solution.py:31
  30.9 4.4 %collective-permute-done.11.refs_2_ = bf16[512,128]{1,0:T(8,128)(2,1)S(1)} collective-permute-done((bf16[512,128]{1,0:T(8,128)(2,1)S(1)}, bf16[512,128]{1,0:T(8,128)(2,1)S(1)}, u32[]{:S(2)}, u32[]{:S(2)}) %collective-permute-start.11) | collective-permute-done | bytes 131104 | tf_op jit(solution)/shard_map/ppermute | solution.py:31
  35.3 2.0 %collective-permute-start.13 = (bf16[512,128]{1,0:T(8,128)(2,1)S(1)}, bf16[512,128]{1,0:T(8,128)(2,1)S(1)}, u32[]{:S(2)}, u32[]{:S(2)}) collective-permute-start(bf16[512,128]{1,0:T(8,128)(2,1)S(1)} %collective-permute-done.9.refs_0_), channel_id=1, source_target_pairs={{0,6},{2,4},{4,2},{6,0},{8,14},{10,12},{12,10},{14,8},{1,7},{3,5},... | collective-permute-start | bytes 393224 | tf_op jit(solution)/shard_map/ppermute | solution.py:31
  37.3 1.5 %collective-permute-start.15 = (bf16[512,128]{1,0:T(8,128)(2,1)S(1)}, bf16[512,128]{1,0:T(8,128)(2,1)S(1)}, u32[]{:S(2)}, u32[]{:S(2)}) collective-permute-start(bf16[512,128]{1,0:T(8,128)(2,1)S(1)} %collective-permute-done.9.refs_0_), channel_id=1, source_target_pairs={{0,2},{2,0},{4,6},{6,4},{8,10},{10,8},{12,14},{14,12},{1,3},{3,1},... | collective-permute-start | bytes 393224 | tf_op jit(solution)/shard_map/ppermute | solution.py:31
  38.8 0.7 %shard_map.60.sum_ref = f32[512,128]{1,0:T(8,128)S(1)} custom-call(bf16[4,512,512]{2,1,0:T(8,128)(2,1)S(1)} %get-tuple-element.23.own_ref, bf16[4,512,512]{2,1,0:T(8,128)(2,1)S(1)} %collective-permute-done.1.other_ref, bf16[512,128]{1,0:T(8,128)(2,1)S(1)} %get-tuple-element.28.refs_0_, bf16[512,128]{1,0:T(8,128)(2,1)S(1)} %collective-permute-done.10.refs_1_, ...), custom_call_target="tpu_custom_call" | custom-call | flops 268435456 | tf_op jit(solution)/shard_map/pallas_call | solution.py:224
  39.5 2.1 %collective-permute-done.13.refs_1_ = bf16[512,128]{1,0:T(8,128)(2,1)S(1)} collective-permute-done((bf16[512,128]{1,0:T(8,128)(2,1)S(1)}, bf16[512,128]{1,0:T(8,128)(2,1)S(1)}, u32[]{:S(2)}, u32[]{:S(2)}) %collective-permute-start.13) | collective-permute-done | bytes 131104 | tf_op jit(solution)/shard_map/ppermute | solution.py:31
  41.5 0.4 shard_map.61.sum_ref
  42.0 0.4 collective-permute-done.14.refs_0_
  42.4 0.4 collective-permute-done.15.refs_1_
  42.9 0.5 %shard_map.62 = (bf16[256,128]{1,0:T(8,128)(2,1)S(1)}, bf16[256,128]{1,0:T(8,128)(2,1)S(1)}) custom-call(bf16[4,512,512]{2,1,0:T(8,128)(2,1)S(1)} %get-tuple-element.23.own_ref, bf16[4,512,512]{2,1,0:T(8,128)(2,1)S(1)} %collective-permute-done.1.other_ref, f32[512,128]{1,0:T(8,128)S(1)} %shard_map.61.sum_ref, f32[512,128]{1,0:T(8,128)S(1)} %get-tuple-element.22.scale_ref, ...), custom_call_target="tpu_custom_call" | custom-call | flops 134217728 | tf_op jit(solution)/shard_map/pallas_call | solution.py:224
  43.4 1.2 %collective-permute-done.16.got_ref = bf16[256,128]{1,0:T(8,128)(2,1)S(1)} collective-permute-done((bf16[256,128]{1,0:T(8,128)(2,1)S(1)}, bf16[256,128]{1,0:T(8,128)(2,1)S(1)}, u32[]{:S(2)}, u32[]{:S(2)}) %collective-permute-start.16) | collective-permute-done | bytes 65568 | tf_op jit(solution)/shard_map/ppermute | solution.py:48
  44.7 0.9 %shard_map.63 = bf16[256,256]{1,0:T(8,128)(2,1)} custom-call(bf16[256,128]{1,0:T(8,128)(2,1)S(1)} %get-tuple-element.33.keep_ref, bf16[256,128]{1,0:T(8,128)(2,1)S(1)} %collective-permute-done.16.got_ref, bf16[256,256]{1,0:T(8,128)(2,1)S(1)} %copy-done.1), custom_call_target="tpu_custom_call" | custom-call | tf_op jit(solution)/shard_map/pallas_call | solution.py:277
  (15 shorter events, 0.5 us)
Async XLA Ops:
  0.0 4.1 %copy-start = (bf16[512,256]{1,0:T(8,128)(2,1)S(1)}, bf16[512,256]{1,0:T(8,128)(2,1)}, u32[]{:S(2)}) copy-start(bf16[512,256]{1,0:T(8,128)(2,1)} %feature_ref.3) | copy-start | bytes 786436
  2.5 1.7 %collective-permute-start = (f32[512,128]{1,0:T(8,128)S(1)}, f32[512,128]{1,0:T(8,128)S(1)}, u32[]{:S(2)}, u32[]{:S(2)}) collective-permute-start(f32[512,128]{1,0:T(8,128)S(1)} %get-tuple-element.21.degree_ref), channel_id=1, source_target_pairs={{0,1},{1,0},{2,3},{3,2},{4,5},{5,4},{6,7},{7,6},{8,9},{9,8},{10,11... | collective-permute-start | bytes 786440 | tf_op jit(solution)/shard_map/ppermute | solution.py:48
  4.2 17.0 %collective-permute-start.1 = (bf16[4,512,512]{2,1,0:T(8,128)(2,1)S(1)}, bf16[4,512,512]{2,1,0:T(8,128)(2,1)S(1)}, u32[]{:S(2)}, u32[]{:S(2)}) collective-permute-start(bf16[4,512,512]{2,1,0:T(8,128)(2,1)S(1)} %get-tuple-element.23.own_ref), channel_id=1, source_target_pairs={{0,1},{1,0},{2,3},{3,2},{4,5},{5,4},{6,7},{7,6},{8,9},{9,8},{10,11... | collective-permute-start | bytes 6291464 | tf_op jit(solution)/shard_map/ppermute | solution.py:48
  4.6 10.7 %collective-permute-start.2 = (bf16[512,128]{1,0:T(8,128)(2,1)S(1)}, bf16[512,128]{1,0:T(8,128)(2,1)S(1)}, u32[]{:S(2)}, u32[]{:S(2)}) collective-permute-start(bf16[512,128]{1,0:T(8,128)(2,1)S(1)} %get-tuple-element.24.refs_0_), channel_id=1, source_target_pairs={{0,8},{2,10},{4,12},{6,14},{8,0},{10,2},{12,4},{14,6},{1,9},{3,11}... | collective-permute-start | bytes 393224 | tf_op jit(solution)/shard_map/ppermute | solution.py:31
  8.4 6.9 %collective-permute-start.3 = (bf16[512,128]{1,0:T(8,128)(2,1)S(1)}, bf16[512,128]{1,0:T(8,128)(2,1)S(1)}, u32[]{:S(2)}, u32[]{:S(2)}) collective-permute-start(bf16[512,128]{1,0:T(8,128)(2,1)S(1)} %get-tuple-element.24.refs_0_), channel_id=1, source_target_pairs={{0,2},{2,0},{4,6},{6,4},{8,10},{10,8},{12,14},{14,12},{1,3},{3,1},... | collective-permute-start | bytes 393224 | tf_op jit(solution)/shard_map/ppermute | solution.py:31
  9.9 7.8 %collective-permute-start.4 = (bf16[512,128]{1,0:T(8,128)(2,1)S(1)}, bf16[512,128]{1,0:T(8,128)(2,1)S(1)}, u32[]{:S(2)}, u32[]{:S(2)}) collective-permute-start(bf16[512,128]{1,0:T(8,128)(2,1)S(1)} %get-tuple-element.24.refs_0_), channel_id=1, source_target_pairs={{0,4},{2,6},{4,0},{6,2},{8,12},{10,14},{12,8},{14,10},{1,5},{3,7},... | collective-permute-start | bytes 393224 | tf_op jit(solution)/shard_map/ppermute | solution.py:31
  11.5 9.8 %collective-permute-start.5 = (bf16[512,128]{1,0:T(8,128)(2,1)S(1)}, bf16[512,128]{1,0:T(8,128)(2,1)S(1)}, u32[]{:S(2)}, u32[]{:S(2)}) collective-permute-start(bf16[512,128]{1,0:T(8,128)(2,1)S(1)} %get-tuple-element.24.refs_0_), channel_id=1, source_target_pairs={{0,6},{2,4},{4,2},{6,0},{8,14},{10,12},{12,10},{14,8},{1,7},{3,5},... | collective-permute-start | bytes 393224 | tf_op jit(solution)/shard_map/ppermute | solution.py:31
  17.7 6.1 %collective-permute-start.6 = (bf16[512,128]{1,0:T(8,128)(2,1)S(1)}, bf16[512,128]{1,0:T(8,128)(2,1)S(1)}, u32[]{:S(2)}, u32[]{:S(2)}) collective-permute-start(bf16[512,128]{1,0:T(8,128)(2,1)S(1)} %collective-permute-done.2.refs_0_), channel_id=1, source_target_pairs={{0,6},{2,4},{4,2},{6,0},{8,14},{10,12},{12,10},{14,8},{1,7},{3,5},... | collective-permute-start | bytes 393224 | tf_op jit(solution)/shard_map/ppermute | solution.py:31
  18.5 6.7 %collective-permute-start.7 = (bf16[512,128]{1,0:T(8,128)(2,1)S(1)}, bf16[512,128]{1,0:T(8,128)(2,1)S(1)}, u32[]{:S(2)}, u32[]{:S(2)}) collective-permute-start(bf16[512,128]{1,0:T(8,128)(2,1)S(1)} %collective-permute-done.2.refs_0_), channel_id=1, source_target_pairs={{0,4},{2,6},{4,0},{6,2},{8,12},{10,14},{12,8},{14,10},{1,5},{3,7},... | collective-permute-start | bytes 393224 | tf_op jit(solution)/shard_map/ppermute | solution.py:31
  19.5 5.6 %collective-permute-start.8 = (bf16[512,128]{1,0:T(8,128)(2,1)S(1)}, bf16[512,128]{1,0:T(8,128)(2,1)S(1)}, u32[]{:S(2)}, u32[]{:S(2)}) collective-permute-start(bf16[512,128]{1,0:T(8,128)(2,1)S(1)} %collective-permute-done.2.refs_0_), channel_id=1, source_target_pairs={{0,2},{2,0},{4,6},{6,4},{8,10},{10,8},{12,14},{14,12},{1,3},{3,1},... | collective-permute-start | bytes 393224 | tf_op jit(solution)/shard_map/ppermute | solution.py:31
  25.6 5.3 %collective-permute-start.10 = (bf16[512,128]{1,0:T(8,128)(2,1)S(1)}, bf16[512,128]{1,0:T(8,128)(2,1)S(1)}, u32[]{:S(2)}, u32[]{:S(2)}) collective-permute-start(bf16[512,128]{1,0:T(8,128)(2,1)S(1)} %get-tuple-element.28.refs_0_), channel_id=1, source_target_pairs={{0,2},{2,0},{4,6},{6,4},{8,10},{10,8},{12,14},{14,12},{1,3},{3,1},... | collective-permute-start | bytes 393224 | tf_op jit(solution)/shard_map/ppermute | solution.py:31
  27.1 8.1 %collective-permute-start.11 = (bf16[512,128]{1,0:T(8,128)(2,1)S(1)}, bf16[512,128]{1,0:T(8,128)(2,1)S(1)}, u32[]{:S(2)}, u32[]{:S(2)}) collective-permute-start(bf16[512,128]{1,0:T(8,128)(2,1)S(1)} %get-tuple-element.28.refs_0_), channel_id=1, source_target_pairs={{0,4},{2,6},{4,0},{6,2},{8,12},{10,14},{12,8},{14,10},{1,5},{3,7},... | collective-permute-start | bytes 393224 | tf_op jit(solution)/shard_map/ppermute | solution.py:31
  27.7 7.6 %collective-permute-start.9 = (bf16[512,128]{1,0:T(8,128)(2,1)S(1)}, bf16[512,128]{1,0:T(8,128)(2,1)S(1)}, u32[]{:S(2)}, u32[]{:S(2)}) collective-permute-start(bf16[512,128]{1,0:T(8,128)(2,1)S(1)} %get-tuple-element.28.refs_0_), channel_id=1, source_target_pairs={{0,8},{2,10},{4,12},{6,14},{8,0},{10,2},{12,4},{14,6},{1,9},{3,11}... | collective-permute-start | bytes 393224 | tf_op jit(solution)/shard_map/ppermute | solution.py:31
  30.6 8.2 %collective-permute-start.12 = (bf16[512,128]{1,0:T(8,128)(2,1)S(1)}, bf16[512,128]{1,0:T(8,128)(2,1)S(1)}, u32[]{:S(2)}, u32[]{:S(2)}) collective-permute-start(bf16[512,128]{1,0:T(8,128)(2,1)S(1)} %get-tuple-element.28.refs_0_), channel_id=1, source_target_pairs={{0,6},{2,4},{4,2},{6,0},{8,14},{10,12},{12,10},{14,8},{1,7},{3,5},... | collective-permute-start | bytes 393224 | tf_op jit(solution)/shard_map/ppermute | solution.py:31
  35.3 6.3 %collective-permute-start.13 = (bf16[512,128]{1,0:T(8,128)(2,1)S(1)}, bf16[512,128]{1,0:T(8,128)(2,1)S(1)}, u32[]{:S(2)}, u32[]{:S(2)}) collective-permute-start(bf16[512,128]{1,0:T(8,128)(2,1)S(1)} %collective-permute-done.9.refs_0_), channel_id=1, source_target_pairs={{0,6},{2,4},{4,2},{6,0},{8,14},{10,12},{12,10},{14,8},{1,7},{3,5},... | collective-permute-start | bytes 393224 | tf_op jit(solution)/shard_map/ppermute | solution.py:31
  37.3 5.2 %collective-permute-start.14 = (bf16[512,128]{1,0:T(8,128)(2,1)S(1)}, bf16[512,128]{1,0:T(8,128)(2,1)S(1)}, u32[]{:S(2)}, u32[]{:S(2)}) collective-permute-start(bf16[512,128]{1,0:T(8,128)(2,1)S(1)} %collective-permute-done.9.refs_0_), channel_id=1, source_target_pairs={{0,4},{2,6},{4,0},{6,2},{8,12},{10,14},{12,8},{14,10},{1,5},{3,7},... | collective-permute-start | bytes 393224 | tf_op jit(solution)/shard_map/ppermute | solution.py:31
  37.3 5.6 %collective-permute-start.15 = (bf16[512,128]{1,0:T(8,128)(2,1)S(1)}, bf16[512,128]{1,0:T(8,128)(2,1)S(1)}, u32[]{:S(2)}, u32[]{:S(2)}) collective-permute-start(bf16[512,128]{1,0:T(8,128)(2,1)S(1)} %collective-permute-done.9.refs_0_), channel_id=1, source_target_pairs={{0,2},{2,0},{4,6},{6,4},{8,10},{10,8},{12,14},{14,12},{1,3},{3,1},... | collective-permute-start | bytes 393224 | tf_op jit(solution)/shard_map/ppermute | solution.py:31
  42.9 1.8 %copy-start.1 = (bf16[256,256]{1,0:T(8,128)(2,1)S(1)}, bf16[256,256]{1,0:T(8,128)(2,1)}, u32[]{:S(2)}) copy-start(bf16[256,256]{1,0:T(8,128)(2,1)} %weight_ref.1) | copy-start | bytes 393220
  43.4 1.3 %collective-permute-start.16 = (bf16[256,128]{1,0:T(8,128)(2,1)S(1)}, bf16[256,128]{1,0:T(8,128)(2,1)S(1)}, u32[]{:S(2)}, u32[]{:S(2)}) collective-permute-start(bf16[256,128]{1,0:T(8,128)(2,1)S(1)} %get-tuple-element.34), channel_id=1, source_target_pairs={{0,1},{1,0},{2,3},{3,2},{4,5},{5,4},{6,7},{7,6},{8,9},{9,8},{10,11... | collective-permute-start | bytes 196616 | tf_op jit(solution)/shard_map/ppermute | solution.py:48

commit v6 on v5

--- a/solution.py
+++ b/solution.py
@@ -78,14 +78,16 @@
             dense_ref[s, pl.ds(row, tile_dim), pl.ds(col, tile_dim)] = jnp.where(
                 k < count_ref[s], tile, jnp.zeros_like(tile)
             )
-    ones = jnp.ones((rows_here, degree_ref.shape[1]), BF16)
+    ones = jnp.ones((rows_here, tile_dim), BF16)
     chunk = rows_here // 2
     for low in range(0, rows_here, chunk):
         rows = pl.ds(low, chunk)
         total = 0.0
         for s in range(section_total):
             total += jnp.dot(dense_ref[s, rows], ones, preferred_element_type=F32)
-        degree_ref[rows] = total
+        for i in range(chunk // tile_dim):
+            square = total[i * tile_dim : (i + 1) * tile_dim]
+            degree_ref[pl.ds(low // tile_dim + i, 1)] = square.T[:1]
 
 
 def part_of(ref, index, size):
@@ -93,29 +95,47 @@
 
 
 def scale_kernel(degree_ref, other_ref, feature_ref, scale_ref, first_ref):
-    scale = lax.rsqrt(1.0 + (degree_ref[...] + other_ref[...]))
-    scale_ref[...] = scale
-    feature = part_of(feature_ref, lax.axis_index("rep"), scale.shape[1])
-    first_ref[...] = (scale * feature.astype(F32)).astype(BF16)
+    spans, side = degree_ref.shape
+    row_scale = lax.rsqrt(1.0 + (degree_ref[...] + other_ref[...]))
+    for i in range(spans):
+        rows = pl.ds(i * side, side)
+        scale = jnp.broadcast_to(row_scale[i : i + 1], (side, side)).T[:, : scale_ref.shape[1]]
+        scale_ref[rows] = scale
+        low = pl.multiple_of(lax.axis_index("rep") * side, side)
+        feature = feature_ref[rows, pl.ds(low, side)]
+        first_ref[rows] = (scale * feature.astype(F32)).astype(BF16)
 
 
 def add_image(far, row_total, own_ref, other_ref, block_refs, held, start, finish, chunk=256):
     rep_total = row_total // own_ref.shape[0]
     row_index = lax.axis_index("rows")
     replica = lax.axis_index("rep")
-    for i, block_ref in enumerate(block_refs):
-        held[i] = block_ref[...]
-    for first_row in range(0, own_ref.shape[1], chunk):
-        rows = pl.ds(first_row, chunk)
-        total = start(rows)
-        for i in range(0, len(block_refs), rep_total):
-            for dense_ref, core in ((own_ref, replica), (other_ref, 1 - replica)):
-                column = row_index ^ (far[i] + core * (far[i + 1] - far[i]))
-                section = lax.rem(row_index - column + row_total, row_total) // rep_total
-                total += jnp.dot(
-                    dense_ref[section, rows], held[i + core], preferred_element_type=F32
-                )
-        finish(rows, total)
+
+    def product(rows, dense_ref, distance, block):
+        column = row_index ^ distance
+        section = lax.rem(row_index - column + row_total, row_total) // rep_total
+        return jnp.dot(dense_ref[section, rows], block, preferred_element_type=F32)
+
+    def run(single):
+        for first_row in range(0, own_ref.shape[1], chunk):
+            rows = pl.ds(first_row, chunk)
+            total = start(rows)
+            if single is not None:
+                total += product(rows, single, far[0], block_refs[0][...])
+            else:
+                for i in range(0, len(block_refs), rep_total):
+                    for dense_ref, core in ((own_ref, replica), (other_ref, 1 - replica)):
+                        distance = far[i] + core * (far[i + 1] - far[i])
+                        total += product(rows, dense_ref, distance, held[i + core])
+            finish(rows, total)
+
+    if len(far) > 1:
+        for i, block_ref in enumerate(block_refs):
+            held[i] = block_ref[...]
+        run(None)
+    else:
+        pl.when(replica == far[0] % rep_total)(lambda: run(own_ref))
+        pl.when(replica != far[0] % rep_total)(lambda: run(other_ref))
 
 
 def near_kernel(far, row_total, own_ref, other_ref, *refs):
@@ -195,7 +215,7 @@
 
     dense, degree = pl.pallas_call(
         place_kernel,
-        out_shape=(shape(*panels), shape(*column)),
+        out_shape=(shape(*panels), shape((rows_here // tiles.shape[1], tiles.shape[1]), F32)),
         in_specs=[HBM, HBM, HBM],
         out_specs=(VMEM, VMEM),
         scratch_shapes=[
@@ -238,7 +258,8 @@
     cut = row_total // 2
     early = list(range(cut))
     arriving = [cut, *range(row_total - 1, cut, -1)]
-    middle, late = arriving[: cut // 2], arriving[cut // 2 :]
+    stages = [arriving[: cut // 2], *([d] for d in arriving[cut // 2 :])]
+    late = stages.pop()
 
     def image_start(blocks):
         total = image(
@@ -246,12 +267,13 @@
             shape(*column),
             [blocks[d] for d in early],
         )
-        total = image(
-            functools.partial(more_kernel, middle, row_total),
-            shape(*column),
-            [blocks[d] for d in middle],
-            total,
-        )
+        for stage in stages:
+            total = image(
+                functools.partial(more_kernel, stage, row_total),
+                shape(*column),
+                [blocks[d] for d in stage],
+                total,
+            )
         return total, [blocks[d] for d in late]
 
     total, blocks = image_start(blocks)

time: 45.7 us -> 45.1 us (0.987)
  waiting for transfers between devices: 18.4 us -> 17.6 us
    pallas_call x6 -> x8, Pallas kernels: 3.25 us -> 3.49 us  [image(): pl.pallas_call(kernel, out_shape=out_shape, in_specs=[VMEM] * (2 + len(ot...]
  transfers between devices with their start and end apart: 17 -> 17, of which waited for: 10 -> 10; matrix products, arithmetic and copies ran while one was open for 0% -> 0% of each run, Pallas kernels for 5% -> 6%
where the time goes in v6:
time: 45.1 us; the launch traced here: 44.9 us
  starting transfers between devices  20.3 us (45%)
  waiting for transfers between devices  17.6 us (39%)
  Pallas kernels  6.98 us (15%)
    ppermute x14, starting transfers between devices, xor_permute(): lax.ppermute(block, axis, [(i, i ^ distance) for i in range(lax.axis_size...  19.3 us
    ppermute x14, waiting for transfers between devices, xor_permute(): lax.ppermute(block, axis, [(i, i ^ distance) for i in range(lax.axis_size...  15.5 us
    pallas_call x8, Pallas kernels, image(): pl.pallas_call(kernel, out_shape=out_shape, in_specs=[VMEM] * (2 + len(ot...  3.49 us
    pallas_call x1, Pallas kernels, per_device(): pl.pallas_call(place_kernel, out_shape=(shape(*panels), shape((rows_here...  2.48 us
    ppermute x3, waiting for transfers between devices, swapped(): return lax.ppermute(block, axis, [(0, 1), (1, 0)])  2.06 us
    ppermute x3, starting transfers between devices, swapped(): return lax.ppermute(block, axis, [(0, 1), (1, 0)])  0.99 us
  transfers between devices with their start and end apart: 17, of which 10 were waited for; matrix products, arithmetic and copies ran while one was open for 0% of the time, Pallas kernels for 6%

profile of v6, /device:TPU:0, one launch (start us, length us, event | category | flops | bytes accessed | tf_op | source)
XLA Modules:
  0.0 44.9 jit_solution(7421019890709009631)
XLA Ops:
  0.0 2.5 %shard_map.55 = (bf16[4,512,512]{2,1,0:T(8,128)(2,1)S(1)}, f32[4,128]{1,0:T(4,128)S(1)}) custom-call(s32[4,16]{1,0:T(4,128)} %place_hbm.1, s32[4]{0:T(128)} %count_hbm.1, bf16[64,128,128]{2,1,0:T(8,128)(2,1)} %tiles_ref.1), custom_call_target="tpu_custom_call" | custom-call | tf_op jit(solution)/shard_map/pallas_call | solution.py:216
  2.5 0.5 %collective-permute-start = (f32[4,128]{1,0:T(4,128)S(1)}, f32[4,128]{1,0:T(4,128)S(1)}, u32[]{:S(2)}, u32[]{:S(2)}) collective-permute-start(f32[4,128]{1,0:T(4,128)S(1)} %get-tuple-element.21.degree_ref), channel_id=1, source_target_pairs={{0,1},{1,0},{2,3},{3,2},{4,5},{5,4},{6,7},{7,6},{8,9},{9,8},{10,11... | collective-permute-start | bytes 6152 | tf_op jit(solution)/shard_map/ppermute | solution.py:48
  3.0 0.8 %collective-permute-done.other_ref = f32[4,128]{1,0:T(4,128)S(1)} collective-permute-done((f32[4,128]{1,0:T(4,128)S(1)}, f32[4,128]{1,0:T(4,128)S(1)}, u32[]{:S(2)}, u32[]{:S(2)}) %collective-permute-start) | collective-permute-done | bytes 2080 | tf_op jit(solution)/shard_map/ppermute | solution.py:48
  4.0 0.4 collective-permute-start.1
  4.4 3.8 %collective-permute-start.2 = (bf16[512,128]{1,0:T(8,128)(2,1)S(1)}, bf16[512,128]{1,0:T(8,128)(2,1)S(1)}, u32[]{:S(2)}, u32[]{:S(2)}) collective-permute-start(bf16[512,128]{1,0:T(8,128)(2,1)S(1)} %get-tuple-element.24.refs_0_), channel_id=1, source_target_pairs={{0,8},{2,10},{4,12},{6,14},{8,0},{10,2},{12,4},{14,6},{1,9},{3,11}... | collective-permute-start | bytes 393224 | tf_op jit(solution)/shard_map/ppermute | solution.py:31
  8.1 1.5 %collective-permute-start.3 = (bf16[512,128]{1,0:T(8,128)(2,1)S(1)}, bf16[512,128]{1,0:T(8,128)(2,1)S(1)}, u32[]{:S(2)}, u32[]{:S(2)}) collective-permute-start(bf16[512,128]{1,0:T(8,128)(2,1)S(1)} %get-tuple-element.24.refs_0_), channel_id=1, source_target_pairs={{0,2},{2,0},{4,6},{6,4},{8,10},{10,8},{12,14},{14,12},{1,3},{3,1},... | collective-permute-start | bytes 393224 | tf_op jit(solution)/shard_map/ppermute | solution.py:31
  9.7 1.6 %collective-permute-start.4 = (bf16[512,128]{1,0:T(8,128)(2,1)S(1)}, bf16[512,128]{1,0:T(8,128)(2,1)S(1)}, u32[]{:S(2)}, u32[]{:S(2)}) collective-permute-start(bf16[512,128]{1,0:T(8,128)(2,1)S(1)} %get-tuple-element.24.refs_0_), channel_id=1, source_target_pairs={{0,4},{2,6},{4,0},{6,2},{8,12},{10,14},{12,8},{14,10},{1,5},{3,7},... | collective-permute-start | bytes 393224 | tf_op jit(solution)/shard_map/ppermute | solution.py:31
  11.2 0.4 collective-permute-start.5
  11.6 3.4 %collective-permute-done.2.refs_0_ = bf16[512,128]{1,0:T(8,128)(2,1)S(1)} collective-permute-done((bf16[512,128]{1,0:T(8,128)(2,1)S(1)}, bf16[512,128]{1,0:T(8,128)(2,1)S(1)}, u32[]{:S(2)}, u32[]{:S(2)}) %collective-permute-start.2) | collective-permute-done | bytes 131104 | tf_op jit(solution)/shard_map/ppermute | solution.py:31
  15.1 2.4 %collective-permute-done.4.refs_2_ = bf16[512,128]{1,0:T(8,128)(2,1)S(1)} collective-permute-done((bf16[512,128]{1,0:T(8,128)(2,1)S(1)}, bf16[512,128]{1,0:T(8,128)(2,1)S(1)}, u32[]{:S(2)}, u32[]{:S(2)}) %collective-permute-start.4) | collective-permute-done | bytes 131104 | tf_op jit(solution)/shard_map/ppermute | solution.py:31
  17.5 0.8 %collective-permute-start.6 = (bf16[512,128]{1,0:T(8,128)(2,1)S(1)}, bf16[512,128]{1,0:T(8,128)(2,1)S(1)}, u32[]{:S(2)}, u32[]{:S(2)}) collective-permute-start(bf16[512,128]{1,0:T(8,128)(2,1)S(1)} %collective-permute-done.2.refs_0_), channel_id=1, source_target_pairs={{0,6},{2,4},{4,2},{6,0},{8,14},{10,12},{12,10},{14,8},{1,7},{3,5},... | collective-permute-start | bytes 393224 | tf_op jit(solution)/shard_map/ppermute | solution.py:31
  18.3 1.0 %collective-permute-start.7 = (bf16[512,128]{1,0:T(8,128)(2,1)S(1)}, bf16[512,128]{1,0:T(8,128)(2,1)S(1)}, u32[]{:S(2)}, u32[]{:S(2)}) collective-permute-start(bf16[512,128]{1,0:T(8,128)(2,1)S(1)} %collective-permute-done.2.refs_0_), channel_id=1, source_target_pairs={{0,4},{2,6},{4,0},{6,2},{8,12},{10,14},{12,8},{14,10},{1,5},{3,7},... | collective-permute-start | bytes 393224 | tf_op jit(solution)/shard_map/ppermute | solution.py:31
  19.3 1.7 %collective-permute-start.8 = (bf16[512,128]{1,0:T(8,128)(2,1)S(1)}, bf16[512,128]{1,0:T(8,128)(2,1)S(1)}, u32[]{:S(2)}, u32[]{:S(2)}) collective-permute-start(bf16[512,128]{1,0:T(8,128)(2,1)S(1)} %collective-permute-done.2.refs_0_), channel_id=1, source_target_pairs={{0,2},{2,0},{4,6},{6,4},{8,10},{10,8},{12,14},{14,12},{1,3},{3,1},... | collective-permute-start | bytes 393224 | tf_op jit(solution)/shard_map/ppermute | solution.py:31
  21.0 0.7 %shard_map.57.sum_ref = f32[512,128]{1,0:T(8,128)S(1)} custom-call(bf16[4,512,512]{2,1,0:T(8,128)(2,1)S(1)} %get-tuple-element.23.own_ref, bf16[4,512,512]{2,1,0:T(8,128)(2,1)S(1)} %collective-permute-done.1.other_ref, bf16[512,128]{1,0:T(8,128)(2,1)S(1)} %get-tuple-element.24.refs_0_, bf16[512,128]{1,0:T(8,128)(2,1)S(1)} %collective-permute-done.3.refs_1_, ...), custom_call_target="tpu_custom_call" | custom-call | flops 268435456 | tf_op jit(solution)/shard_map/pallas_call | solution.py:244
  21.7 1.9 %collective-permute-done.6.refs_1_ = bf16[512,128]{1,0:T(8,128)(2,1)S(1)} collective-permute-done((bf16[512,128]{1,0:T(8,128)(2,1)S(1)}, bf16[512,128]{1,0:T(8,128)(2,1)S(1)}, u32[]{:S(2)}, u32[]{:S(2)}) %collective-permute-start.6) | collective-permute-done | bytes 131104 | tf_op jit(solution)/shard_map/ppermute | solution.py:31
  23.6 0.4 shard_map.58.sum_ref
  24.0 0.9 %collective-permute-done.7.refs_0_ = bf16[512,128]{1,0:T(8,128)(2,1)S(1)} collective-permute-done((bf16[512,128]{1,0:T(8,128)(2,1)S(1)}, bf16[512,128]{1,0:T(8,128)(2,1)S(1)}, u32[]{:S(2)}, u32[]{:S(2)}) %collective-permute-start.7) | collective-permute-done | bytes 131104 | tf_op jit(solution)/shard_map/ppermute | solution.py:31
  25.2 0.3 shard_map.60
  25.5 1.2 %collective-permute-start.10 = (bf16[512,128]{1,0:T(8,128)(2,1)S(1)}, bf16[512,128]{1,0:T(8,128)(2,1)S(1)}, u32[]{:S(2)}, u32[]{:S(2)}) collective-permute-start(bf16[512,128]{1,0:T(8,128)(2,1)S(1)} %get-tuple-element.28.refs_0_), channel_id=1, source_target_pairs={{0,2},{2,0},{4,6},{6,4},{8,10},{10,8},{12,14},{14,12},{1,3},{3,1},... | collective-permute-start | bytes 393224 | tf_op jit(solution)/shard_map/ppermute | solution.py:31
  26.7 0.6 %collective-permute-start.11 = (bf16[512,128]{1,0:T(8,128)(2,1)S(1)}, bf16[512,128]{1,0:T(8,128)(2,1)S(1)}, u32[]{:S(2)}, u32[]{:S(2)}) collective-permute-start(bf16[512,128]{1,0:T(8,128)(2,1)S(1)} %get-tuple-element.28.refs_0_), channel_id=1, source_target_pairs={{0,4},{2,6},{4,0},{6,2},{8,12},{10,14},{12,8},{14,10},{1,5},{3,7},... | collective-permute-start | bytes 393224 | tf_op jit(solution)/shard_map/ppermute | solution.py:31
  27.4 2.8 %collective-permute-start.9 = (bf16[512,128]{1,0:T(8,128)(2,1)S(1)}, bf16[512,128]{1,0:T(8,128)(2,1)S(1)}, u32[]{:S(2)}, u32[]{:S(2)}) collective-permute-start(bf16[512,128]{1,0:T(8,128)(2,1)S(1)} %get-tuple-element.28.refs_0_), channel_id=1, source_target_pairs={{0,8},{2,10},{4,12},{6,14},{8,0},{10,2},{12,4},{14,6},{1,9},{3,11}... | collective-permute-start | bytes 393224 | tf_op jit(solution)/shard_map/ppermute | solution.py:31
  30.1 0.5 %collective-permute-start.12 = (bf16[512,128]{1,0:T(8,128)(2,1)S(1)}, bf16[512,128]{1,0:T(8,128)(2,1)S(1)}, u32[]{:S(2)}, u32[]{:S(2)}) collective-permute-start(bf16[512,128]{1,0:T(8,128)(2,1)S(1)} %get-tuple-element.28.refs_0_), channel_id=1, source_target_pairs={{0,6},{2,4},{4,2},{6,0},{8,14},{10,12},{12,10},{14,8},{1,7},{3,5},... | collective-permute-start | bytes 393224 | tf_op jit(solution)/shard_map/ppermute | solution.py:31
  30.6 4.1 %collective-permute-done.11.refs_2_ = bf16[512,128]{1,0:T(8,128)(2,1)S(1)} collective-permute-done((bf16[512,128]{1,0:T(8,128)(2,1)S(1)}, bf16[512,128]{1,0:T(8,128)(2,1)S(1)}, u32[]{:S(2)}, u32[]{:S(2)}) %collective-permute-start.11) | collective-permute-done | bytes 131104 | tf_op jit(solution)/shard_map/ppermute | solution.py:31
  34.7 2.1 %collective-permute-start.13 = (bf16[512,128]{1,0:T(8,128)(2,1)S(1)}, bf16[512,128]{1,0:T(8,128)(2,1)S(1)}, u32[]{:S(2)}, u32[]{:S(2)}) collective-permute-start(bf16[512,128]{1,0:T(8,128)(2,1)S(1)} %collective-permute-done.9.refs_0_), channel_id=1, source_target_pairs={{0,6},{2,4},{4,2},{6,0},{8,14},{10,12},{12,10},{14,8},{1,7},{3,5},... | collective-permute-start | bytes 393224 | tf_op jit(solution)/shard_map/ppermute | solution.py:31
  36.9 1.3 %collective-permute-start.15 = (bf16[512,128]{1,0:T(8,128)(2,1)S(1)}, bf16[512,128]{1,0:T(8,128)(2,1)S(1)}, u32[]{:S(2)}, u32[]{:S(2)}) collective-permute-start(bf16[512,128]{1,0:T(8,128)(2,1)S(1)} %collective-permute-done.9.refs_0_), channel_id=1, source_target_pairs={{0,2},{2,0},{4,6},{6,4},{8,10},{10,8},{12,14},{14,12},{1,3},{3,1},... | collective-permute-start | bytes 393224 | tf_op jit(solution)/shard_map/ppermute | solution.py:31
  38.2 0.7 %shard_map.61.sum_ref = f32[512,128]{1,0:T(8,128)S(1)} custom-call(bf16[4,512,512]{2,1,0:T(8,128)(2,1)S(1)} %get-tuple-element.23.own_ref, bf16[4,512,512]{2,1,0:T(8,128)(2,1)S(1)} %collective-permute-done.1.other_ref, bf16[512,128]{1,0:T(8,128)(2,1)S(1)} %get-tuple-element.28.refs_0_, bf16[512,128]{1,0:T(8,128)(2,1)S(1)} %collective-permute-done.10.refs_1_, ...), custom_call_target="tpu_custom_call" | custom-call | flops 268435456 | tf_op jit(solution)/shard_map/pallas_call | solution.py:244
  39.0 2.2 %collective-permute-done.13.refs_1_ = bf16[512,128]{1,0:T(8,128)(2,1)S(1)} collective-permute-done((bf16[512,128]{1,0:T(8,128)(2,1)S(1)}, bf16[512,128]{1,0:T(8,128)(2,1)S(1)}, u32[]{:S(2)}, u32[]{:S(2)}) %collective-permute-start.13) | collective-permute-done | bytes 131104 | tf_op jit(solution)/shard_map/ppermute | solution.py:31
  41.1 0.4 shard_map.62.sum_ref
  41.6 0.4 collective-permute-done.14.refs_0_
  42.5 0.3 shard_map.64
  42.8 1.2 %collective-permute-done.16.got_ref = bf16[256,128]{1,0:T(8,128)(2,1)S(1)} collective-permute-done((bf16[256,128]{1,0:T(8,128)(2,1)S(1)}, bf16[256,128]{1,0:T(8,128)(2,1)S(1)}, u32[]{:S(2)}, u32[]{:S(2)}) %collective-permute-start.16) | collective-permute-done | bytes 65568 | tf_op jit(solution)/shard_map/ppermute | solution.py:48
  44.1 0.9 %shard_map.65 = bf16[256,256]{1,0:T(8,128)(2,1)} custom-call(bf16[256,128]{1,0:T(8,128)(2,1)S(1)} %get-tuple-element.33.keep_ref, bf16[256,128]{1,0:T(8,128)(2,1)S(1)} %collective-permute-done.16.got_ref, bf16[256,256]{1,0:T(8,128)(2,1)S(1)} %copy-done.1), custom_call_target="tpu_custom_call" | custom-call | tf_op jit(solution)/shard_map/pallas_call | solution.py:299
  (17 shorter events, 1.0 us)
Async XLA Ops:
  0.0 3.8 %copy-start = (bf16[512,256]{1,0:T(8,128)(2,1)S(1)}, bf16[512,256]{1,0:T(8,128)(2,1)}, u32[]{:S(2)}) copy-start(bf16[512,256]{1,0:T(8,128)(2,1)} %feature_ref.3) | copy-start | bytes 786436
  2.5 1.3 %collective-permute-start = (f32[4,128]{1,0:T(4,128)S(1)}, f32[4,128]{1,0:T(4,128)S(1)}, u32[]{:S(2)}, u32[]{:S(2)}) collective-permute-start(f32[4,128]{1,0:T(4,128)S(1)} %get-tuple-element.21.degree_ref), channel_id=1, source_target_pairs={{0,1},{1,0},{2,3},{3,2},{4,5},{5,4},{6,7},{7,6},{8,9},{9,8},{10,11... | collective-permute-start | bytes 6152 | tf_op jit(solution)/shard_map/ppermute | solution.py:48
  4.0 17.0 %collective-permute-start.1 = (bf16[4,512,512]{2,1,0:T(8,128)(2,1)S(1)}, bf16[4,512,512]{2,1,0:T(8,128)(2,1)S(1)}, u32[]{:S(2)}, u32[]{:S(2)}) collective-permute-start(bf16[4,512,512]{2,1,0:T(8,128)(2,1)S(1)} %get-tuple-element.23.own_ref), channel_id=1, source_target_pairs={{0,1},{1,0},{2,3},{3,2},{4,5},{5,4},{6,7},{7,6},{8,9},{9,8},{10,11... | collective-permute-start | bytes 6291464 | tf_op jit(solution)/shard_map/ppermute | solution.py:48
  4.4 10.7 %collective-permute-start.2 = (bf16[512,128]{1,0:T(8,128)(2,1)S(1)}, bf16[512,128]{1,0:T(8,128)(2,1)S(1)}, u32[]{:S(2)}, u32[]{:S(2)}) collective-permute-start(bf16[512,128]{1,0:T(8,128)(2,1)S(1)} %get-tuple-element.24.refs_0_), channel_id=1, source_target_pairs={{0,8},{2,10},{4,12},{6,14},{8,0},{10,2},{12,4},{14,6},{1,9},{3,11}... | collective-permute-start | bytes 393224 | tf_op jit(solution)/shard_map/ppermute | solution.py:31
  8.1 6.9 %collective-permute-start.3 = (bf16[512,128]{1,0:T(8,128)(2,1)S(1)}, bf16[512,128]{1,0:T(8,128)(2,1)S(1)}, u32[]{:S(2)}, u32[]{:S(2)}) collective-permute-start(bf16[512,128]{1,0:T(8,128)(2,1)S(1)} %get-tuple-element.24.refs_0_), channel_id=1, source_target_pairs={{0,2},{2,0},{4,6},{6,4},{8,10},{10,8},{12,14},{14,12},{1,3},{3,1},... | collective-permute-start | bytes 393224 | tf_op jit(solution)/shard_map/ppermute | solution.py:31
  9.7 7.8 %collective-permute-start.4 = (bf16[512,128]{1,0:T(8,128)(2,1)S(1)}, bf16[512,128]{1,0:T(8,128)(2,1)S(1)}, u32[]{:S(2)}, u32[]{:S(2)}) collective-permute-start(bf16[512,128]{1,0:T(8,128)(2,1)S(1)} %get-tuple-element.24.refs_0_), channel_id=1, source_target_pairs={{0,4},{2,6},{4,0},{6,2},{8,12},{10,14},{12,8},{14,10},{1,5},{3,7},... | collective-permute-start | bytes 393224 | tf_op jit(solution)/shard_map/ppermute | solution.py:31
  11.2 9.7 %collective-permute-start.5 = (bf16[512,128]{1,0:T(8,128)(2,1)S(1)}, bf16[512,128]{1,0:T(8,128)(2,1)S(1)}, u32[]{:S(2)}, u32[]{:S(2)}) collective-permute-start(bf16[512,128]{1,0:T(8,128)(2,1)S(1)} %get-tuple-element.24.refs_0_), channel_id=1, source_target_pairs={{0,6},{2,4},{4,2},{6,0},{8,14},{10,12},{12,10},{14,8},{1,7},{3,5},... | collective-permute-start | bytes 393224 | tf_op jit(solution)/shard_map/ppermute | solution.py:31
  17.5 6.1 %collective-permute-start.6 = (bf16[512,128]{1,0:T(8,128)(2,1)S(1)}, bf16[512,128]{1,0:T(8,128)(2,1)S(1)}, u32[]{:S(2)}, u32[]{:S(2)}) collective-permute-start(bf16[512,128]{1,0:T(8,128)(2,1)S(1)} %collective-permute-done.2.refs_0_), channel_id=1, source_target_pairs={{0,6},{2,4},{4,2},{6,0},{8,14},{10,12},{12,10},{14,8},{1,7},{3,5},... | collective-permute-start | bytes 393224 | tf_op jit(solution)/shard_map/ppermute | solution.py:31
  18.3 6.6 %collective-permute-start.7 = (bf16[512,128]{1,0:T(8,128)(2,1)S(1)}, bf16[512,128]{1,0:T(8,128)(2,1)S(1)}, u32[]{:S(2)}, u32[]{:S(2)}) collective-permute-start(bf16[512,128]{1,0:T(8,128)(2,1)S(1)} %collective-permute-done.2.refs_0_), channel_id=1, source_target_pairs={{0,4},{2,6},{4,0},{6,2},{8,12},{10,14},{12,8},{14,10},{1,5},{3,7},... | collective-permute-start | bytes 393224 | tf_op jit(solution)/shard_map/ppermute | solution.py:31
  19.3 5.9 %collective-permute-start.8 = (bf16[512,128]{1,0:T(8,128)(2,1)S(1)}, bf16[512,128]{1,0:T(8,128)(2,1)S(1)}, u32[]{:S(2)}, u32[]{:S(2)}) collective-permute-start(bf16[512,128]{1,0:T(8,128)(2,1)S(1)} %collective-permute-done.2.refs_0_), channel_id=1, source_target_pairs={{0,2},{2,0},{4,6},{6,4},{8,10},{10,8},{12,14},{14,12},{1,3},{3,1},... | collective-permute-start | bytes 393224 | tf_op jit(solution)/shard_map/ppermute | solution.py:31
  25.5 5.1 %collective-permute-start.10 = (bf16[512,128]{1,0:T(8,128)(2,1)S(1)}, bf16[512,128]{1,0:T(8,128)(2,1)S(1)}, u32[]{:S(2)}, u32[]{:S(2)}) collective-permute-start(bf16[512,128]{1,0:T(8,128)(2,1)S(1)} %get-tuple-element.28.refs_0_), channel_id=1, source_target_pairs={{0,2},{2,0},{4,6},{6,4},{8,10},{10,8},{12,14},{14,12},{1,3},{3,1},... | collective-permute-start | bytes 393224 | tf_op jit(solution)/shard_map/ppermute | solution.py:31
  26.7 8.0 %collective-permute-start.11 = (bf16[512,128]{1,0:T(8,128)(2,1)S(1)}, bf16[512,128]{1,0:T(8,128)(2,1)S(1)}, u32[]{:S(2)}, u32[]{:S(2)}) collective-permute-start(bf16[512,128]{1,0:T(8,128)(2,1)S(1)} %get-tuple-element.28.refs_0_), channel_id=1, source_target_pairs={{0,4},{2,6},{4,0},{6,2},{8,12},{10,14},{12,8},{14,10},{1,5},{3,7},... | collective-permute-start | bytes 393224 | tf_op jit(solution)/shard_map/ppermute | solution.py:31
  27.4 7.4 %collective-permute-start.9 = (bf16[512,128]{1,0:T(8,128)(2,1)S(1)}, bf16[512,128]{1,0:T(8,128)(2,1)S(1)}, u32[]{:S(2)}, u32[]{:S(2)}) collective-permute-start(bf16[512,128]{1,0:T(8,128)(2,1)S(1)} %get-tuple-element.28.refs_0_), channel_id=1, source_target_pairs={{0,8},{2,10},{4,12},{6,14},{8,0},{10,2},{12,4},{14,6},{1,9},{3,11}... | collective-permute-start | bytes 393224 | tf_op jit(solution)/shard_map/ppermute | solution.py:31
  30.1 8.1 %collective-permute-start.12 = (bf16[512,128]{1,0:T(8,128)(2,1)S(1)}, bf16[512,128]{1,0:T(8,128)(2,1)S(1)}, u32[]{:S(2)}, u32[]{:S(2)}) collective-permute-start(bf16[512,128]{1,0:T(8,128)(2,1)S(1)} %get-tuple-element.28.refs_0_), channel_id=1, source_target_pairs={{0,6},{2,4},{4,2},{6,0},{8,14},{10,12},{12,10},{14,8},{1,7},{3,5},... | collective-permute-start | bytes 393224 | tf_op jit(solution)/shard_map/ppermute | solution.py:31
  34.7 6.4 %collective-permute-start.13 = (bf16[512,128]{1,0:T(8,128)(2,1)S(1)}, bf16[512,128]{1,0:T(8,128)(2,1)S(1)}, u32[]{:S(2)}, u32[]{:S(2)}) collective-permute-start(bf16[512,128]{1,0:T(8,128)(2,1)S(1)} %collective-permute-done.9.refs_0_), channel_id=1, source_target_pairs={{0,6},{2,4},{4,2},{6,0},{8,14},{10,12},{12,10},{14,8},{1,7},{3,5},... | collective-permute-start | bytes 393224 | tf_op jit(solution)/shard_map/ppermute | solution.py:31
  36.9 5.1 %collective-permute-start.14 = (bf16[512,128]{1,0:T(8,128)(2,1)S(1)}, bf16[512,128]{1,0:T(8,128)(2,1)S(1)}, u32[]{:S(2)}, u32[]{:S(2)}) collective-permute-start(bf16[512,128]{1,0:T(8,128)(2,1)S(1)} %collective-permute-done.9.refs_0_), channel_id=1, source_target_pairs={{0,4},{2,6},{4,0},{6,2},{8,12},{10,14},{12,8},{14,10},{1,5},{3,7},... | collective-permute-start | bytes 393224 | tf_op jit(solution)/shard_map/ppermute | solution.py:31
  36.9 5.6 %collective-permute-start.15 = (bf16[512,128]{1,0:T(8,128)(2,1)S(1)}, bf16[512,128]{1,0:T(8,128)(2,1)S(1)}, u32[]{:S(2)}, u32[]{:S(2)}) collective-permute-start(bf16[512,128]{1,0:T(8,128)(2,1)S(1)} %collective-permute-done.9.refs_0_), channel_id=1, source_target_pairs={{0,2},{2,0},{4,6},{6,4},{8,10},{10,8},{12,14},{14,12},{1,3},{3,1},... | collective-permute-start | bytes 393224 | tf_op jit(solution)/shard_map/ppermute | solution.py:31
  42.4 1.6 %copy-start.1 = (bf16[256,256]{1,0:T(8,128)(2,1)S(1)}, bf16[256,256]{1,0:T(8,128)(2,1)}, u32[]{:S(2)}) copy-start(bf16[256,256]{1,0:T(8,128)(2,1)} %weight_ref.1) | copy-start | bytes 393220
  42.8 1.3 %collective-permute-start.16 = (bf16[256,128]{1,0:T(8,128)(2,1)S(1)}, bf16[256,128]{1,0:T(8,128)(2,1)S(1)}, u32[]{:S(2)}, u32[]{:S(2)}) collective-permute-start(bf16[256,128]{1,0:T(8,128)(2,1)S(1)} %get-tuple-element.34), channel_id=1, source_target_pairs={{0,1},{1,0},{2,3},{3,2},{4,5},{5,4},{6,7},{7,6},{8,9},{9,8},{10,11... | collective-permute-start | bytes 196616 | tf_op jit(solution)/shard_map/ppermute | solution.py:48

commit v7 on v6

--- a/solution.py
+++ b/solution.py
@@ -31,12 +31,13 @@
     return lax.ppermute(block, axis, [(i, i ^ distance) for i in range(lax.axis_size(axis))])
 
 
-def gathered(block, axis, size, also=None):
+def gathered(block, axis, size, also=None, far_last=False):
     half = size // 2
     blocks = {0: block}
     for d in [1, half, *range(2, half)]:
         blocks[d] = xor_permute(block, axis, d)
-    early = [half, *range(1, half - 1)]
+    near = range(1, half - 1)
+    early = [*near[::-1], half] if far_last else [half, *near]
     tied, also = lax.optimization_barrier(([blocks[d] for d in early], also))
     blocks.update(zip(early, tied))
     for d in range(half - 1, 0, -1):
@@ -106,7 +107,7 @@
         first_ref[rows] = (scale * feature.astype(F32)).astype(BF16)
 
 
-def add_image(far, row_total, own_ref, other_ref, block_refs, held, start, finish, chunk=256):
+def add_image(far, row_total, own_ref, other_ref, block_refs, held, start, finish, lows=None, chunk=256):
     rep_total = row_total // own_ref.shape[0]
     row_index = lax.axis_index("rows")
     replica = lax.axis_index("rep")
@@ -117,7 +118,7 @@
         return jnp.dot(dense_ref[section, rows], block, preferred_element_type=F32)
 
     def run(single):
-        for first_row in range(0, own_ref.shape[1], chunk):
+        for first_row in lows or range(0, own_ref.shape[1], chunk):
             rows = pl.ds(first_row, chunk)
             total = start(rows)
             if single is not None:
@@ -171,32 +172,57 @@
     add_image(far, row_total, own_ref, other_ref, block_refs, held, lambda rows: sum_ref[rows], finish)
 
 
-def second_kernel(
-    far, row_total, own_ref, other_ref, sum_ref, scale_ref, heat_ref, feature_ref, *refs
-):
-    *block_refs, keep_ref, send_ref, held, mixed = refs
+def mixed_half(far, row_total, core, refs, block_refs, held, put):
+    own_ref, other_ref, sum_ref, scale_ref, heat_ref, feature_ref = refs
+    half = own_ref.shape[1] // 2
+    part = sum_ref.shape[1]
+    low = pl.multiple_of(lax.axis_index("rep") * part, part)
+
+    def finish(rows, total):
+        feature = feature_ref[rows, pl.ds(low, part)]
+        heat_two = scale_ref[rows] * total
+        put((feature.astype(F32) + 5.0 * heat_ref[rows] + 12.5 * heat_two).astype(BF16))
+
+    add_image(
+        far,
+        row_total,
+        own_ref,
+        other_ref,
+        block_refs,
+        held,
+        lambda rows: sum_ref[rows],
+        finish,
+        [pl.multiple_of(core * half, half)],
+        half,
+    )
+
+
+def send_kernel(far, row_total, *refs):
+    *block_refs, send_ref, held = refs[6:]
+
+    def put(mixed):
+        send_ref[...] = mixed
+
+    mixed_half(far, row_total, 1 - lax.axis_index("rep"), refs[:6], block_refs, held, put)
+
+
+def keep_kernel(far, row_total, *refs):
+    weight_ref, *block_refs, product_ref, held = refs[6:]
     replica = lax.axis_index("rep")
-    part = mixed.shape[1]
-
-    def finish(rows, total):
-        feature = feature_ref[rows, pl.ds(pl.multiple_of(replica * part, part), part)]
-        heat_two = scale_ref[rows] * total
-        mixed[rows] = (feature.astype(F32) + 5.0 * heat_ref[rows] + 12.5 * heat_two).astype(BF16)
-
-    add_image(far, row_total, own_ref, other_ref, block_refs, held, lambda rows: sum_ref[rows], finish)
-    half = keep_ref.shape[0]
-    keep_ref[...] = mixed[pl.ds(pl.multiple_of(replica * half, half), half), :]
-    send_ref[...] = mixed[pl.ds(pl.multiple_of((1 - replica) * half, half), half), :]
-
-
-def project_kernel(keep_ref, got_ref, weight_ref, out_ref):
-    replica = lax.axis_index("rep")
-    part = keep_ref.shape[1]
-    total = 0.0
-    for mixed_ref, core in ((keep_ref, replica), (got_ref, 1 - replica)):
-        weight = weight_ref[pl.ds(pl.multiple_of(core * part, part), part), :]
-        total += jnp.dot(mixed_ref[...], weight, preferred_element_type=F32)
-    out_ref[...] = total.astype(BF16)
+    part = block_refs[0].shape[1]
+
+    def put(mixed):
+        weight = weight_ref[pl.ds(pl.multiple_of(replica * part, part), part), :]
+        product_ref[...] = jnp.dot(mixed, weight, preferred_element_type=F32)
+
+    mixed_half(far, row_total, replica, refs[:6], block_refs, held, put)
+
+
+def project_kernel(product_ref, got_ref, weight_ref, out_ref):
+    part = got_ref.shape[1]
+    low = pl.multiple_of((1 - lax.axis_index("rep")) * part, part)
+    product = jnp.dot(got_ref[...], weight_ref[pl.ds(low, part), :], preferred_element_type=F32)
+    out_ref[...] = (product_ref[...] + product).astype(BF16)
 
 
 def per_device(features, weight, tiles, tile_place, panel_count):
@@ -236,7 +262,7 @@
     )(degree, degree_other, features)
 
     dense_late, _ = lax.optimization_barrier((dense, scale))
-    blocks, _ = gathered(first, "rows", row_total)
+    blocks, _ = gathered(first, "rows", row_total, far_last=True)
     dense_other = swapped(dense_late, "rep")
     dense_other = in_vmem(dense_other)
 
@@ -284,25 +310,25 @@
         total,
         scale,
     )
+    weight, second = lax.optimization_barrier((weight, second))
     total, blocks = image_start(gathered(second, "rows", row_total)[0])
-    keep, send = image(
-        functools.partial(second_kernel, late, row_total),
-        (shape(*half), shape(*half)),
+    given = total, scale, heat_one, features
+    send = image(functools.partial(send_kernel, late, row_total), shape(*half), blocks, *given)
+    got = swapped(send, "rep")
+    product = image(
+        functools.partial(keep_kernel, late, row_total),
+        shape((half_rows, width), F32),
         blocks,
-        total,
-        scale,
-        heat_one,
-        features,
-        scratch=[pltpu.VMEM(*field)],
-    )
-    got = swapped(send, "rep")
+        *given,
+        in_vmem(weight),
+    )
     return pl.pallas_call(
         project_kernel,
         out_shape=jax.ShapeDtypeStruct((half_rows, width), BF16),
         in_specs=[VMEM] * 3,
         out_specs=VMEM,
         compiler_params=params(column, column),
-    )(keep, got, in_vmem(weight))
+    )(product, got, in_vmem(weight))
 
 
 def solution(mesh):

time: 45.1 us -> 44.9 us (level)
  starting transfers between devices: 20.3 us -> 19.7 us
  local copies, waits for them, and re-layouts: 0.01 us -> 0.61 us
  waiting for transfers between devices: 17.6 us -> 17.1 us
    ppermute x3, waiting for transfers between devices: 2.06 us -> 1.09 us  [swapped(): return lax.ppermute(block, axis, [(0, 1), (1, 0)])]
    unnamed x4, local copies, waits for them, and re-layouts: 0.01 us -> 0.61 us
    ppermute x14, starting transfers between devices: 19.3 us -> 18.7 us  [xor_permute(): lax.ppermute(block, axis, [(i, i ^ distance) for i in range(lax.axis_size...]
    ppermute x14, waiting for transfers between devices: 15.5 us -> 16 us  [xor_permute(): lax.ppermute(block, axis, [(i, i ^ distance) for i in range(lax.axis_size...]
    pallas_call x8 -> x9, Pallas kernels: 3.49 us -> 3.78 us  [image(): pl.pallas_call(kernel, out_shape=out_shape, in_specs=[VMEM] * (2 + len(ot...]
  transfers between devices with their start and end apart: 17 -> 17, of which waited for: 10 -> 11; matrix products, arithmetic and copies ran while one was open for 0% -> 0% of each run, Pallas kernels for 6% -> 7%
where the time goes in v7:
time: 44.9 us; the launch traced here: 44.8 us
  starting transfers between devices  19.7 us (44%)
  waiting for transfers between devices  17.1 us (38%)
  Pallas kernels  7.23 us (16%)
  local copies, waits for them, and re-layouts  0.61 us (1%)
    ppermute x14, starting transfers between devices, xor_permute(): lax.ppermute(block, axis, [(i, i ^ distance) for i in range(lax.axis_size...  18.7 us
    ppermute x14, waiting for transfers between devices, xor_permute(): lax.ppermute(block, axis, [(i, i ^ distance) for i in range(lax.axis_size...  16 us
    pallas_call x9, Pallas kernels, image(): pl.pallas_call(kernel, out_shape=out_shape, in_specs=[VMEM] * (2 + len(ot...  3.78 us
    pallas_call x1, Pallas kernels, per_device(): pl.pallas_call(place_kernel, out_shape=(shape(*panels), shape((rows_here...  2.48 us
    ppermute x3, waiting for transfers between devices, swapped(): return lax.ppermute(block, axis, [(0, 1), (1, 0)])  1.09 us
    ppermute x3, starting transfers between devices, swapped(): return lax.ppermute(block, axis, [(0, 1), (1, 0)])  0.99 us
  transfers between devices with their start and end apart: 17, of which 11 were waited for; matrix products, arithmetic and copies ran while one was open for 0% of the time, Pallas kernels for 7%

profile of v7, /device:TPU:0, one launch (start us, length us, event | category | flops | bytes accessed | tf_op | source)
XLA Modules:
  0.0 44.8 jit_solution(10371845972916569917)
XLA Ops:
  0.0 2.5 %shard_map.55 = (bf16[4,512,512]{2,1,0:T(8,128)(2,1)S(1)}, f32[4,128]{1,0:T(4,128)S(1)}) custom-call(s32[4,16]{1,0:T(4,128)} %place_hbm.1, s32[4]{0:T(128)} %count_hbm.1, bf16[64,128,128]{2,1,0:T(8,128)(2,1)} %tiles_ref.1), custom_call_target="tpu_custom_call" | custom-call | tf_op jit(solution)/shard_map/pallas_call | solution.py:242
  2.5 0.5 %collective-permute-start = (f32[4,128]{1,0:T(4,128)S(1)}, f32[4,128]{1,0:T(4,128)S(1)}, u32[]{:S(2)}, u32[]{:S(2)}) collective-permute-start(f32[4,128]{1,0:T(4,128)S(1)} %get-tuple-element.21.degree_ref), channel_id=1, source_target_pairs={{0,1},{1,0},{2,3},{3,2},{4,5},{5,4},{6,7},{7,6},{8,9},{9,8},{10,11... | collective-permute-start | bytes 6152 | tf_op jit(solution)/shard_map/ppermute | solution.py:49
  3.0 0.8 %collective-permute-done.other_ref = f32[4,128]{1,0:T(4,128)S(1)} collective-permute-done((f32[4,128]{1,0:T(4,128)S(1)}, f32[4,128]{1,0:T(4,128)S(1)}, u32[]{:S(2)}, u32[]{:S(2)}) %collective-permute-start) | collective-permute-done | bytes 2080 | tf_op jit(solution)/shard_map/ppermute | solution.py:49
  4.0 0.4 collective-permute-start.1
  4.4 2.7 %collective-permute-start.2 = (bf16[512,128]{1,0:T(8,128)(2,1)S(1)}, bf16[512,128]{1,0:T(8,128)(2,1)S(1)}, u32[]{:S(2)}, u32[]{:S(2)}) collective-permute-start(bf16[512,128]{1,0:T(8,128)(2,1)S(1)} %get-tuple-element.24.refs_0_), channel_id=1, source_target_pairs={{0,4},{2,6},{4,0},{6,2},{8,12},{10,14},{12,8},{14,10},{1,5},{3,7},... | collective-permute-start | bytes 393224 | tf_op jit(solution)/shard_map/ppermute | solution.py:31
  7.1 1.5 %collective-permute-start.3 = (bf16[512,128]{1,0:T(8,128)(2,1)S(1)}, bf16[512,128]{1,0:T(8,128)(2,1)S(1)}, u32[]{:S(2)}, u32[]{:S(2)}) collective-permute-start(bf16[512,128]{1,0:T(8,128)(2,1)S(1)} %get-tuple-element.24.refs_0_), channel_id=1, source_target_pairs={{0,2},{2,0},{4,6},{6,4},{8,10},{10,8},{12,14},{14,12},{1,3},{3,1},... | collective-permute-start | bytes 393224 | tf_op jit(solution)/shard_map/ppermute | solution.py:31
  8.6 2.6 %collective-permute-start.4 = (bf16[512,128]{1,0:T(8,128)(2,1)S(1)}, bf16[512,128]{1,0:T(8,128)(2,1)S(1)}, u32[]{:S(2)}, u32[]{:S(2)}) collective-permute-start(bf16[512,128]{1,0:T(8,128)(2,1)S(1)} %get-tuple-element.24.refs_0_), channel_id=1, source_target_pairs={{0,8},{2,10},{4,12},{6,14},{8,0},{10,2},{12,4},{14,6},{1,9},{3,11}... | collective-permute-start | bytes 393224 | tf_op jit(solution)/shard_map/ppermute | solution.py:31
  11.2 0.4 collective-permute-start.5
  11.6 1.0 %collective-permute-done.3.refs_1_ = bf16[512,128]{1,0:T(8,128)(2,1)S(1)} collective-permute-done((bf16[512,128]{1,0:T(8,128)(2,1)S(1)}, bf16[512,128]{1,0:T(8,128)(2,1)S(1)}, u32[]{:S(2)}, u32[]{:S(2)}) %collective-permute-start.3) | collective-permute-done | bytes 131104 | tf_op jit(solution)/shard_map/ppermute | solution.py:31
  12.6 5.1 %collective-permute-done.4.refs_0_ = bf16[512,128]{1,0:T(8,128)(2,1)S(1)} collective-permute-done((bf16[512,128]{1,0:T(8,128)(2,1)S(1)}, bf16[512,128]{1,0:T(8,128)(2,1)S(1)}, u32[]{:S(2)}, u32[]{:S(2)}) %collective-permute-start.4) | collective-permute-done | bytes 131104 | tf_op jit(solution)/shard_map/ppermute | solution.py:31
  17.6 0.6 %collective-permute-start.6 = (bf16[512,128]{1,0:T(8,128)(2,1)S(1)}, bf16[512,128]{1,0:T(8,128)(2,1)S(1)}, u32[]{:S(2)}, u32[]{:S(2)}) collective-permute-start(bf16[512,128]{1,0:T(8,128)(2,1)S(1)} %collective-permute-done.4.refs_0_), channel_id=1, source_target_pairs={{0,6},{2,4},{4,2},{6,0},{8,14},{10,12},{12,10},{14,8},{1,7},{3,5},... | collective-permute-start | bytes 393224 | tf_op jit(solution)/shard_map/ppermute | solution.py:31
  18.3 1.1 %collective-permute-start.7 = (bf16[512,128]{1,0:T(8,128)(2,1)S(1)}, bf16[512,128]{1,0:T(8,128)(2,1)S(1)}, u32[]{:S(2)}, u32[]{:S(2)}) collective-permute-start(bf16[512,128]{1,0:T(8,128)(2,1)S(1)} %collective-permute-done.4.refs_0_), channel_id=1, source_target_pairs={{0,4},{2,6},{4,0},{6,2},{8,12},{10,14},{12,8},{14,10},{1,5},{3,7},... | collective-permute-start | bytes 393224 | tf_op jit(solution)/shard_map/ppermute | solution.py:31
  19.4 1.8 %collective-permute-start.8 = (bf16[512,128]{1,0:T(8,128)(2,1)S(1)}, bf16[512,128]{1,0:T(8,128)(2,1)S(1)}, u32[]{:S(2)}, u32[]{:S(2)}) collective-permute-start(bf16[512,128]{1,0:T(8,128)(2,1)S(1)} %collective-permute-done.4.refs_0_), channel_id=1, source_target_pairs={{0,2},{2,0},{4,6},{6,4},{8,10},{10,8},{12,14},{14,12},{1,3},{3,1},... | collective-permute-start | bytes 393224 | tf_op jit(solution)/shard_map/ppermute | solution.py:31
  21.1 0.7 %shard_map.57.sum_ref = f32[512,128]{1,0:T(8,128)S(1)} custom-call(bf16[4,512,512]{2,1,0:T(8,128)(2,1)S(1)} %get-tuple-element.23.own_ref.refs_0_, bf16[4,512,512]{2,1,0:T(8,128)(2,1)S(1)} %collective-permute-done.1.other_ref.refs_1_, bf16[512,128]{1,0:T(8,128)(2,1)S(1)} %get-tuple-element.24.refs_0_, bf16[512,128]{1,0:T(8,128)(2,1)S(1)} %collective-permute-done.3.refs_1_, ...), custom_call_target="tpu_custom_call" | custom-call | flops 268435456 | tf_op jit(solution)/shard_map/pallas_call | solution.py:270
  21.9 2.3 %collective-permute-done.6.refs_1_ = bf16[512,128]{1,0:T(8,128)(2,1)S(1)} collective-permute-done((bf16[512,128]{1,0:T(8,128)(2,1)S(1)}, bf16[512,128]{1,0:T(8,128)(2,1)S(1)}, u32[]{:S(2)}, u32[]{:S(2)}) %collective-permute-start.6) | collective-permute-done | bytes 131104 | tf_op jit(solution)/shard_map/ppermute | solution.py:31
  24.2 0.4 shard_map.58.sum_ref
  24.9 0.5 %collective-permute-done.8.refs_0_ = bf16[512,128]{1,0:T(8,128)(2,1)S(1)} collective-permute-done((bf16[512,128]{1,0:T(8,128)(2,1)S(1)}, bf16[512,128]{1,0:T(8,128)(2,1)S(1)}, u32[]{:S(2)}, u32[]{:S(2)}) %collective-permute-start.8) | collective-permute-done | bytes 131104 | tf_op jit(solution)/shard_map/ppermute | solution.py:31
  25.8 0.9 %collective-permute-start.10 = (bf16[512,128]{1,0:T(8,128)(2,1)S(1)}, bf16[512,128]{1,0:T(8,128)(2,1)S(1)}, u32[]{:S(2)}, u32[]{:S(2)}) collective-permute-start(bf16[512,128]{1,0:T(8,128)(2,1)S(1)} %get-tuple-element.29.refs_0_), channel_id=1, source_target_pairs={{0,2},{2,0},{4,6},{6,4},{8,10},{10,8},{12,14},{14,12},{1,3},{3,1},... | collective-permute-start | bytes 393224 | tf_op jit(solution)/shard_map/ppermute | solution.py:31
  26.7 0.5 %collective-permute-start.11 = (bf16[512,128]{1,0:T(8,128)(2,1)S(1)}, bf16[512,128]{1,0:T(8,128)(2,1)S(1)}, u32[]{:S(2)}, u32[]{:S(2)}) collective-permute-start(bf16[512,128]{1,0:T(8,128)(2,1)S(1)} %get-tuple-element.29.refs_0_), channel_id=1, source_target_pairs={{0,4},{2,6},{4,0},{6,2},{8,12},{10,14},{12,8},{14,10},{1,5},{3,7},... | collective-permute-start | bytes 393224 | tf_op jit(solution)/shard_map/ppermute | solution.py:31
  27.3 2.3 %collective-permute-start.9 = (bf16[512,128]{1,0:T(8,128)(2,1)S(1)}, bf16[512,128]{1,0:T(8,128)(2,1)S(1)}, u32[]{:S(2)}, u32[]{:S(2)}) collective-permute-start(bf16[512,128]{1,0:T(8,128)(2,1)S(1)} %get-tuple-element.29.refs_0_), channel_id=1, source_target_pairs={{0,8},{2,10},{4,12},{6,14},{8,0},{10,2},{12,4},{14,6},{1,9},{3,11}... | collective-permute-start | bytes 393224 | tf_op jit(solution)/shard_map/ppermute | solution.py:31
  29.5 0.7 %collective-permute-start.12 = (bf16[512,128]{1,0:T(8,128)(2,1)S(1)}, bf16[512,128]{1,0:T(8,128)(2,1)S(1)}, u32[]{:S(2)}, u32[]{:S(2)}) collective-permute-start(bf16[512,128]{1,0:T(8,128)(2,1)S(1)} %get-tuple-element.29.refs_0_), channel_id=1, source_target_pairs={{0,6},{2,4},{4,2},{6,0},{8,14},{10,12},{12,10},{14,8},{1,7},{3,5},... | collective-permute-start | bytes 393224 | tf_op jit(solution)/shard_map/ppermute | solution.py:31
  30.3 0.9 %collective-permute-done.10.refs_1_ = bf16[512,128]{1,0:T(8,128)(2,1)S(1)} collective-permute-done((bf16[512,128]{1,0:T(8,128)(2,1)S(1)}, bf16[512,128]{1,0:T(8,128)(2,1)S(1)}, u32[]{:S(2)}, u32[]{:S(2)}) %collective-permute-start.10) | collective-permute-done | bytes 131104 | tf_op jit(solution)/shard_map/ppermute | solution.py:31
  31.2 3.7 %collective-permute-done.11.refs_2_ = bf16[512,128]{1,0:T(8,128)(2,1)S(1)} collective-permute-done((bf16[512,128]{1,0:T(8,128)(2,1)S(1)}, bf16[512,128]{1,0:T(8,128)(2,1)S(1)}, u32[]{:S(2)}, u32[]{:S(2)}) %collective-permute-start.11) | collective-permute-done | bytes 131104 | tf_op jit(solution)/shard_map/ppermute | solution.py:31
  34.9 0.9 %collective-permute-start.13 = (bf16[512,128]{1,0:T(8,128)(2,1)S(1)}, bf16[512,128]{1,0:T(8,128)(2,1)S(1)}, u32[]{:S(2)}, u32[]{:S(2)}) collective-permute-start(bf16[512,128]{1,0:T(8,128)(2,1)S(1)} %collective-permute-done.9.refs_0_), channel_id=1, source_target_pairs={{0,6},{2,4},{4,2},{6,0},{8,14},{10,12},{12,10},{14,8},{1,7},{3,5},... | collective-permute-start | bytes 393224 | tf_op jit(solution)/shard_map/ppermute | solution.py:31
  35.8 1.7 %collective-permute-start.14 = (bf16[512,128]{1,0:T(8,128)(2,1)S(1)}, bf16[512,128]{1,0:T(8,128)(2,1)S(1)}, u32[]{:S(2)}, u32[]{:S(2)}) collective-permute-start(bf16[512,128]{1,0:T(8,128)(2,1)S(1)} %collective-permute-done.9.refs_0_), channel_id=1, source_target_pairs={{0,4},{2,6},{4,0},{6,2},{8,12},{10,14},{12,8},{14,10},{1,5},{3,7},... | collective-permute-start | bytes 393224 | tf_op jit(solution)/shard_map/ppermute | solution.py:31
  37.4 0.9 %collective-permute-start.15 = (bf16[512,128]{1,0:T(8,128)(2,1)S(1)}, bf16[512,128]{1,0:T(8,128)(2,1)S(1)}, u32[]{:S(2)}, u32[]{:S(2)}) collective-permute-start(bf16[512,128]{1,0:T(8,128)(2,1)S(1)} %collective-permute-done.9.refs_0_), channel_id=1, source_target_pairs={{0,2},{2,0},{4,6},{6,4},{8,10},{10,8},{12,14},{14,12},{1,3},{3,1},... | collective-permute-start | bytes 393224 | tf_op jit(solution)/shard_map/ppermute | solution.py:31
  38.4 0.7 %shard_map.61.sum_ref = f32[512,128]{1,0:T(8,128)S(1)} custom-call(bf16[4,512,512]{2,1,0:T(8,128)(2,1)S(1)} %get-tuple-element.23.own_ref.refs_0_, bf16[4,512,512]{2,1,0:T(8,128)(2,1)S(1)} %collective-permute-done.1.other_ref.refs_1_, bf16[512,128]{1,0:T(8,128)(2,1)S(1)} %get-tuple-element.29.refs_0_, bf16[512,128]{1,0:T(8,128)(2,1)S(1)} %collective-permute-done.10.refs_1_, ...), custom_call_target="tpu_custom_call" | custom-call | flops 268435456 | tf_op jit(solution)/shard_map/pallas_call | solution.py:270
  39.1 1.7 %collective-permute-done.13.refs_1_ = bf16[512,128]{1,0:T(8,128)(2,1)S(1)} collective-permute-done((bf16[512,128]{1,0:T(8,128)(2,1)S(1)}, bf16[512,128]{1,0:T(8,128)(2,1)S(1)}, u32[]{:S(2)}, u32[]{:S(2)}) %collective-permute-start.13) | collective-permute-done | bytes 131104 | tf_op jit(solution)/shard_map/ppermute | solution.py:31
  40.8 0.4 shard_map.62.sum_ref
  41.3 0.5 %collective-permute-done.14.refs_0_ = bf16[512,128]{1,0:T(8,128)(2,1)S(1)} collective-permute-done((bf16[512,128]{1,0:T(8,128)(2,1)S(1)}, bf16[512,128]{1,0:T(8,128)(2,1)S(1)}, u32[]{:S(2)}, u32[]{:S(2)}) %collective-permute-start.14) | collective-permute-done | bytes 131104 | tf_op jit(solution)/shard_map/ppermute | solution.py:31
  42.7 0.6 %copy-done.1 = bf16[256,256]{1,0:T(8,128)(2,1)S(1)} copy-done((bf16[256,256]{1,0:T(8,128)(2,1)S(1)}, bf16[256,256]{1,0:T(8,128)(2,1)}, u32[]{:S(2)}) %copy-start.1) | copy-done | bytes 131096
  43.9 0.8 %shard_map.66 = bf16[256,256]{1,0:T(8,128)(2,1)} custom-call(f32[256,256]{1,0:T(8,128)S(1)} %shard_map.64.product_ref, bf16[256,128]{1,0:T(8,128)(2,1)S(1)} %collective-permute-done.16.got_ref, bf16[256,256]{1,0:T(8,128)(2,1)S(1)} %copy-done.1), custom_call_target="tpu_custom_call" | custom-call | tf_op jit(solution)/shard_map/pallas_call | solution.py:325
  (18 shorter events, 2.3 us)
Async XLA Ops:
  0.0 3.8 %copy-start = (bf16[512,256]{1,0:T(8,128)(2,1)S(1)}, bf16[512,256]{1,0:T(8,128)(2,1)}, u32[]{:S(2)}) copy-start(bf16[512,256]{1,0:T(8,128)(2,1)} %refs_5_.3) | copy-start | bytes 786436
  2.5 1.3 %collective-permute-start = (f32[4,128]{1,0:T(4,128)S(1)}, f32[4,128]{1,0:T(4,128)S(1)}, u32[]{:S(2)}, u32[]{:S(2)}) collective-permute-start(f32[4,128]{1,0:T(4,128)S(1)} %get-tuple-element.21.degree_ref), channel_id=1, source_target_pairs={{0,1},{1,0},{2,3},{3,2},{4,5},{5,4},{6,7},{7,6},{8,9},{9,8},{10,11... | collective-permute-start | bytes 6152 | tf_op jit(solution)/shard_map/ppermute | solution.py:49
  4.0 17.1 %collective-permute-start.1 = (bf16[4,512,512]{2,1,0:T(8,128)(2,1)S(1)}, bf16[4,512,512]{2,1,0:T(8,128)(2,1)S(1)}, u32[]{:S(2)}, u32[]{:S(2)}) collective-permute-start(bf16[4,512,512]{2,1,0:T(8,128)(2,1)S(1)} %get-tuple-element.23.own_ref.refs_0_), channel_id=1, source_target_pairs={{0,1},{1,0},{2,3},{3,2},{4,5},{5,4},{6,7},{7,6},{8,9},{9,8},{10,11... | collective-permute-start | bytes 6291464 | tf_op jit(solution)/shard_map/ppermute | solution.py:49
  4.4 7.2 %collective-permute-start.2 = (bf16[512,128]{1,0:T(8,128)(2,1)S(1)}, bf16[512,128]{1,0:T(8,128)(2,1)S(1)}, u32[]{:S(2)}, u32[]{:S(2)}) collective-permute-start(bf16[512,128]{1,0:T(8,128)(2,1)S(1)} %get-tuple-element.24.refs_0_), channel_id=1, source_target_pairs={{0,4},{2,6},{4,0},{6,2},{8,12},{10,14},{12,8},{14,10},{1,5},{3,7},... | collective-permute-start | bytes 393224 | tf_op jit(solution)/shard_map/ppermute | solution.py:31
  7.1 5.5 %collective-permute-start.3 = (bf16[512,128]{1,0:T(8,128)(2,1)S(1)}, bf16[512,128]{1,0:T(8,128)(2,1)S(1)}, u32[]{:S(2)}, u32[]{:S(2)}) collective-permute-start(bf16[512,128]{1,0:T(8,128)(2,1)S(1)} %get-tuple-element.24.refs_0_), channel_id=1, source_target_pairs={{0,2},{2,0},{4,6},{6,4},{8,10},{10,8},{12,14},{14,12},{1,3},{3,1},... | collective-permute-start | bytes 393224 | tf_op jit(solution)/shard_map/ppermute | solution.py:31
  8.6 9.0 %collective-permute-start.4 = (bf16[512,128]{1,0:T(8,128)(2,1)S(1)}, bf16[512,128]{1,0:T(8,128)(2,1)S(1)}, u32[]{:S(2)}, u32[]{:S(2)}) collective-permute-start(bf16[512,128]{1,0:T(8,128)(2,1)S(1)} %get-tuple-element.24.refs_0_), channel_id=1, source_target_pairs={{0,8},{2,10},{4,12},{6,14},{8,0},{10,2},{12,4},{14,6},{1,9},{3,11}... | collective-permute-start | bytes 393224 | tf_op jit(solution)/shard_map/ppermute | solution.py:31
  11.2 9.9 %collective-permute-start.5 = (bf16[512,128]{1,0:T(8,128)(2,1)S(1)}, bf16[512,128]{1,0:T(8,128)(2,1)S(1)}, u32[]{:S(2)}, u32[]{:S(2)}) collective-permute-start(bf16[512,128]{1,0:T(8,128)(2,1)S(1)} %get-tuple-element.24.refs_0_), channel_id=1, source_target_pairs={{0,6},{2,4},{4,2},{6,0},{8,14},{10,12},{12,10},{14,8},{1,7},{3,5},... | collective-permute-start | bytes 393224 | tf_op jit(solution)/shard_map/ppermute | solution.py:31
  17.6 6.5 %collective-permute-start.6 = (bf16[512,128]{1,0:T(8,128)(2,1)S(1)}, bf16[512,128]{1,0:T(8,128)(2,1)S(1)}, u32[]{:S(2)}, u32[]{:S(2)}) collective-permute-start(bf16[512,128]{1,0:T(8,128)(2,1)S(1)} %collective-permute-done.4.refs_0_), channel_id=1, source_target_pairs={{0,6},{2,4},{4,2},{6,0},{8,14},{10,12},{12,10},{14,8},{1,7},{3,5},... | collective-permute-start | bytes 393224 | tf_op jit(solution)/shard_map/ppermute | solution.py:31
  18.3 6.4 %collective-permute-start.7 = (bf16[512,128]{1,0:T(8,128)(2,1)S(1)}, bf16[512,128]{1,0:T(8,128)(2,1)S(1)}, u32[]{:S(2)}, u32[]{:S(2)}) collective-permute-start(bf16[512,128]{1,0:T(8,128)(2,1)S(1)} %collective-permute-done.4.refs_0_), channel_id=1, source_target_pairs={{0,4},{2,6},{4,0},{6,2},{8,12},{10,14},{12,8},{14,10},{1,5},{3,7},... | collective-permute-start | bytes 393224 | tf_op jit(solution)/shard_map/ppermute | solution.py:31
  19.4 6.1 %collective-permute-start.8 = (bf16[512,128]{1,0:T(8,128)(2,1)S(1)}, bf16[512,128]{1,0:T(8,128)(2,1)S(1)}, u32[]{:S(2)}, u32[]{:S(2)}) collective-permute-start(bf16[512,128]{1,0:T(8,128)(2,1)S(1)} %collective-permute-done.4.refs_0_), channel_id=1, source_target_pairs={{0,2},{2,0},{4,6},{6,4},{8,10},{10,8},{12,14},{14,12},{1,3},{3,1},... | collective-permute-start | bytes 393224 | tf_op jit(solution)/shard_map/ppermute | solution.py:31
  25.8 5.4 %collective-permute-start.10 = (bf16[512,128]{1,0:T(8,128)(2,1)S(1)}, bf16[512,128]{1,0:T(8,128)(2,1)S(1)}, u32[]{:S(2)}, u32[]{:S(2)}) collective-permute-start(bf16[512,128]{1,0:T(8,128)(2,1)S(1)} %get-tuple-element.29.refs_0_), channel_id=1, source_target_pairs={{0,2},{2,0},{4,6},{6,4},{8,10},{10,8},{12,14},{14,12},{1,3},{3,1},... | collective-permute-start | bytes 393224 | tf_op jit(solution)/shard_map/ppermute | solution.py:31
  26.7 8.1 %collective-permute-start.11 = (bf16[512,128]{1,0:T(8,128)(2,1)S(1)}, bf16[512,128]{1,0:T(8,128)(2,1)S(1)}, u32[]{:S(2)}, u32[]{:S(2)}) collective-permute-start(bf16[512,128]{1,0:T(8,128)(2,1)S(1)} %get-tuple-element.29.refs_0_), channel_id=1, source_target_pairs={{0,4},{2,6},{4,0},{6,2},{8,12},{10,14},{12,8},{14,10},{1,5},{3,7},... | collective-permute-start | bytes 393224 | tf_op jit(solution)/shard_map/ppermute | solution.py:31
  27.3 7.6 %collective-permute-start.9 = (bf16[512,128]{1,0:T(8,128)(2,1)S(1)}, bf16[512,128]{1,0:T(8,128)(2,1)S(1)}, u32[]{:S(2)}, u32[]{:S(2)}) collective-permute-start(bf16[512,128]{1,0:T(8,128)(2,1)S(1)} %get-tuple-element.29.refs_0_), channel_id=1, source_target_pairs={{0,8},{2,10},{4,12},{6,14},{8,0},{10,2},{12,4},{14,6},{1,9},{3,11}... | collective-permute-start | bytes 393224 | tf_op jit(solution)/shard_map/ppermute | solution.py:31
  29.5 8.8 %collective-permute-start.12 = (bf16[512,128]{1,0:T(8,128)(2,1)S(1)}, bf16[512,128]{1,0:T(8,128)(2,1)S(1)}, u32[]{:S(2)}, u32[]{:S(2)}) collective-permute-start(bf16[512,128]{1,0:T(8,128)(2,1)S(1)} %get-tuple-element.29.refs_0_), channel_id=1, source_target_pairs={{0,6},{2,4},{4,2},{6,0},{8,14},{10,12},{12,10},{14,8},{1,7},{3,5},... | collective-permute-start | bytes 393224 | tf_op jit(solution)/shard_map/ppermute | solution.py:31
  34.9 6.0 %collective-permute-start.13 = (bf16[512,128]{1,0:T(8,128)(2,1)S(1)}, bf16[512,128]{1,0:T(8,128)(2,1)S(1)}, u32[]{:S(2)}, u32[]{:S(2)}) collective-permute-start(bf16[512,128]{1,0:T(8,128)(2,1)S(1)} %collective-permute-done.9.refs_0_), channel_id=1, source_target_pairs={{0,6},{2,4},{4,2},{6,0},{8,14},{10,12},{12,10},{14,8},{1,7},{3,5},... | collective-permute-start | bytes 393224 | tf_op jit(solution)/shard_map/ppermute | solution.py:31
  35.8 6.0 %collective-permute-start.14 = (bf16[512,128]{1,0:T(8,128)(2,1)S(1)}, bf16[512,128]{1,0:T(8,128)(2,1)S(1)}, u32[]{:S(2)}, u32[]{:S(2)}) collective-permute-start(bf16[512,128]{1,0:T(8,128)(2,1)S(1)} %collective-permute-done.9.refs_0_), channel_id=1, source_target_pairs={{0,4},{2,6},{4,0},{6,2},{8,12},{10,14},{12,8},{14,10},{1,5},{3,7},... | collective-permute-start | bytes 393224 | tf_op jit(solution)/shard_map/ppermute | solution.py:31
  37.4 5.0 %collective-permute-start.15 = (bf16[512,128]{1,0:T(8,128)(2,1)S(1)}, bf16[512,128]{1,0:T(8,128)(2,1)S(1)}, u32[]{:S(2)}, u32[]{:S(2)}) collective-permute-start(bf16[512,128]{1,0:T(8,128)(2,1)S(1)} %collective-permute-done.9.refs_0_), channel_id=1, source_target_pairs={{0,2},{2,0},{4,6},{6,4},{8,10},{10,8},{12,14},{14,12},{1,3},{3,1},... | collective-permute-start | bytes 393224 | tf_op jit(solution)/shard_map/ppermute | solution.py:31
  42.4 0.9 %copy-start.1 = (bf16[256,256]{1,0:T(8,128)(2,1)S(1)}, bf16[256,256]{1,0:T(8,128)(2,1)}, u32[]{:S(2)}) copy-start(bf16[256,256]{1,0:T(8,128)(2,1)} %weight_ref) | copy-start | bytes 393220
  42.6 1.3 %collective-permute-start.16 = (bf16[256,128]{1,0:T(8,128)(2,1)S(1)}, bf16[256,128]{1,0:T(8,128)(2,1)S(1)}, u32[]{:S(2)}, u32[]{:S(2)}) collective-permute-start(bf16[256,128]{1,0:T(8,128)(2,1)S(1)} %shard_map.65), channel_id=1, source_target_pairs={{0,1},{1,0},{2,3},{3,2},{4,5},{5,4},{6,7},{7,6},{8,9},{9,8},{10,11... | collective-permute-start | bytes 196616 | tf_op jit(solution)/shard_map/ppermute | solution.py:49

commit v8 on v7

--- a/solution.py
+++ b/solution.py
@@ -37,7 +37,7 @@
     for d in [1, half, *range(2, half)]:
         blocks[d] = xor_permute(block, axis, d)
     near = range(1, half - 1)
-    early = [*near[::-1], half] if far_last else [half, *near]
+    early = [*near[::-1], half] if far_last else [half, *near[::-1]]
     tied, also = lax.optimization_barrier(([blocks[d] for d in early], also))
     blocks.update(zip(early, tied))
     for d in range(half - 1, 0, -1):

time: 44.9 us -> 44.1 us (0.982)
  waiting for transfers between devices: 17.1 us -> 16.2 us
    ppermute x14, waiting for transfers between devices: 16 us -> 15.1 us  [xor_permute(): lax.ppermute(block, axis, [(i, i ^ distance) for i in range(lax.axis_size...]
  transfers between devices with their start and end apart: 17 -> 17, of which waited for: 11 -> 9; matrix products, arithmetic and copies ran while one was open for 0% -> 0% of each run, Pallas kernels for 7% -> 7%
where the time goes in v8:
time: 44.1 us; the launch traced here: 43.9 us
  starting transfers between devices  19.7 us (45%)
  waiting for transfers between devices  16.2 us (37%)
  Pallas kernels  7.25 us (16%)
  local copies, waits for them, and re-layouts  0.59 us (1%)
    ppermute x14, starting transfers between devices, xor_permute(): lax.ppermute(block, axis, [(i, i ^ distance) for i in range(lax.axis_size...  18.7 us
    ppermute x14, waiting for transfers between devices, xor_permute(): lax.ppermute(block, axis, [(i, i ^ distance) for i in range(lax.axis_size...  15.1 us
    pallas_call x9, Pallas kernels, image(): pl.pallas_call(kernel, out_shape=out_shape, in_specs=[VMEM] * (2 + len(ot...  3.79 us
    pallas_call x1, Pallas kernels, per_device(): pl.pallas_call(place_kernel, out_shape=(shape(*panels), shape((rows_here...  2.48 us
    ppermute x3, waiting for transfers between devices, swapped(): return lax.ppermute(block, axis, [(0, 1), (1, 0)])  1.12 us
    ppermute x3, starting transfers between devices, swapped(): return lax.ppermute(block, axis, [(0, 1), (1, 0)])  0.99 us
  transfers between devices with their start and end apart: 17, of which 9 were waited for; matrix products, arithmetic and copies ran while one was open for 0% of the time, Pallas kernels for 7%

profile of v8, /device:TPU:0, one launch (start us, length us, event | category | flops | bytes accessed | tf_op | source)
XLA Modules:
  0.0 43.9 jit_solution(10758382600761707475)
XLA Ops:
  0.0 2.5 %shard_map.55 = (bf16[4,512,512]{2,1,0:T(8,128)(2,1)S(1)}, f32[4,128]{1,0:T(4,128)S(1)}) custom-call(s32[4,16]{1,0:T(4,128)} %place_hbm.1, s32[4]{0:T(128)} %count_hbm.1, bf16[64,128,128]{2,1,0:T(8,128)(2,1)} %tiles_ref.1), custom_call_target="tpu_custom_call" | custom-call | tf_op jit(solution)/shard_map/pallas_call | solution.py:242
  2.5 0.5 %collective-permute-start = (f32[4,128]{1,0:T(4,128)S(1)}, f32[4,128]{1,0:T(4,128)S(1)}, u32[]{:S(2)}, u32[]{:S(2)}) collective-permute-start(f32[4,128]{1,0:T(4,128)S(1)} %get-tuple-element.21.degree_ref), channel_id=1, source_target_pairs={{0,1},{1,0},{2,3},{3,2},{4,5},{5,4},{6,7},{7,6},{8,9},{9,8},{10,11... | collective-permute-start | bytes 6152 | tf_op jit(solution)/shard_map/ppermute | solution.py:49
  3.0 0.8 %collective-permute-done.other_ref = f32[4,128]{1,0:T(4,128)S(1)} collective-permute-done((f32[4,128]{1,0:T(4,128)S(1)}, f32[4,128]{1,0:T(4,128)S(1)}, u32[]{:S(2)}, u32[]{:S(2)}) %collective-permute-start) | collective-permute-done | bytes 2080 | tf_op jit(solution)/shard_map/ppermute | solution.py:49
  4.0 0.4 collective-permute-start.1
  4.4 2.7 %collective-permute-start.2 = (bf16[512,128]{1,0:T(8,128)(2,1)S(1)}, bf16[512,128]{1,0:T(8,128)(2,1)S(1)}, u32[]{:S(2)}, u32[]{:S(2)}) collective-permute-start(bf16[512,128]{1,0:T(8,128)(2,1)S(1)} %get-tuple-element.24.refs_0_), channel_id=1, source_target_pairs={{0,4},{2,6},{4,0},{6,2},{8,12},{10,14},{12,8},{14,10},{1,5},{3,7},... | collective-permute-start | bytes 393224 | tf_op jit(solution)/shard_map/ppermute | solution.py:31
  7.1 1.5 %collective-permute-start.3 = (bf16[512,128]{1,0:T(8,128)(2,1)S(1)}, bf16[512,128]{1,0:T(8,128)(2,1)S(1)}, u32[]{:S(2)}, u32[]{:S(2)}) collective-permute-start(bf16[512,128]{1,0:T(8,128)(2,1)S(1)} %get-tuple-element.24.refs_0_), channel_id=1, source_target_pairs={{0,2},{2,0},{4,6},{6,4},{8,10},{10,8},{12,14},{14,12},{1,3},{3,1},... | collective-permute-start | bytes 393224 | tf_op jit(solution)/shard_map/ppermute | solution.py:31
  8.6 2.6 %collective-permute-start.4 = (bf16[512,128]{1,0:T(8,128)(2,1)S(1)}, bf16[512,128]{1,0:T(8,128)(2,1)S(1)}, u32[]{:S(2)}, u32[]{:S(2)}) collective-permute-start(bf16[512,128]{1,0:T(8,128)(2,1)S(1)} %get-tuple-element.24.refs_0_), channel_id=1, source_target_pairs={{0,8},{2,10},{4,12},{6,14},{8,0},{10,2},{12,4},{14,6},{1,9},{3,11}... | collective-permute-start | bytes 393224 | tf_op jit(solution)/shard_map/ppermute | solution.py:31
  11.2 0.4 collective-permute-start.5
  11.6 1.0 %collective-permute-done.3.refs_1_ = bf16[512,128]{1,0:T(8,128)(2,1)S(1)} collective-permute-done((bf16[512,128]{1,0:T(8,128)(2,1)S(1)}, bf16[512,128]{1,0:T(8,128)(2,1)S(1)}, u32[]{:S(2)}, u32[]{:S(2)}) %collective-permute-start.3) | collective-permute-done | bytes 131104 | tf_op jit(solution)/shard_map/ppermute | solution.py:31
  12.6 5.1 %collective-permute-done.4.refs_0_ = bf16[512,128]{1,0:T(8,128)(2,1)S(1)} collective-permute-done((bf16[512,128]{1,0:T(8,128)(2,1)S(1)}, bf16[512,128]{1,0:T(8,128)(2,1)S(1)}, u32[]{:S(2)}, u32[]{:S(2)}) %collective-permute-start.4) | collective-permute-done | bytes 131104 | tf_op jit(solution)/shard_map/ppermute | solution.py:31
  17.6 0.6 %collective-permute-start.6 = (bf16[512,128]{1,0:T(8,128)(2,1)S(1)}, bf16[512,128]{1,0:T(8,128)(2,1)S(1)}, u32[]{:S(2)}, u32[]{:S(2)}) collective-permute-start(bf16[512,128]{1,0:T(8,128)(2,1)S(1)} %collective-permute-done.4.refs_0_), channel_id=1, source_target_pairs={{0,6},{2,4},{4,2},{6,0},{8,14},{10,12},{12,10},{14,8},{1,7},{3,5},... | collective-permute-start | bytes 393224 | tf_op jit(solution)/shard_map/ppermute | solution.py:31
  18.3 1.1 %collective-permute-start.7 = (bf16[512,128]{1,0:T(8,128)(2,1)S(1)}, bf16[512,128]{1,0:T(8,128)(2,1)S(1)}, u32[]{:S(2)}, u32[]{:S(2)}) collective-permute-start(bf16[512,128]{1,0:T(8,128)(2,1)S(1)} %collective-permute-done.4.refs_0_), channel_id=1, source_target_pairs={{0,4},{2,6},{4,0},{6,2},{8,12},{10,14},{12,8},{14,10},{1,5},{3,7},... | collective-permute-start | bytes 393224 | tf_op jit(solution)/shard_map/ppermute | solution.py:31
  19.4 1.8 %collective-permute-start.8 = (bf16[512,128]{1,0:T(8,128)(2,1)S(1)}, bf16[512,128]{1,0:T(8,128)(2,1)S(1)}, u32[]{:S(2)}, u32[]{:S(2)}) collective-permute-start(bf16[512,128]{1,0:T(8,128)(2,1)S(1)} %collective-permute-done.4.refs_0_), channel_id=1, source_target_pairs={{0,2},{2,0},{4,6},{6,4},{8,10},{10,8},{12,14},{14,12},{1,3},{3,1},... | collective-permute-start | bytes 393224 | tf_op jit(solution)/shard_map/ppermute | solution.py:31
  21.1 0.7 %shard_map.57.sum_ref = f32[512,128]{1,0:T(8,128)S(1)} custom-call(bf16[4,512,512]{2,1,0:T(8,128)(2,1)S(1)} %get-tuple-element.23.own_ref.refs_0_, bf16[4,512,512]{2,1,0:T(8,128)(2,1)S(1)} %collective-permute-done.1.other_ref.refs_1_, bf16[512,128]{1,0:T(8,128)(2,1)S(1)} %get-tuple-element.24.refs_0_, bf16[512,128]{1,0:T(8,128)(2,1)S(1)} %collective-permute-done.3.refs_1_, ...), custom_call_target="tpu_custom_call" | custom-call | flops 268435456 | tf_op jit(solution)/shard_map/pallas_call | solution.py:270
  21.9 2.3 %collective-permute-done.6.refs_1_ = bf16[512,128]{1,0:T(8,128)(2,1)S(1)} collective-permute-done((bf16[512,128]{1,0:T(8,128)(2,1)S(1)}, bf16[512,128]{1,0:T(8,128)(2,1)S(1)}, u32[]{:S(2)}, u32[]{:S(2)}) %collective-permute-start.6) | collective-permute-done | bytes 131104 | tf_op jit(solution)/shard_map/ppermute | solution.py:31
  24.2 0.4 %shard_map.58.sum_ref = f32[512,128]{1,0:T(8,128)S(1)} custom-call(bf16[4,512,512]{2,1,0:T(8,128)(2,1)S(1)} %get-tuple-element.23.own_ref.refs_0_, bf16[4,512,512]{2,1,0:T(8,128)(2,1)S(1)} %collective-permute-done.1.other_ref.refs_1_, f32[512,128]{1,0:T(8,128)S(1)} %shard_map.57.sum_ref, bf16[512,128]{1,0:T(8,128)(2,1)S(1)} %collective-permute-done.4.refs_0_, ...), custom_call_target="tpu_custom_call" | custom-call | flops 134217728 | tf_op jit(solution)/shard_map/pallas_call | solution.py:270
  24.9 0.5 %collective-permute-done.8.refs_0_ = bf16[512,128]{1,0:T(8,128)(2,1)S(1)} collective-permute-done((bf16[512,128]{1,0:T(8,128)(2,1)S(1)}, bf16[512,128]{1,0:T(8,128)(2,1)S(1)}, u32[]{:S(2)}, u32[]{:S(2)}) %collective-permute-start.8) | collective-permute-done | bytes 131104 | tf_op jit(solution)/shard_map/ppermute | solution.py:31
  25.8 0.3 collective-permute-start.10
  26.1 1.1 %collective-permute-start.11 = (bf16[512,128]{1,0:T(8,128)(2,1)S(1)}, bf16[512,128]{1,0:T(8,128)(2,1)S(1)}, u32[]{:S(2)}, u32[]{:S(2)}) collective-permute-start(bf16[512,128]{1,0:T(8,128)(2,1)S(1)} %get-tuple-element.29.refs_0_), channel_id=1, source_target_pairs={{0,2},{2,0},{4,6},{6,4},{8,10},{10,8},{12,14},{14,12},{1,3},{3,1},... | collective-permute-start | bytes 393224 | tf_op jit(solution)/shard_map/ppermute | solution.py:31
  27.3 2.3 %collective-permute-start.9 = (bf16[512,128]{1,0:T(8,128)(2,1)S(1)}, bf16[512,128]{1,0:T(8,128)(2,1)S(1)}, u32[]{:S(2)}, u32[]{:S(2)}) collective-permute-start(bf16[512,128]{1,0:T(8,128)(2,1)S(1)} %get-tuple-element.29.refs_0_), channel_id=1, source_target_pairs={{0,8},{2,10},{4,12},{6,14},{8,0},{10,2},{12,4},{14,6},{1,9},{3,11}... | collective-permute-start | bytes 393224 | tf_op jit(solution)/shard_map/ppermute | solution.py:31
  29.5 0.7 %collective-permute-start.12 = (bf16[512,128]{1,0:T(8,128)(2,1)S(1)}, bf16[512,128]{1,0:T(8,128)(2,1)S(1)}, u32[]{:S(2)}, u32[]{:S(2)}) collective-permute-start(bf16[512,128]{1,0:T(8,128)(2,1)S(1)} %get-tuple-element.29.refs_0_), channel_id=1, source_target_pairs={{0,6},{2,4},{4,2},{6,0},{8,14},{10,12},{12,10},{14,8},{1,7},{3,5},... | collective-permute-start | bytes 393224 | tf_op jit(solution)/shard_map/ppermute | solution.py:31
  30.3 3.9 %collective-permute-done.10.refs_2_ = bf16[512,128]{1,0:T(8,128)(2,1)S(1)} collective-permute-done((bf16[512,128]{1,0:T(8,128)(2,1)S(1)}, bf16[512,128]{1,0:T(8,128)(2,1)S(1)}, u32[]{:S(2)}, u32[]{:S(2)}) %collective-permute-start.10) | collective-permute-done | bytes 131104 | tf_op jit(solution)/shard_map/ppermute | solution.py:31
  34.1 1.6 %collective-permute-start.13 = (bf16[512,128]{1,0:T(8,128)(2,1)S(1)}, bf16[512,128]{1,0:T(8,128)(2,1)S(1)}, u32[]{:S(2)}, u32[]{:S(2)}) collective-permute-start(bf16[512,128]{1,0:T(8,128)(2,1)S(1)} %collective-permute-done.9.refs_0_), channel_id=1, source_target_pairs={{0,6},{2,4},{4,2},{6,0},{8,14},{10,12},{12,10},{14,8},{1,7},{3,5},... | collective-permute-start | bytes 393224 | tf_op jit(solution)/shard_map/ppermute | solution.py:31
  35.7 0.3 collective-permute-start.14
  36.1 1.6 %collective-permute-start.15 = (bf16[512,128]{1,0:T(8,128)(2,1)S(1)}, bf16[512,128]{1,0:T(8,128)(2,1)S(1)}, u32[]{:S(2)}, u32[]{:S(2)}) collective-permute-start(bf16[512,128]{1,0:T(8,128)(2,1)S(1)} %collective-permute-done.9.refs_0_), channel_id=1, source_target_pairs={{0,2},{2,0},{4,6},{6,4},{8,10},{10,8},{12,14},{14,12},{1,3},{3,1},... | collective-permute-start | bytes 393224 | tf_op jit(solution)/shard_map/ppermute | solution.py:31
  37.6 0.7 %shard_map.61.sum_ref = f32[512,128]{1,0:T(8,128)S(1)} custom-call(bf16[4,512,512]{2,1,0:T(8,128)(2,1)S(1)} %get-tuple-element.23.own_ref.refs_0_, bf16[4,512,512]{2,1,0:T(8,128)(2,1)S(1)} %collective-permute-done.1.other_ref.refs_1_, bf16[512,128]{1,0:T(8,128)(2,1)S(1)} %get-tuple-element.29.refs_0_, bf16[512,128]{1,0:T(8,128)(2,1)S(1)} %collective-permute-done.11.refs_1_, ...), custom_call_target="tpu_custom_call" | custom-call | flops 268435456 | tf_op jit(solution)/shard_map/pallas_call | solution.py:270
  38.4 1.7 %collective-permute-done.13.refs_1_ = bf16[512,128]{1,0:T(8,128)(2,1)S(1)} collective-permute-done((bf16[512,128]{1,0:T(8,128)(2,1)S(1)}, bf16[512,128]{1,0:T(8,128)(2,1)S(1)}, u32[]{:S(2)}, u32[]{:S(2)}) %collective-permute-start.13) | collective-permute-done | bytes 131104 | tf_op jit(solution)/shard_map/ppermute | solution.py:31
  40.0 0.4 %shard_map.62.sum_ref = f32[512,128]{1,0:T(8,128)S(1)} custom-call(bf16[4,512,512]{2,1,0:T(8,128)(2,1)S(1)} %get-tuple-element.23.own_ref.refs_0_, bf16[4,512,512]{2,1,0:T(8,128)(2,1)S(1)} %collective-permute-done.1.other_ref.refs_1_, f32[512,128]{1,0:T(8,128)S(1)} %shard_map.61.sum_ref, bf16[512,128]{1,0:T(8,128)(2,1)S(1)} %collective-permute-done.9.refs_0_, ...), custom_call_target="tpu_custom_call" | custom-call | flops 134217728 | tf_op jit(solution)/shard_map/pallas_call | solution.py:270
  40.5 0.7 %collective-permute-done.14.refs_0_ = bf16[512,128]{1,0:T(8,128)(2,1)S(1)} collective-permute-done((bf16[512,128]{1,0:T(8,128)(2,1)S(1)}, bf16[512,128]{1,0:T(8,128)(2,1)S(1)}, u32[]{:S(2)}, u32[]{:S(2)}) %collective-permute-start.14) | collective-permute-done | bytes 131104 | tf_op jit(solution)/shard_map/ppermute | solution.py:31
  41.8 0.6 %copy-done.1 = bf16[256,256]{1,0:T(8,128)(2,1)S(1)} copy-done((bf16[256,256]{1,0:T(8,128)(2,1)S(1)}, bf16[256,256]{1,0:T(8,128)(2,1)}, u32[]{:S(2)}) %copy-start.1) | copy-done | bytes 131096
  42.4 0.4 shard_map.64.product_ref
  43.1 0.8 %shard_map.66 = bf16[256,256]{1,0:T(8,128)(2,1)} custom-call(f32[256,256]{1,0:T(8,128)S(1)} %shard_map.64.product_ref, bf16[256,128]{1,0:T(8,128)(2,1)S(1)} %collective-permute-done.16.got_ref, bf16[256,256]{1,0:T(8,128)(2,1)S(1)} %copy-done.1), custom_call_target="tpu_custom_call" | custom-call | tf_op jit(solution)/shard_map/pallas_call | solution.py:325
  (18 shorter events, 1.6 us)
Async XLA Ops:
  0.0 3.8 %copy-start = (bf16[512,256]{1,0:T(8,128)(2,1)S(1)}, bf16[512,256]{1,0:T(8,128)(2,1)}, u32[]{:S(2)}) copy-start(bf16[512,256]{1,0:T(8,128)(2,1)} %refs_5_.3) | copy-start | bytes 786436
  2.5 1.3 %collective-permute-start = (f32[4,128]{1,0:T(4,128)S(1)}, f32[4,128]{1,0:T(4,128)S(1)}, u32[]{:S(2)}, u32[]{:S(2)}) collective-permute-start(f32[4,128]{1,0:T(4,128)S(1)} %get-tuple-element.21.degree_ref), channel_id=1, source_target_pairs={{0,1},{1,0},{2,3},{3,2},{4,5},{5,4},{6,7},{7,6},{8,9},{9,8},{10,11... | collective-permute-start | bytes 6152 | tf_op jit(solution)/shard_map/ppermute | solution.py:49
  4.0 17.1 %collective-permute-start.1 = (bf16[4,512,512]{2,1,0:T(8,128)(2,1)S(1)}, bf16[4,512,512]{2,1,0:T(8,128)(2,1)S(1)}, u32[]{:S(2)}, u32[]{:S(2)}) collective-permute-start(bf16[4,512,512]{2,1,0:T(8,128)(2,1)S(1)} %get-tuple-element.23.own_ref.refs_0_), channel_id=1, source_target_pairs={{0,1},{1,0},{2,3},{3,2},{4,5},{5,4},{6,7},{7,6},{8,9},{9,8},{10,11... | collective-permute-start | bytes 6291464 | tf_op jit(solution)/shard_map/ppermute | solution.py:49
  4.4 7.2 %collective-permute-start.2 = (bf16[512,128]{1,0:T(8,128)(2,1)S(1)}, bf16[512,128]{1,0:T(8,128)(2,1)S(1)}, u32[]{:S(2)}, u32[]{:S(2)}) collective-permute-start(bf16[512,128]{1,0:T(8,128)(2,1)S(1)} %get-tuple-element.24.refs_0_), channel_id=1, source_target_pairs={{0,4},{2,6},{4,0},{6,2},{8,12},{10,14},{12,8},{14,10},{1,5},{3,7},... | collective-permute-start | bytes 393224 | tf_op jit(solution)/shard_map/ppermute | solution.py:31
  7.1 5.5 %collective-permute-start.3 = (bf16[512,128]{1,0:T(8,128)(2,1)S(1)}, bf16[512,128]{1,0:T(8,128)(2,1)S(1)}, u32[]{:S(2)}, u32[]{:S(2)}) collective-permute-start(bf16[512,128]{1,0:T(8,128)(2,1)S(1)} %get-tuple-element.24.refs_0_), channel_id=1, source_target_pairs={{0,2},{2,0},{4,6},{6,4},{8,10},{10,8},{12,14},{14,12},{1,3},{3,1},... | collective-permute-start | bytes 393224 | tf_op jit(solution)/shard_map/ppermute | solution.py:31
  8.6 9.0 %collective-permute-start.4 = (bf16[512,128]{1,0:T(8,128)(2,1)S(1)}, bf16[512,128]{1,0:T(8,128)(2,1)S(1)}, u32[]{:S(2)}, u32[]{:S(2)}) collective-permute-start(bf16[512,128]{1,0:T(8,128)(2,1)S(1)} %get-tuple-element.24.refs_0_), channel_id=1, source_target_pairs={{0,8},{2,10},{4,12},{6,14},{8,0},{10,2},{12,4},{14,6},{1,9},{3,11}... | collective-permute-start | bytes 393224 | tf_op jit(solution)/shard_map/ppermute | solution.py:31
  11.2 9.9 %collective-permute-start.5 = (bf16[512,128]{1,0:T(8,128)(2,1)S(1)}, bf16[512,128]{1,0:T(8,128)(2,1)S(1)}, u32[]{:S(2)}, u32[]{:S(2)}) collective-permute-start(bf16[512,128]{1,0:T(8,128)(2,1)S(1)} %get-tuple-element.24.refs_0_), channel_id=1, source_target_pairs={{0,6},{2,4},{4,2},{6,0},{8,14},{10,12},{12,10},{14,8},{1,7},{3,5},... | collective-permute-start | bytes 393224 | tf_op jit(solution)/shard_map/ppermute | solution.py:31
  17.6 6.5 %collective-permute-start.6 = (bf16[512,128]{1,0:T(8,128)(2,1)S(1)}, bf16[512,128]{1,0:T(8,128)(2,1)S(1)}, u32[]{:S(2)}, u32[]{:S(2)}) collective-permute-start(bf16[512,128]{1,0:T(8,128)(2,1)S(1)} %collective-permute-done.4.refs_0_), channel_id=1, source_target_pairs={{0,6},{2,4},{4,2},{6,0},{8,14},{10,12},{12,10},{14,8},{1,7},{3,5},... | collective-permute-start | bytes 393224 | tf_op jit(solution)/shard_map/ppermute | solution.py:31
  18.3 6.4 %collective-permute-start.7 = (bf16[512,128]{1,0:T(8,128)(2,1)S(1)}, bf16[512,128]{1,0:T(8,128)(2,1)S(1)}, u32[]{:S(2)}, u32[]{:S(2)}) collective-permute-start(bf16[512,128]{1,0:T(8,128)(2,1)S(1)} %collective-permute-done.4.refs_0_), channel_id=1, source_target_pairs={{0,4},{2,6},{4,0},{6,2},{8,12},{10,14},{12,8},{14,10},{1,5},{3,7},... | collective-permute-start | bytes 393224 | tf_op jit(solution)/shard_map/ppermute | solution.py:31
  19.4 6.1 %collective-permute-start.8 = (bf16[512,128]{1,0:T(8,128)(2,1)S(1)}, bf16[512,128]{1,0:T(8,128)(2,1)S(1)}, u32[]{:S(2)}, u32[]{:S(2)}) collective-permute-start(bf16[512,128]{1,0:T(8,128)(2,1)S(1)} %collective-permute-done.4.refs_0_), channel_id=1, source_target_pairs={{0,2},{2,0},{4,6},{6,4},{8,10},{10,8},{12,14},{14,12},{1,3},{3,1},... | collective-permute-start | bytes 393224 | tf_op jit(solution)/shard_map/ppermute | solution.py:31
  25.8 8.4 %collective-permute-start.10 = (bf16[512,128]{1,0:T(8,128)(2,1)S(1)}, bf16[512,128]{1,0:T(8,128)(2,1)S(1)}, u32[]{:S(2)}, u32[]{:S(2)}) collective-permute-start(bf16[512,128]{1,0:T(8,128)(2,1)S(1)} %get-tuple-element.29.refs_0_), channel_id=1, source_target_pairs={{0,4},{2,6},{4,0},{6,2},{8,12},{10,14},{12,8},{14,10},{1,5},{3,7},... | collective-permute-start | bytes 393224 | tf_op jit(solution)/shard_map/ppermute | solution.py:31
  26.1 8.0 %collective-permute-start.11 = (bf16[512,128]{1,0:T(8,128)(2,1)S(1)}, bf16[512,128]{1,0:T(8,128)(2,1)S(1)}, u32[]{:S(2)}, u32[]{:S(2)}) collective-permute-start(bf16[512,128]{1,0:T(8,128)(2,1)S(1)} %get-tuple-element.29.refs_0_), channel_id=1, source_target_pairs={{0,2},{2,0},{4,6},{6,4},{8,10},{10,8},{12,14},{14,12},{1,3},{3,1},... | collective-permute-start | bytes 393224 | tf_op jit(solution)/shard_map/ppermute | solution.py:31
  27.3 6.9 %collective-permute-start.9 = (bf16[512,128]{1,0:T(8,128)(2,1)S(1)}, bf16[512,128]{1,0:T(8,128)(2,1)S(1)}, u32[]{:S(2)}, u32[]{:S(2)}) collective-permute-start(bf16[512,128]{1,0:T(8,128)(2,1)S(1)} %get-tuple-element.29.refs_0_), channel_id=1, source_target_pairs={{0,8},{2,10},{4,12},{6,14},{8,0},{10,2},{12,4},{14,6},{1,9},{3,11}... | collective-permute-start | bytes 393224 | tf_op jit(solution)/shard_map/ppermute | solution.py:31
  29.5 8.1 %collective-permute-start.12 = (bf16[512,128]{1,0:T(8,128)(2,1)S(1)}, bf16[512,128]{1,0:T(8,128)(2,1)S(1)}, u32[]{:S(2)}, u32[]{:S(2)}) collective-permute-start(bf16[512,128]{1,0:T(8,128)(2,1)S(1)} %get-tuple-element.29.refs_0_), channel_id=1, source_target_pairs={{0,6},{2,4},{4,2},{6,0},{8,14},{10,12},{12,10},{14,8},{1,7},{3,5},... | collective-permute-start | bytes 393224 | tf_op jit(solution)/shard_map/ppermute | solution.py:31
  34.1 5.9 %collective-permute-start.13 = (bf16[512,128]{1,0:T(8,128)(2,1)S(1)}, bf16[512,128]{1,0:T(8,128)(2,1)S(1)}, u32[]{:S(2)}, u32[]{:S(2)}) collective-permute-start(bf16[512,128]{1,0:T(8,128)(2,1)S(1)} %collective-permute-done.9.refs_0_), channel_id=1, source_target_pairs={{0,6},{2,4},{4,2},{6,0},{8,14},{10,12},{12,10},{14,8},{1,7},{3,5},... | collective-permute-start | bytes 393224 | tf_op jit(solution)/shard_map/ppermute | solution.py:31
  35.7 5.5 %collective-permute-start.14 = (bf16[512,128]{1,0:T(8,128)(2,1)S(1)}, bf16[512,128]{1,0:T(8,128)(2,1)S(1)}, u32[]{:S(2)}, u32[]{:S(2)}) collective-permute-start(bf16[512,128]{1,0:T(8,128)(2,1)S(1)} %collective-permute-done.9.refs_0_), channel_id=1, source_target_pairs={{0,4},{2,6},{4,0},{6,2},{8,12},{10,14},{12,8},{14,10},{1,5},{3,7},... | collective-permute-start | bytes 393224 | tf_op jit(solution)/shard_map/ppermute | solution.py:31
  36.1 5.4 %collective-permute-start.15 = (bf16[512,128]{1,0:T(8,128)(2,1)S(1)}, bf16[512,128]{1,0:T(8,128)(2,1)S(1)}, u32[]{:S(2)}, u32[]{:S(2)}) collective-permute-start(bf16[512,128]{1,0:T(8,128)(2,1)S(1)} %collective-permute-done.9.refs_0_), channel_id=1, source_target_pairs={{0,2},{2,0},{4,6},{6,4},{8,10},{10,8},{12,14},{14,12},{1,3},{3,1},... | collective-permute-start | bytes 393224 | tf_op jit(solution)/shard_map/ppermute | solution.py:31
  41.5 0.9 %copy-start.1 = (bf16[256,256]{1,0:T(8,128)(2,1)S(1)}, bf16[256,256]{1,0:T(8,128)(2,1)}, u32[]{:S(2)}) copy-start(bf16[256,256]{1,0:T(8,128)(2,1)} %weight_ref) | copy-start | bytes 393220
  41.8 1.3 %collective-permute-start.16 = (bf16[256,128]{1,0:T(8,128)(2,1)S(1)}, bf16[256,128]{1,0:T(8,128)(2,1)S(1)}, u32[]{:S(2)}, u32[]{:S(2)}) collective-permute-start(bf16[256,128]{1,0:T(8,128)(2,1)S(1)} %shard_map.65), channel_id=1, source_target_pairs={{0,1},{1,0},{2,3},{3,2},{4,5},{5,4},{6,7},{7,6},{8,9},{9,8},{10,11... | collective-permute-start | bytes 196616 | tf_op jit(solution)/shard_map/ppermute | solution.py:49
